TPU v7x, 32 devices: a whole 2x2x4 slice. The times are simulated.
32 devices in a mesh: tok: 4 (over y, core), exp: 8 (over z, x).
Axes of the slice: x: 2, y: 2, z: 4, core: 2. Of those that a mesh axis runs over, the one named last changes fastest.
Arguments:
- tokens: bfloat16 [2048, 4096], P(('tok', 'exp')), may hold values from -6 to 6
- cotangent: bfloat16 [2048, 4096], P(('tok', 'exp')), may hold values from -6 to 6
- expert_ids: int32 [2048, 8], P(('tok', 'exp')), may hold values from 0 to 127, as said below
- gate_weights: bfloat16 [2048, 8], P(('tok', 'exp')), may hold values from 0.099609375 to 1
- w_in: bfloat16 [8, 2, 1536, 4096], P('exp', None, 'tok'), may hold values from -0.09375 to 0.09375
- w_down: bfloat16 [8, 1536, 4096], P('exp', 'tok'), may hold values from -0.3125 to 0.3125
Outputs:
- moe_out: bfloat16 [2048, 4096], P(('tok', 'exp'))
- token_grad: bfloat16 [2048, 4096], P(('tok', 'exp'))
- grad_w_in: bfloat16 [8, 2, 1536, 4096], P('exp', None, 'tok')
- grad_w_down: bfloat16 [8, 1536, 4096], P('exp', 'tok')
Inputs may be any that keep to these rules, and one draw needn't show every extreme that they name: `expert_ids`: each row names 8 different experts. Among the 64 rows of one device no expert below 8 is named by more than 2 rows, and one expert below 8, the same on every device, is named by exactly 2 rows of every device.
All inputs are finite; a program needn't handle non-finite values.
Results may differ from a plain program's by a relative error of at most 0.0058.
Values may be sent and summed in bfloat16 or wider, within the bound.
No kernel may reach another device: no remote copies, remote signals or barrier semaphores. Data moves between devices by JAX's collectives and lax.ppermute only.
A program may use at most 128 MiB of HBM per device.

v0:
```python
import jax
import jax.numpy as jnp
from jax import lax
from jax.sharding import PartitionSpec as P

CAP = 2


def build_tables(expert_ids, gate_weights, experts, capacity):
    count_rows, count_top = expert_ids.shape
    flat_ids = expert_ids.reshape(count_rows * count_top)
    owners = jnp.arange(experts, dtype=jnp.int32)
    onehot = (flat_ids[:, None] == owners[None, :]).astype(jnp.int32)
    before = jnp.cumsum(onehot, axis=0) - onehot
    slots = jnp.sum(before * onehot, axis=1)
    target = jnp.where(flat_ids < experts, flat_ids * capacity + slots, experts * capacity)
    place_table = jnp.arange(experts * capacity, dtype=jnp.int32)
    matches = (place_table[:, None] == target[None, :]).reshape(
        experts * capacity, count_rows, count_top
    )
    picked = jnp.sum(matches.astype(jnp.float32), axis=2).astype(jnp.bfloat16)
    weighted = jnp.sum(
        jnp.where(matches, gate_weights.astype(jnp.float32)[None, :, :], 0.0), axis=2
    )
    return (picked, weighted.astype(jnp.bfloat16))


def expert_slice(routed, routed_cot, weight_in, weight_down):
    gate_act = jnp.einsum("rd,fd->rf", routed, weight_in[0], preferred_element_type=jnp.float32)
    up_act = jnp.einsum("rd,fd->rf", routed, weight_in[1], preferred_element_type=jnp.float32)
    sigmoid_gate = jax.nn.sigmoid(gate_act)
    silu_gate = gate_act * sigmoid_gate
    hidden = (silu_gate * up_act).astype(jnp.bfloat16)
    out_part = jnp.dot(hidden, weight_down, preferred_element_type=jnp.float32)
    hidden_grad = jnp.einsum(
        "rd,fd->rf", routed_cot, weight_down, preferred_element_type=jnp.float32
    )
    gate_grad = (
        hidden_grad * up_act * sigmoid_gate * (1.0 + gate_act * (1.0 - sigmoid_gate))
    ).astype(jnp.bfloat16)
    up_grad = (hidden_grad * silu_gate).astype(jnp.bfloat16)
    grad_part = jnp.dot(gate_grad, weight_in[0], preferred_element_type=jnp.float32) + jnp.dot(
        up_grad, weight_in[1], preferred_element_type=jnp.float32
    )
    grad_gate = jnp.einsum("rf,rd->fd", gate_grad, routed, preferred_element_type=jnp.float32)
    grad_up = jnp.einsum("rf,rd->fd", up_grad, routed, preferred_element_type=jnp.float32)
    grad_down = jnp.einsum("rf,rd->fd", hidden, routed_cot, preferred_element_type=jnp.float32)
    grad_in = jnp.stack([grad_gate, grad_up]).astype(jnp.bfloat16)
    return (out_part, grad_part, grad_in, grad_down.astype(jnp.bfloat16))


def body(tokens, cotangent, expert_ids, gate_weights, w_in, w_down):
    experts = lax.axis_size("exp")
    groups = lax.axis_size("tok")
    width = tokens.shape[1]
    picked, weighted = build_tables(expert_ids, gate_weights, experts, CAP)
    send_rows = jnp.dot(picked, tokens, preferred_element_type=jnp.float32).astype(jnp.bfloat16)
    send_cot = jnp.dot(weighted, cotangent, preferred_element_type=jnp.float32).astype(jnp.bfloat16)
    wide_rows = jnp.broadcast_to(send_rows[None], (groups,) + send_rows.shape).reshape(
        groups * experts * CAP, width
    )
    wide_cot = jnp.broadcast_to(send_cot[None], (groups,) + send_cot.shape).reshape(
        groups * experts * CAP, width
    )
    routed, routed_cot = (
        lax.all_to_all(wide_rows, ("tok", "exp"), split_axis=0, concat_axis=0, tiled=True),
        lax.all_to_all(wide_cot, ("tok", "exp"), split_axis=0, concat_axis=0, tiled=True),
    )
    out_part, grad_part, grad_in, grad_down = expert_slice(routed, routed_cot, w_in[0], w_down[0])
    back_out, back_grad = (
        lax.all_to_all(out_part, ("tok", "exp"), split_axis=0, concat_axis=0, tiled=True),
        lax.all_to_all(grad_part, ("tok", "exp"), split_axis=0, concat_axis=0, tiled=True),
    )
    out_rows = jnp.sum(back_out.reshape(groups, experts * CAP, width), axis=0).astype(jnp.bfloat16)
    grad_rows = jnp.sum(back_grad.reshape(groups, experts * CAP, width), axis=0).astype(
        jnp.bfloat16
    )
    moe_out = jnp.dot(weighted.T, out_rows, preferred_element_type=jnp.float32).astype(jnp.bfloat16)
    token_grad = jnp.dot(picked.T, grad_rows, preferred_element_type=jnp.float32).astype(
        jnp.bfloat16
    )
    return (moe_out, token_grad, grad_in[None], grad_down[None])


def solution(mesh):
    placed = (
        P(("tok", "exp"), None),
        P(("tok", "exp"), None),
        P(("tok", "exp"), None),
        P(("tok", "exp"), None),
        P("exp", None, "tok", None),
        P("exp", "tok", None),
    )
    return jax.shard_map(
        body,
        mesh=mesh,
        in_specs=placed,
        out_specs=(
            P(("tok", "exp"), None),
            P(("tok", "exp"), None),
            P("exp", None, "tok", None),
            P("exp", "tok", None),
        ),
        check_vma=False,
    )
```

profile of v0, /device:TPU:0, one launch (start us, length us, event | category | flops | bytes accessed | tf_op | source)
XLA Modules:
  0.0 132.9 jit_solution(18431069957399264338)
XLA Ops:
  0.6 0.0 copy-start
  0.6 0.9 copy.40
  1.6 0.1 eq.44
  1.7 0.1 eq.40
  1.8 1.1 reduce-window.6
  2.9 0.2 slice_reduce_fusion
  3.2 0.1 fusion.23
  3.3 0.1 reduce_sum.48
  3.4 0.1 copy.42
  3.4 0.7 add_select_fusion
  4.1 0.7 convert_element_type.59
  4.8 0.1 select_reduce_fusion
  4.9 1.2 convolution_convert_fusion.6
  6.1 0.8 broadcast_in_dim.39
  6.9 2.2 %all_to_all.26 = bf16[32,2,4096]{2,1,0:T(2,128)(2,1)} reshape(bf16[4,16,4096]{2,1,0:T(8,128)(2,1)} %broadcast_in_dim.39) | data formatting | bytes 1048576 | tf_op jit(solution)/shard_map/all_to_all | solution.py:66
  9.1 7.4 %all-to-all-start = ((bf16[32,2,4096]{2,1,0:T(2,128)(2,1)}), bf16[32,2,4096]{2,1,0:T(2,128)(2,1)}, u32[]{:S(2)}, u32[]{:S(2)}) async-start(bf16[32,2,4096]{2,1,0:T(2,128)(2,1)} %all_to_all.26), calls=%async_computation | async-start | bytes 1048576 | tf_op jit(solution)/shard_map/all_to_all | solution.py:66
  16.5 1.2 convolution_convert_fusion.5
  17.8 0.8 broadcast_in_dim.40
  18.6 2.2 %all_to_all.30 = bf16[32,2,4096]{2,1,0:T(2,128)(2,1)} reshape(bf16[4,16,4096]{2,1,0:T(8,128)(2,1)} %broadcast_in_dim.40) | data formatting | bytes 1048576 | tf_op jit(solution)/shard_map/all_to_all | solution.py:67
  20.8 12.1 %all-to-all-done = bf16[32,2,4096]{2,1,0:T(2,128)(2,1)} async-done(((bf16[32,2,4096]{2,1,0:T(2,128)(2,1)}), bf16[32,2,4096]{2,1,0:T(2,128)(2,1)}, u32[]{:S(2)}, u32[]{:S(2)}) %all-to-all-start) | async-done | bytes 524320 | tf_op jit(solution)/shard_map/all_to_all | solution.py:66
  32.9 3.3 %all-to-all-start.2 = ((bf16[32,2,4096]{2,1,0:T(2,128)(2,1)}), bf16[32,2,4096]{2,1,0:T(2,128)(2,1)}, u32[]{:S(2)}, u32[]{:S(2)}) async-start(bf16[32,2,4096]{2,1,0:T(2,128)(2,1)} %all_to_all.30), calls=%async_computation.2 | async-start | bytes 1048576 | tf_op jit(solution)/shard_map/all_to_all | solution.py:67
  36.2 2.0 %all_to_all.28 = bf16[64,4096]{1,0:T(8,128)(2,1)} reshape(bf16[32,2,4096]{2,1,0:T(2,128)(2,1)} %all-to-all-done) | data formatting | bytes 1048576 | tf_op jit(solution)/shard_map/all_to_all | solution.py:66
  38.2 0.0 copy-start.1
  38.2 3.2 %fusion.12 = f32[64,384]{1,0:T(8,128)S(1)} fusion(bf16[64,4096]{1,0:T(8,128)(2,1)} %all_to_all.28, bf16[1,2,384,4096]{3,2,1,0:T(8,128)(2,1)} %param.10), kind=kOutput, calls=%fused_computation.21 | convolution fusion | flops 201326592 | bytes 3768320 | tf_op jit(solution)/shard_map/rd,fd->rf/dot_general | solution.py:29
  41.4 0.0 copy-done.1
  41.4 3.0 %fusion.8 = f32[64,384]{1,0:T(8,128)S(1)} fusion(bf16[64,4096]{1,0:T(8,128)(2,1)S(1)} %copy-done.1, bf16[1,2,384,4096]{3,2,1,0:T(8,128)(2,1)} %param.10), kind=kOutput, calls=%fused_computation.17 | convolution fusion | flops 201326592 | bytes 3768320 | tf_op jit(solution)/shard_map/rd,fd->rf/dot_general | solution.py:30
  44.4 8.1 %all-to-all-done.2 = bf16[32,2,4096]{2,1,0:T(2,128)(2,1)} async-done(((bf16[32,2,4096]{2,1,0:T(2,128)(2,1)}), bf16[32,2,4096]{2,1,0:T(2,128)(2,1)}, u32[]{:S(2)}, u32[]{:S(2)}) %all-to-all-start.2) | async-done | bytes 524320 | tf_op jit(solution)/shard_map/all_to_all | solution.py:67
  52.5 2.0 %all_to_all.32 = bf16[64,4096]{1,0:T(8,128)(2,1)} reshape(bf16[32,2,4096]{2,1,0:T(2,128)(2,1)} %all-to-all-done.2) | data formatting | bytes 1048576 | tf_op jit(solution)/shard_map/all_to_all | solution.py:67
  54.6 0.0 copy-done
  54.6 2.1 %multiply_convert_fusion = (bf16[64,384]{1,0:T(8,128)(2,1)S(1)}, bf16[64,384]{1,0:T(8,128)(2,1)S(1)}, bf16[64,384]{1,0:T(8,128)(2,1)S(1)}) fusion(f32[64,384]{1,0:T(8,128)S(1)} %fusion.12, f32[64,384]{1,0:T(8,128)S(1)} %fusion.8, bf16[64,4096]{1,0:T(8,128)(2,1)} %all_to_all.32, bf16[1,384,4096]{2,1,0:T(8,128)(2,1)S(1)} %copy-done), kind=kOutput, calls=%fused_computation.29 | convolution fusion | flops 201695232 | bytes 4014080 | tf_op jit(solution)/shard_map/rd,fd->rf/dot_general | solution.py:35
  56.7 2.6 %fusion.10 = f32[64,4096]{1,0:T(8,128)S(1)} fusion(bf16[64,384]{1,0:T(8,128)(2,1)S(1)} %get-tuple-element.7, bf16[1,2,384,4096]{3,2,1,0:T(8,128)(2,1)} %param.10), kind=kOutput, calls=%fused_computation.19 | convolution fusion | flops 201326592 | bytes 4243456 | tf_op jit(solution)/shard_map/dot_general | solution.py:42
  59.3 3.6 %convolution_add_fusion = f32[64,4096]{1,0:T(8,128)} fusion(f32[64,4096]{1,0:T(8,128)S(1)} %fusion.10, bf16[64,384]{1,0:T(8,128)(2,1)S(1)} %get-tuple-element.6, bf16[1,2,384,4096]{3,2,1,0:T(8,128)(2,1)} %param.10), kind=kOutput, calls=%fused_computation.7 | convolution fusion | flops 201588736 | bytes 5292032 | tf_op jit(solution)/shard_map/dot_general | solution.py:42
  62.8 2.8 %all_to_all.33 = f32[32,2,4096]{2,1,0:T(2,128)} reshape(f32[64,4096]{1,0:T(8,128)} %convolution_add_fusion) | data formatting | bytes 2097152 | tf_op jit(solution)/shard_map/all_to_all | solution.py:72
  65.6 3.4 %all-to-all-start.3 = ((f32[32,2,4096]{2,1,0:T(2,128)}), f32[32,2,4096]{2,1,0:T(2,128)}, u32[]{:S(2)}, u32[]{:S(2)}) async-start(f32[32,2,4096]{2,1,0:T(2,128)} %all_to_all.33), calls=%async_computation.3 | async-start | bytes 2097152 | tf_op jit(solution)/shard_map/all_to_all | solution.py:72
  69.1 0.7 fusion.3
  69.7 1.8 %copy.44 = f32[32,2,4096]{2,1,0:T(2,128)} copy(f32[32,2,4096]{2,0,1:T(8,128)S(1)} %fusion.3) | data formatting | bytes 2097152 | tf_op jit(solution)/shard_map/dot_general | solution.py:34
  71.6 25.0 %all-to-all-done.3 = f32[32,2,4096]{2,1,0:T(2,128)} async-done(((f32[32,2,4096]{2,1,0:T(2,128)}), f32[32,2,4096]{2,1,0:T(2,128)}, u32[]{:S(2)}, u32[]{:S(2)}) %all-to-all-start.3) | async-done | bytes 1048608 | tf_op jit(solution)/shard_map/all_to_all | solution.py:72
  96.6 3.6 %all-to-all-start.1 = ((f32[32,2,4096]{2,1,0:T(2,128)}), f32[32,2,4096]{2,1,0:T(2,128)}, u32[]{:S(2)}, u32[]{:S(2)}) async-start(f32[32,2,4096]{2,1,0:T(2,128)} %copy.44), calls=%async_computation.1 | async-start | bytes 2097152 | tf_op jit(solution)/shard_map/all_to_all | solution.py:71
  100.2 0.0 copy-start.2
  100.2 0.0 copy-start.3
  100.2 2.1 %fusion = bf16[1,1,384,4096]{3,2,1,0:T(8,128)(2,1)S(1)} fusion(bf16[64,384]{1,0:T(8,128)(2,1)S(1)} %get-tuple-element.7, bf16[64,4096]{1,0:T(8,128)(2,1)} %all_to_all.28), kind=kOutput, calls=%fused_computation.4 | convolution fusion | flops 202899456 | bytes 3719168 | tf_op jit(solution)/shard_map/rf,rd->fd/dot_general | solution.py:45
  102.3 0.0 copy-done.2
  102.3 1.0 fusion.1
  103.3 0.0 copy-done.3
  103.3 2.7 %fusion.2 = bf16[1,384,4096]{2,1,0:T(8,128)(2,1)} fusion(bf16[64,384]{1,0:T(8,128)(2,1)S(1)} %get-tuple-element.8, bf16[64,4096]{1,0:T(8,128)(2,1)S(1)} %copy-done.3), kind=kOutput, calls=%fused_computation.6 | convolution fusion | flops 202899456 | bytes 3719168 | tf_op jit(solution)/shard_map/rf,rd->fd/dot_general | solution.py:47
  106.0 3.2 %pad_maximum_fusion = bf16[1,2,384,4096]{3,2,1,0:T(8,128)(2,1)} fusion(bf16[1,1,384,4096]{3,2,1,0:T(8,128)(2,1)S(1)} %fusion.1, bf16[1,1,384,4096]{3,2,1,0:T(8,128)(2,1)S(1)} %fusion), kind=kLoop, calls=%fused_computation | loop fusion | flops 3145728 | bytes 12582912 | tf_op jit(solution)/shard_map/stack | solution.py:48
  109.3 2.9 %reshape.110 = f32[4,16,4096]{2,1,0:T(8,128)} reshape(f32[32,2,4096]{2,1,0:T(2,128)} %all-to-all-done.3) | data formatting | bytes 2097152 | tf_op jit(solution)/shard_map/reshape | solution.py:75
  112.2 1.3 reduce_sum.52
  113.5 1.1 convolution_convert_fusion.3
  114.6 13.0 %all-to-all-done.1 = f32[32,2,4096]{2,1,0:T(2,128)} async-done(((f32[32,2,4096]{2,1,0:T(2,128)}), f32[32,2,4096]{2,1,0:T(2,128)}, u32[]{:S(2)}, u32[]{:S(2)}) %all-to-all-start.1) | async-done | bytes 1048608 | tf_op jit(solution)/shard_map/all_to_all | solution.py:71
  127.5 3.0 %reshape.109 = f32[4,16,4096]{2,1,0:T(8,128)} reshape(f32[32,2,4096]{2,1,0:T(2,128)} %all-to-all-done.1) | data formatting | bytes 2097152 | tf_op jit(solution)/shard_map/reshape | solution.py:74
  130.5 1.3 reduce_sum.51
  131.8 1.1 convolution_convert_fusion.4
  (4 shorter events, 0.1 us)
Async XLA Ops:
  0.6 53.9 %copy-start = (bf16[1,384,4096]{2,1,0:T(8,128)(2,1)S(1)}, bf16[1,384,4096]{2,1,0:T(8,128)(2,1)}, u32[]{:S(2)}) copy-start(bf16[1,384,4096]{2,1,0:T(8,128)(2,1)} %param.11) | copy-start | bytes 9437188
  9.1 23.8 %all-to-all-start = ((bf16[32,2,4096]{2,1,0:T(2,128)(2,1)}), bf16[32,2,4096]{2,1,0:T(2,128)(2,1)}, u32[]{:S(2)}, u32[]{:S(2)}) async-start(bf16[32,2,4096]{2,1,0:T(2,128)(2,1)} %all_to_all.26), calls=%async_computation | async-start | bytes 1048576 | tf_op jit(solution)/shard_map/all_to_all | solution.py:66
  32.9 19.7 %all-to-all-start.2 = ((bf16[32,2,4096]{2,1,0:T(2,128)(2,1)}), bf16[32,2,4096]{2,1,0:T(2,128)(2,1)}, u32[]{:S(2)}, u32[]{:S(2)}) async-start(bf16[32,2,4096]{2,1,0:T(2,128)(2,1)} %all_to_all.30), calls=%async_computation.2 | async-start | bytes 1048576 | tf_op jit(solution)/shard_map/all_to_all | solution.py:67
  38.2 3.2 %copy-start.1 = (bf16[64,4096]{1,0:T(8,128)(2,1)S(1)}, bf16[64,4096]{1,0:T(8,128)(2,1)}, u32[]{:S(2)}) copy-start(bf16[64,4096]{1,0:T(8,128)(2,1)} %all_to_all.28) | copy-start | bytes 1572868
  65.6 30.9 %all-to-all-start.3 = ((f32[32,2,4096]{2,1,0:T(2,128)}), f32[32,2,4096]{2,1,0:T(2,128)}, u32[]{:S(2)}, u32[]{:S(2)}) async-start(f32[32,2,4096]{2,1,0:T(2,128)} %all_to_all.33), calls=%async_computation.3 | async-start | bytes 2097152 | tf_op jit(solution)/shard_map/all_to_all | solution.py:72
  96.6 30.9 %all-to-all-start.1 = ((f32[32,2,4096]{2,1,0:T(2,128)}), f32[32,2,4096]{2,1,0:T(2,128)}, u32[]{:S(2)}, u32[]{:S(2)}) async-start(f32[32,2,4096]{2,1,0:T(2,128)} %copy.44), calls=%async_computation.1 | async-start | bytes 2097152 | tf_op jit(solution)/shard_map/all_to_all | solution.py:71
  100.2 2.2 %copy-start.2 = (bf16[64,4096]{1,0:T(8,128)(2,1)S(1)}, bf16[64,4096]{1,0:T(8,128)(2,1)}, u32[]{:S(2)}) copy-start(bf16[64,4096]{1,0:T(8,128)(2,1)} %all_to_all.28) | copy-start | bytes 1572868
  100.2 3.2 %copy-start.3 = (bf16[64,4096]{1,0:T(8,128)(2,1)S(1)}, bf16[64,4096]{1,0:T(8,128)(2,1)}, u32[]{:S(2)}) copy-start(bf16[64,4096]{1,0:T(8,128)(2,1)} %all_to_all.32) | copy-start | bytes 1572868
where the time goes:
time: 134 us; the launch traced here: 133 us
  waiting for transfers between devices  58.2 us (43%)
  matrix products  25.6 us (19%)
  local copies, waits for them, and re-layouts  22.1 us (16%)
  starting transfers between devices  17.7 us (13%)
  other arithmetic  8.54 us (6%)
    all_to_all x1, waiting for transfers between devices, body(): lax.all_to_all(grad_part, ('tok', 'exp'), split_axis=0, concat_axis=0, ti...  25 us
    all_to_all x1, waiting for transfers between devices, body(): lax.all_to_all(out_part, ('tok', 'exp'), split_axis=0, concat_axis=0, til...  13 us
    all_to_all x1, waiting for transfers between devices, body(): lax.all_to_all(wide_rows, ('tok', 'exp'), split_axis=0, concat_axis=0, ti...  12.1 us
    all_to_all x1, waiting for transfers between devices, body(): lax.all_to_all(wide_cot, ('tok', 'exp'), split_axis=0, concat_axis=0, til...  8.1 us
    all_to_all x1, starting transfers between devices, body(): lax.all_to_all(wide_rows, ('tok', 'exp'), split_axis=0, concat_axis=0, ti...  7.43 us
    all_to_all x2, local copies, waits for them, and re-layouts, body(): lax.all_to_all(wide_rows, ('tok', 'exp'), split_axis=0, concat_axis=0, ti...  4.2 us
    all_to_all x2, local copies, waits for them, and re-layouts, body(): lax.all_to_all(wide_cot, ('tok', 'exp'), split_axis=0, concat_axis=0, til...  4.2 us
    dot_general x1, matrix products, expert_slice(): jnp.dot(up_grad, weight_in[1], preferred_element_type=jnp.float32)  3.57 us
  transfers between devices with their start and end apart: 4, of which 4 were waited for; matrix products, arithmetic and copies ran while one was open for 19% of the time, Pallas kernels for 0%

commit v1 on v0

v1 whole, which is shorter than its diff:
```python
import functools

import jax
import jax.numpy as jnp
from jax import lax
from jax.experimental import pallas as pl
from jax.experimental.pallas import tpu as pltpu
from jax.sharding import Mesh, PartitionSpec as P

CAP = 2
TILE = 16
CHUNKS = TILE // CAP
PAIR = 2
F32 = jnp.float32
BF16 = jnp.bfloat16
LIMIT = 48 * 1024 * 1024


def iota(shape, dim):
    return lax.broadcasted_iota(jnp.int32, shape, dim)


def dot(a, b, dims=((1,), (0,))):
    return lax.dot_general(a, b, (dims, ((), ())), preferred_element_type=F32)


def vmem():
    return pl.BlockSpec(memory_space=pltpu.VMEM)


def params():
    return pltpu.CompilerParams(vmem_limit_bytes=LIMIT)


def folded(ref, rows, width):
    return jnp.concatenate([ref[0:rows, c * width : (c + 1) * width] for c in range(CHUNKS)], axis=0)


def gather_kernel(ids_ref, gates_ref, tok_ref, cot_ref, send_ref, pick_ref, weigh_ref):
    top, rows = ids_ref.shape
    groups, experts, _, width = send_ref.shape
    ids = ids_ref[...]
    gates = gates_ref[...].astype(F32)
    owner = iota((experts, rows), 0)
    member = jnp.zeros((experts, rows), F32)
    gate = jnp.zeros((experts, rows), F32)
    for k in range(top):
        hit = ids[k : k + 1, :] == owner
        member = member + jnp.where(hit, 1.0, 0.0)
        gate = gate + jnp.where(hit, gates[k : k + 1, :], 0.0)
    earlier = jnp.where(iota((rows, rows), 0) < iota((rows, rows), 1), 1.0, 0.0)
    slot = dot(member.astype(BF16), earlier.astype(BF16))
    picks = jnp.concatenate([jnp.where(slot == c, member, 0.0) for c in range(CAP)], axis=0)
    weights = jnp.concatenate([jnp.where(slot == c, gate, 0.0) for c in range(CAP)], axis=0)
    total = experts * TILE
    line = iota((total, CAP * experts), 0)
    spread = jnp.where(
        iota((total, CAP * experts), 1) == (line % CAP) * experts + line // TILE, 1.0, 0.0
    ).astype(BF16)
    repeat = jnp.where(iota((rows, CHUNKS * rows), 1) % rows == iota((rows, CHUNKS * rows), 0), 1.0, 0.0)
    repeat = repeat.astype(BF16)
    shape = (total, CHUNKS * rows)
    chunk = (iota(shape, 0) // CAP) % CHUNKS == iota(shape, 1) // rows
    for part, (table, source, out) in enumerate(
        ((picks, tok_ref, pick_ref), (weights, cot_ref, weigh_ref))
    ):
        small = dot(spread, table.astype(BF16)).astype(BF16)
        wide = jnp.where(chunk, dot(small, repeat), 0.0).astype(BF16)
        out[...] = wide
        moved = dot(wide, folded(source, rows, width)).astype(BF16).reshape(experts, TILE, width)
        for g in range(groups):
            send_ref[g, :, part * TILE : (part + 1) * TILE, :] = moved


def expert_kernel(
    near_ref, far_ref, w_in_ref, w_down_ref,
    keep_ref, away_ref, x_ref, c_ref, hid_ref, gg_ref, ug_ref,
):
    sources, _, width = near_ref.shape
    half = sources * CAP
    lines = sources * TILE
    row, col = iota((lines, lines), 0), iota((lines, lines), 1)
    perm = (row % half // CAP) * TILE + (row // half) * CAP + row % CAP == col
    perm = jnp.where(perm, 1.0, 0.0).astype(BF16)
    for side, ref in enumerate((near_ref, far_ref)):
        for part, out in enumerate((x_ref, c_ref)):
            flat = ref[:, part * TILE : (part + 1) * TILE, :].reshape(lines, width)
            flat = dot(perm, flat).astype(BF16)
            for c in range(CHUNKS):
                out[side * half : (side + 1) * half, c * width : (c + 1) * width] = flat[
                    c * half : (c + 1) * half
                ]
    x = x_ref[...]
    gate = dot(w_in_ref[0], x, ((1,), (1,)))
    up = dot(w_in_ref[1], x, ((1,), (1,)))
    sig = jax.nn.sigmoid(gate)
    silu = gate * sig
    hid = silu * up
    hid_ref[...] = hid.astype(BF16)
    grad = dot(w_down_ref[...], c_ref[...], ((1,), (1,)))
    gg = grad * up * sig * (1.0 + gate * (1.0 - sig))
    ug = grad * silu
    gg_ref[...] = gg.astype(BF16)
    ug_ref[...] = ug.astype(BF16)
    hid_rows = hid.T.astype(BF16)
    gg_rows = gg.T.astype(BF16)
    ug_rows = ug.T.astype(BF16)
    for c in range(CHUNKS):
        cols = pl.ds(c * width, width)
        out = dot(hid_rows, w_down_ref[:, cols])
        back = dot(gg_rows, w_in_ref[0, :, cols]) + dot(ug_rows, w_in_ref[1, :, cols])
        keep_ref[0, :, cols] = out[:half]
        keep_ref[1, :, cols] = back[:half]
        away_ref[0, :, cols] = out[half:].astype(BF16)
        away_ref[1, :, cols] = back[half:].astype(BF16)


def merge_kernel(keep_ref, other_ref, send_ref):
    sources, _, width = send_ref.shape
    half = sources * CAP
    lines = sources * TILE
    row, col = iota((lines, lines), 0), iota((lines, lines), 1)
    perm = (row // CAP % CHUNKS) * half + (row // TILE) * CAP + row % CAP == col
    perm = jnp.where(perm, 1.0, 0.0).astype(BF16)
    for part in range(2):
        pieces = []
        for c in range(CHUNKS):
            cols = pl.ds(c * width, width)
            pieces.append((keep_ref[part, :, cols] + other_ref[part, :, cols].astype(F32)).astype(BF16))
        flat = dot(perm, jnp.concatenate(pieces, axis=0)).astype(BF16)
        send_ref[:, part * TILE : (part + 1) * TILE, :] = flat.reshape(sources, TILE, width)


def weight_kernel(x_ref, c_ref, hid_ref, gg_ref, ug_ref, win_ref, wdown_ref):
    x = x_ref[...]
    win_ref[0] = dot(gg_ref[...], x).astype(BF16)
    win_ref[1] = dot(ug_ref[...], x).astype(BF16)
    wdown_ref[...] = dot(hid_ref[...], c_ref[...]).astype(BF16)


def combine_kernel(back_ref, pick_ref, weigh_ref, moe_ref, grad_ref):
    groups, experts, _, width = back_ref.shape
    rows = moe_ref.shape[0]
    for part, (table, out) in enumerate(((weigh_ref, moe_ref), (pick_ref, grad_ref))):
        total = back_ref[0, :, part * TILE : (part + 1) * TILE, :].astype(F32)
        for g in range(1, groups):
            total = total + back_ref[g, :, part * TILE : (part + 1) * TILE, :].astype(F32)
        flat = total.astype(BF16).reshape(experts * TILE, width)
        wide = dot(table[...], flat, ((0,), (0,))).astype(BF16)
        for c in range(CHUNKS):
            out[:, c * width : (c + 1) * width] = wide[c * rows : (c + 1) * rows]


def body(tokens, cotangent, expert_ids, gate_weights, w_in, w_down):
    groups, experts = lax.axis_size("row"), lax.axis_size("exp")
    rows, depth = tokens.shape
    width = depth // CHUNKS
    sources = groups * experts
    hidden = w_down.shape[1]
    w_in, w_down = w_in[0], w_down[0]
    table = jax.ShapeDtypeStruct((experts * TILE, CHUNKS * rows), BF16)
    send, pick, weigh = pl.pallas_call(
        gather_kernel,
        out_shape=(jax.ShapeDtypeStruct((groups, experts, 2 * TILE, width), BF16), table, table),
        in_specs=[vmem()] * 4,
        out_specs=[vmem()] * 3,
        compiler_params=params(),
        name="gather_rows",
    )(expert_ids.T, gate_weights.T, tokens, cotangent)

    def exchange(array):
        return lax.all_to_all(array, ("row", "exp"), split_axis=0, concat_axis=0, tiled=True)

    def swap(array):
        return lax.ppermute(array, "pair", [(i, PAIR - 1 - i) for i in range(PAIR)])

    near = exchange(send.reshape(sources, 2 * TILE, width))
    far = swap(near)
    half = sources * CAP
    wide = jax.ShapeDtypeStruct((2 * half, depth), BF16)
    tall = jax.ShapeDtypeStruct((hidden, 2 * half), BF16)
    keep, away, x, c, hid, gg, ug = pl.pallas_call(
        expert_kernel,
        out_shape=(
            jax.ShapeDtypeStruct((2, half, depth), F32),
            jax.ShapeDtypeStruct((2, half, depth), BF16),
            wide, wide, tall, tall, tall,
        ),
        in_specs=[vmem()] * 4,
        out_specs=[vmem()] * 7,
        compiler_params=params(),
        name="expert_rows",
    )(near, far, w_in, w_down)
    other = swap(away)
    merged = pl.pallas_call(
        merge_kernel,
        out_shape=jax.ShapeDtypeStruct((sources, 2 * TILE, width), BF16),
        in_specs=[vmem()] * 2,
        out_specs=vmem(),
        compiler_params=params(),
        name="merge_pair",
    )(keep, other)
    back = exchange(merged).reshape(groups, experts, 2 * TILE, width)
    flops = 2 * 3 * hidden * depth * 2 * half
    grad_in, grad_down = pl.pallas_call(
        weight_kernel,
        grid=(CHUNKS,),
        out_shape=(
            jax.ShapeDtypeStruct((2, hidden, depth), BF16),
            jax.ShapeDtypeStruct((hidden, depth), BF16),
        ),
        in_specs=[
            pl.BlockSpec((2 * half, width), lambda i: (0, i)),
            pl.BlockSpec((2 * half, width), lambda i: (0, i)),
        ]
        + [pl.BlockSpec((hidden, 2 * half), lambda i: (0, 0))] * 3,
        out_specs=(
            pl.BlockSpec((2, hidden, width), lambda i: (0, 0, i)),
            pl.BlockSpec((hidden, width), lambda i: (0, i)),
        ),
        compiler_params=params(),
        cost_estimate=pl.CostEstimate(
            flops=flops, bytes_accessed=3 * hidden * depth * 2 + 4 * half * depth, transcendentals=0
        ),
        name="weight_grads",
    )(x, c, hid, gg, ug)
    moe_out, token_grad = pl.pallas_call(
        combine_kernel,
        out_shape=(jax.ShapeDtypeStruct((rows, depth), BF16),) * 2,
        in_specs=[vmem()] * 3,
        out_specs=[vmem()] * 2,
        compiler_params=params(),
        name="combine_rows",
    )(back, pick, weigh)
    return (moe_out, token_grad, grad_in[None], grad_down[None])


def solution(mesh):
    tok, exp = mesh.shape["tok"], mesh.shape["exp"]
    fine = Mesh(mesh.devices.reshape(tok // PAIR, PAIR, exp), ("row", "pair", "exp"))
    rows = P(("row", "pair", "exp"), None)
    win, wdown = P("exp", None, ("row", "pair"), None), P("exp", ("row", "pair"), None)
    return jax.shard_map(
        body,
        mesh=fine,
        in_specs=(rows, rows, rows, rows, win, wdown),
        out_specs=(rows, rows, win, wdown),
        check_vma=False,
    )
```

time: 134 us -> 63.7 us (0.48)
  waiting for transfers between devices: 58.2 us -> 13.2 us
  matrix products: 25.6 us -> 0 us
  blocking collectives: 0 us -> 23.2 us
  Pallas kernels: 0 us -> 18.9 us
  local copies, waits for them, and re-layouts: 22.1 us -> 3.44 us
  starting transfers between devices: 17.7 us -> 3.78 us
  other arithmetic: 8.54 us -> 0 us
    all_to_all x4 -> x1, waiting for transfers between devices: 58.2 us -> 9.57 us  [exchange(): lax.all_to_all(array, ('row', 'exp'), split_axis=0, concat_axis=0, tiled=...]
    dot_general x13 -> x0, matrix products: 25.6 us -> none  [the longest x1 3.57 us: expert_slice(): jnp.dot(up_grad, weight_in[1], preferred_element_type=jnp.float32)]
    all_to_all x0 -> x1, blocking collectives: none -> 23.2 us  [exchange(): lax.all_to_all(array, ('row', 'exp'), split_axis=0, concat_axis=0, tiled=...]
    pallas_call x0 -> x5, Pallas kernels: none -> 18.9 us  [the longest x1 9.69 us: body(): pl.pallas_call(expert_kernel, out_shape=(jax.ShapeDtypeStruct((2, half, d...]
    all_to_all x4 -> x1, starting transfers between devices: 17.7 us -> 3.57 us  [exchange(): lax.all_to_all(array, ('row', 'exp'), split_axis=0, concat_axis=0, tiled=...]
    all_to_all x5 -> x0, local copies, waits for them, and re-layouts: 11.2 us -> none  [the longest x2 4.2 us: body(): lax.all_to_all(wide_rows, ('tok', 'exp'), split_axis=0, concat_axis=0, ti...]
    reshape x2 -> x0, local copies, waits for them, and re-layouts: 5.9 us -> none  [the longest x1 2.98 us: body(): back_out.reshape(groups, experts * CAP, width)]
    another operation x3 -> x0, other arithmetic: 4.43 us -> none  [the longest x1 3.24 us: expert_slice(): grad_in = jnp.stack([grad_gate, grad_up]).astype(jnp.bfloat16)]
  transfers between devices with their start and end apart: 4 -> 3, of which waited for: 4 -> 3; matrix products, arithmetic and copies ran while one was open for 19% -> 0% of each run, Pallas kernels for 0% -> 9%
where the time goes in v1:
time: 63.7 us; the launch traced here: 63.3 us
  blocking collectives  23.2 us (36%)
  Pallas kernels  18.9 us (30%)
  waiting for transfers between devices  13.2 us (21%)
  starting transfers between devices  3.78 us (6%)
  local copies, waits for them, and re-layouts  3.44 us (5%)
  between operations  0.67 us (1%)
    all_to_all x1, blocking collectives, exchange(): lax.all_to_all(array, ('row', 'exp'), split_axis=0, concat_axis=0, tiled=...  23.2 us
    pallas_call x1, Pallas kernels, body(): pl.pallas_call(expert_kernel, out_shape=(jax.ShapeDtypeStruct((2, half, d...  9.69 us
    all_to_all x1, waiting for transfers between devices, exchange(): lax.all_to_all(array, ('row', 'exp'), split_axis=0, concat_axis=0, tiled=...  9.57 us
    pallas_call x1, Pallas kernels, body(): pl.pallas_call(weight_kernel, grid=(CHUNKS,), out_shape=(jax.ShapeDtypeSt...  5.88 us
    ppermute x2, waiting for transfers between devices, swap(): return lax.ppermute(array, 'pair', [(i, PAIR - 1 - i) for i in range(PAIR)])  3.68 us
    all_to_all x1, starting transfers between devices, exchange(): lax.all_to_all(array, ('row', 'exp'), split_axis=0, concat_axis=0, tiled=...  3.57 us
    unnamed x8, local copies, waits for them, and re-layouts  3.44 us
    pallas_call x1, Pallas kernels, body(): pl.pallas_call(combine_kernel, out_shape=(jax.ShapeDtypeStruct((rows, dep...  1.29 us
  transfers between devices with their start and end apart: 3, of which 3 were waited for; matrix products, arithmetic and copies ran while one was open for 0% of the time, Pallas kernels for 9%

profile of v1, /device:TPU:0, one launch (start us, length us, event | category | flops | bytes accessed | tf_op | source)
XLA Modules:
  0.0 63.3 jit_solution(11988465890631847004)
XLA Ops:
  0.6 0.0 copy-start
  0.6 1.0 %copy-done = bf16[64,4096]{1,0:T(8,128)(2,1)S(1)} copy-done((bf16[64,4096]{1,0:T(8,128)(2,1)S(1)}, bf16[64,4096]{1,0:T(8,128)(2,1)}, u32[]{:S(2)}) %copy-start) | copy-done | bytes 524312
  1.7 0.0 copy-start.1
  1.7 1.0 %copy-done.1 = bf16[64,4096]{1,0:T(8,128)(2,1)S(1)} copy-done((bf16[64,4096]{1,0:T(8,128)(2,1)S(1)}, bf16[64,4096]{1,0:T(8,128)(2,1)}, u32[]{:S(2)}) %copy-start.1) | copy-done | bytes 524312
  2.7 0.0 copy-start.2
  2.7 0.7 %copy-done.2 = s32[64,8]{0,1:T(8,128)S(1)} copy-done((s32[64,8]{0,1:T(8,128)S(1)}, s32[64,8]{0,1:T(8,128)}, u32[]{:S(2)}) %copy-start.2) | copy-done | bytes 2072
  3.4 0.0 copy-start.3
  3.4 0.7 %copy-done.3 = bf16[64,8]{0,1:T(8,128)(2,1)S(1)} copy-done((bf16[64,8]{0,1:T(8,128)(2,1)S(1)}, bf16[64,8]{0,1:T(8,128)(2,1)}, u32[]{:S(2)}) %copy-start.3) | copy-done | bytes 1048
  4.1 0.9 %gather_rows.1 = (bf16[2,8,32,512]{3,2,1,0:T(8,128)(2,1)S(1)}, bf16[128,512]{1,0:T(8,128)(2,1)S(1)}, bf16[128,512]{1,0:T(8,128)(2,1)S(1)}) custom-call(s32[8,64]{1,0:T(8,128)S(1)} %bitcast.10, bf16[8,64]{1,0:T(8,128)(2,1)S(1)} %bitcast.11, bf16[64,4096]{1,0:T(8,128)(2,1)S(1)} %copy-done, bf16[64,4096]{1,0:T(8,128)(2,1)S(1)} %copy-done.1), custom_call_target="tpu_custom_call" | custom-call | tf_op jit(solution)/shard_map/gather_rows/pallas_call | solution.py:162
  5.0 23.2 %all_to_all.10.near_ref = bf16[16,32,512]{2,1,0:T(8,128)(2,1)S(1)} all-to-all(bf16[16,32,512]{2,1,0:T(8,128)(2,1)S(1)} %bitcast.9), channel_id=1, replica_groups=mesh['row'=2,'pair'=2,'exp'=8] {'row','exp'}, dimensions={0} | all-to-all | bytes 1048576 | tf_op jit(solution)/shard_map/all_to_all | solution.py:172
  28.2 0.0 collective-permute-start
  28.2 1.9 %collective-permute-done.far_ref = bf16[16,32,512]{2,1,0:T(8,128)(2,1)S(1)} collective-permute-done((bf16[16,32,512]{2,1,0:T(8,128)(2,1)S(1)}, bf16[16,32,512]{2,1,0:T(8,128)(2,1)S(1)}, u32[]{:S(2)}, u32[]{:S(2)}) %collective-permute-start) | collective-permute-done | bytes 524320 | tf_op jit(solution)/shard_map/ppermute | solution.py:175
  30.2 9.7 %expert_rows.1 = (f32[2,32,4096]{2,1,0:T(8,128)S(1)}, bf16[2,32,4096]{2,1,0:T(8,128)(2,1)S(1)}, bf16[64,4096]{1,0:T(8,128)(2,1)S(1)}, bf16[64,4096]{1,0:T(8,128)...) custom-call(bf16[16,32,512]{2,1,0:T(8,128)(2,1)S(1)} %all_to_all.10.near_ref, ...), custom_call_target="tpu_custom_call" | custom-call | tf_op jit(solution)/shard_map/expert_rows/pallas_call | solution.py:182
  39.8 0.2 collective-permute-start.1
  40.1 1.8 %collective-permute-done.1.other_ref = bf16[2,32,4096]{2,1,0:T(8,128)(2,1)S(1)} collective-permute-done((bf16[2,32,4096]{2,1,0:T(8,128)(2,1)S(1)}, bf16[2,32,4096]{2,1,0:T(8,128)(2,1)S(1)}, u32[]{:S(2)}, u32[]{:S(2)}) %collective-permute-start.1) | collective-permute-done | bytes 524320 | tf_op jit(solution)/shard_map/ppermute | solution.py:175
  41.8 1.1 %merge_pair.1 = bf16[16,32,512]{2,1,0:T(8,128)(2,1)} custom-call(f32[2,32,4096]{2,1,0:T(8,128)S(1)} %get-tuple-element.19.keep_ref, bf16[2,32,4096]{2,1,0:T(8,128)(2,1)S(1)} %collective-permute-done.1.other_ref), custom_call_target="tpu_custom_call" | custom-call | tf_op jit(solution)/shard_map/merge_pair/pallas_call | solution.py:195
  43.0 3.6 %all-to-all-start.1 = ((bf16[16,32,512]{2,1,0:T(8,128)(2,1)}), bf16[16,32,512]{2,1,0:T(8,128)(2,1)S(1)}, u32[]{:S(2)}, u32[]{:S(2)}) async-start(bf16[16,32,512]{2,1,0:T(8,128)(2,1)} %merge_pair.1), calls=%async_computation.1 | async-start | bytes 1048576 | tf_op jit(solution)/shard_map/all_to_all | solution.py:172
  46.5 5.9 %weight_grads.1 = (bf16[2,384,4096]{2,1,0:T(8,128)(2,1)}, bf16[384,4096]{1,0:T(8,128)(2,1)}) custom-call(bf16[64,4096]{1,0:T(8,128)(2,1)S(1)} %get-tuple-element.25.x_ref, bf16[64,4096]{1,0:T(8,128)(2,1)S(1)} %get-tuple-element.26.c_ref, bf16[384,64]{1,0:T(8,128)(2,1)S(1)} %get-tuple-element.27.hid_ref, bf16[384,64]{1,0:T(8,128)(2,1)S(1)} %get-tuple-element.28.gg_ref, ...), custom_call_target="tpu_custom_call" | custom-call | flops 603979776 | bytes 9961472 | tf_op jit(solution)/shard_map/weight_grads/pallas_call | solution.py:205
  52.4 9.6 %all-to-all-done.1 = bf16[16,32,512]{2,1,0:T(8,128)(2,1)S(1)} async-done(((bf16[16,32,512]{2,1,0:T(8,128)(2,1)}), bf16[16,32,512]{2,1,0:T(8,128)(2,1)S(1)}, u32[]{:S(2)}, u32[]{:S(2)}) %all-to-all-start.1) | async-done | bytes 524320 | tf_op jit(solution)/shard_map/all_to_all | solution.py:172
  62.0 1.3 %combine_rows.1 = (bf16[64,4096]{1,0:T(8,128)(2,1)}, bf16[64,4096]{1,0:T(8,128)(2,1)}) custom-call(bf16[2,8,32,512]{3,2,1,0:T(8,128)(2,1)S(1)} %bitcast.8, bf16[128,512]{1,0:T(8,128)(2,1)S(1)} %get-tuple-element.21.pick_ref, bf16[128,512]{1,0:T(8,128)(2,1)S(1)} %get-tuple-element.22.weigh_ref), custom_call_target="tpu_custom_call" | custom-call | tf_op jit(solution)/shard_map/combine_rows/pallas_call | solution.py:227
Async XLA Ops:
  0.6 1.0 %copy-start = (bf16[64,4096]{1,0:T(8,128)(2,1)S(1)}, bf16[64,4096]{1,0:T(8,128)(2,1)}, u32[]{:S(2)}) copy-start(bf16[64,4096]{1,0:T(8,128)(2,1)} %tok_ref.1) | copy-start | bytes 1572868
  1.7 1.0 %copy-start.1 = (bf16[64,4096]{1,0:T(8,128)(2,1)S(1)}, bf16[64,4096]{1,0:T(8,128)(2,1)}, u32[]{:S(2)}) copy-start(bf16[64,4096]{1,0:T(8,128)(2,1)} %cot_ref.1) | copy-start | bytes 1572868
  2.7 0.7 %copy-start.2 = (s32[64,8]{0,1:T(8,128)S(1)}, s32[64,8]{0,1:T(8,128)}, u32[]{:S(2)}) copy-start(s32[64,8]{0,1:T(8,128)} %param.8) | copy-start | bytes 6148
  3.4 0.7 %copy-start.3 = (bf16[64,8]{0,1:T(8,128)(2,1)S(1)}, bf16[64,8]{0,1:T(8,128)(2,1)}, u32[]{:S(2)}) copy-start(bf16[64,8]{0,1:T(8,128)(2,1)} %param.9) | copy-start | bytes 3076
  28.2 1.9 %collective-permute-start = (bf16[16,32,512]{2,1,0:T(8,128)(2,1)S(1)}, bf16[16,32,512]{2,1,0:T(8,128)(2,1)S(1)}, u32[]{:S(2)}, u32[]{:S(2)}) collective-permute-start(bf16[16,32,512]{2,1,0:T(8,128)(2,1)S(1)} %all_to_all.10.near_ref), channel_id=1, source_target_pairs={{0,8},{8,0},{1,9},{9,1},{2,10},{10,2},{3,11},{11,3},{4,12},{12,4},... | collective-permute-start | bytes 1572872 | tf_op jit(solution)/shard_map/ppermute | solution.py:175
  39.8 2.0 %collective-permute-start.1 = (bf16[2,32,4096]{2,1,0:T(8,128)(2,1)S(1)}, bf16[2,32,4096]{2,1,0:T(8,128)(2,1)S(1)}, u32[]{:S(2)}, u32[]{:S(2)}) collective-permute-start(bf16[2,32,4096]{2,1,0:T(8,128)(2,1)S(1)} %get-tuple-element.20), channel_id=1, source_target_pairs={{0,8},{8,0},{1,9},{9,1},{2,10},{10,2},{3,11},{11,3},{4,12},{12,4},... | collective-permute-start | bytes 1572872 | tf_op jit(solution)/shard_map/ppermute | solution.py:175
  43.0 19.0 %all-to-all-start.1 = ((bf16[16,32,512]{2,1,0:T(8,128)(2,1)}), bf16[16,32,512]{2,1,0:T(8,128)(2,1)S(1)}, u32[]{:S(2)}, u32[]{:S(2)}) async-start(bf16[16,32,512]{2,1,0:T(8,128)(2,1)} %merge_pair.1), calls=%async_computation.1 | async-start | bytes 1048576 | tf_op jit(solution)/shard_map/all_to_all | solution.py:172

commit v2 on v1

v2 whole, which is shorter than its diff:
```python
import functools

import jax
import jax.numpy as jnp
from jax import lax
from jax.experimental import pallas as pl
from jax.experimental.pallas import tpu as pltpu
from jax.sharding import Mesh, PartitionSpec as P

CAP = 2
TILE = 16
CHUNKS = TILE // CAP
PAIR = 2
F32 = jnp.float32
BF16 = jnp.bfloat16
LIMIT = 24 * 1024 * 1024


def iota(shape, dim):
    return lax.broadcasted_iota(jnp.int32, shape, dim)


def dot(a, b, dims=((1,), (0,))):
    return lax.dot_general(a, b, (dims, ((), ())), preferred_element_type=F32)


def vmem():
    return pl.BlockSpec(memory_space=pltpu.VMEM)


def hbm():
    return pl.BlockSpec(memory_space=pltpu.HBM)


def in_hbm(array):
    return pltpu.with_memory_space_constraint(array, pltpu.HBM)


def params():
    return pltpu.CompilerParams(vmem_limit_bytes=LIMIT)


def folded(ref, rows, width):
    return jnp.concatenate([ref[0:rows, c * width : (c + 1) * width] for c in range(CHUNKS)], axis=0)


def slot_tables(ids, gates, experts):
    top, rows = ids.shape
    gates = gates.astype(F32)
    owner = iota((experts, rows), 0)
    member = jnp.zeros((experts, rows), F32)
    gate = jnp.zeros((experts, rows), F32)
    for k in range(top):
        hit = ids[k : k + 1, :] == owner
        member = member + jnp.where(hit, 1.0, 0.0)
        gate = gate + jnp.where(hit, gates[k : k + 1, :], 0.0)
    earlier = jnp.where(iota((rows, rows), 0) < iota((rows, rows), 1), 1.0, 0.0)
    slot = dot(member.astype(BF16), earlier.astype(BF16))
    picks = jnp.concatenate([jnp.where(slot == c, member, 0.0) for c in range(CAP)], axis=0)
    weights = jnp.concatenate([jnp.where(slot == c, gate, 0.0) for c in range(CAP)], axis=0)
    return picks.astype(BF16), weights.astype(BF16)


def message_masks(experts, rows):
    total = experts * TILE
    line = iota((total, CAP * experts), 0)
    spread = iota((total, CAP * experts), 1) == (line % CAP) * experts + line // TILE
    repeat = iota((rows, CHUNKS * rows), 1) % rows == iota((rows, CHUNKS * rows), 0)
    shape = (total, CHUNKS * rows)
    chunk = (iota(shape, 0) // CAP) % CHUNKS == iota(shape, 1) // rows
    return jnp.where(spread, 1.0, 0.0).astype(BF16), jnp.where(repeat, 1.0, 0.0).astype(BF16), chunk


def widen(table, masks):
    spread, repeat, chunk = masks
    small = dot(spread, table).astype(BF16)
    return jnp.where(chunk, dot(small, repeat), 0.0).astype(BF16)


def gather_kernel(
    ids_hbm, gates_hbm, tok_hbm, cot_hbm,
    send_ref,
    ids_ref, gates_ref, tok_ref, cot_ref, sems,
):
    pairs = ((ids_hbm, ids_ref), (gates_hbm, gates_ref), (tok_hbm, tok_ref), (cot_hbm, cot_ref))
    copies = [pltpu.make_async_copy(a, b, sems.at[i]) for i, (a, b) in enumerate(pairs)]
    for copy in copies:
        copy.start()
    rows = ids_ref.shape[1]
    groups, experts, _, width = send_ref.shape
    masks = message_masks(experts, rows)
    copies[0].wait()
    copies[1].wait()
    tables = slot_tables(ids_ref[...], gates_ref[...], experts)
    wide = [widen(table, masks) for table in tables]
    for part, source in enumerate((tok_ref, cot_ref)):
        copies[2 + part].wait()
        moved = dot(wide[part], folded(source, rows, width)).astype(BF16)
        moved = moved.reshape(experts, TILE, width)
        for g in range(groups):
            send_ref[g, :, part * TILE : (part + 1) * TILE, :] = moved


def table_kernel(ids_ref, gates_ref, after_ref, pick_ref, weigh_ref):
    del after_ref
    rows = ids_ref.shape[1]
    experts = pick_ref.shape[0] // TILE
    masks = message_masks(experts, rows)
    picks, weights = slot_tables(ids_ref[...], gates_ref[...], experts)
    pick_ref[...] = widen(picks, masks)
    weigh_ref[...] = widen(weights, masks)


def unfold(ref, part, perm, out):
    sources, _, width = ref.shape
    half = sources * CAP
    flat = ref[:, part * TILE : (part + 1) * TILE, :].reshape(sources * TILE, width)
    flat = dot(perm, flat).astype(BF16)
    for c in range(CHUNKS):
        out[:, c * width : (c + 1) * width] = flat[c * half : (c + 1) * half]


def unfold_table(sources):
    half, lines = sources * CAP, sources * TILE
    row, col = iota((lines, lines), 0), iota((lines, lines), 1)
    perm = (row % half // CAP) * TILE + (row // half) * CAP + row % CAP == col
    return jnp.where(perm, 1.0, 0.0).astype(BF16)


def near_kernel(near_ref, w_in_hbm, w_down_hbm, w_in_ref, w_down_ref, x_ref, c_ref, sems):
    hidden = w_down_hbm.shape[0]
    part = hidden // 2
    copies = []
    for source, target in (
        (w_in_hbm.at[0], w_in_ref.at[0]),
        (w_in_hbm.at[1], w_in_ref.at[1]),
        (w_down_hbm, w_down_ref),
    ):
        for low in (0, part):
            copies.append(
                pltpu.make_async_copy(
                    source.at[low : low + part], target.at[low : low + part], sems.at[len(copies)]
                )
            )
            copies[-1].start()
    perm = unfold_table(near_ref.shape[0])
    unfold(near_ref, 0, perm, x_ref)
    unfold(near_ref, 1, perm, c_ref)
    for copy in copies:
        copy.wait()


def expert_kernel(
    far_ref, x_near, c_near, w_in_ref, w_down_ref,
    keep_ref, away_ref, x_ref, c_ref, hid_ref, gg_ref, ug_ref,
):
    sources, _, width = far_ref.shape
    half = sources * CAP
    hidden = w_down_ref.shape[0]
    perm = unfold_table(sources)
    x_ref[0:half, :] = x_near[...]
    unfold(far_ref, 0, perm, x_ref.at[half : 2 * half])
    c_ref[0:half, :] = c_near[...]
    unfold(far_ref, 1, perm, c_ref.at[half : 2 * half])
    last = ((1,), (1,))
    both = dot(w_in_ref[...].reshape(2 * hidden, -1), x_ref[...], last)
    grad = dot(w_down_ref[...], c_ref[...], last)
    gate, up = both[:hidden], both[hidden:]
    sig = jax.nn.sigmoid(gate)
    silu = gate * sig
    hid = silu * up
    gg = grad * up * sig * (1.0 + gate * (1.0 - sig))
    ug = grad * silu
    hid_ref[...] = hid.astype(BF16)
    gg_ref[...] = gg.astype(BF16)
    ug_ref[...] = ug.astype(BF16)
    hid_rows = hid.T.astype(BF16)
    grad_rows = jnp.concatenate([gg.T, ug.T], axis=1).astype(BF16)
    for c in range(CHUNKS):
        cols = pl.ds(c * width, width)
        out = dot(hid_rows, w_down_ref[:, cols])
        back = dot(grad_rows, w_in_ref[:, :, cols].reshape(2 * hidden, width))
        keep_ref[0, :, cols] = out[:half]
        keep_ref[1, :, cols] = back[:half]
        away_ref[0, :, cols] = out[half:].astype(BF16)
        away_ref[1, :, cols] = back[half:].astype(BF16)


def merge_kernel(keep_ref, other_ref, send_ref):
    sources, _, width = send_ref.shape
    half = sources * CAP
    lines = sources * TILE
    row, col = iota((lines, lines), 0), iota((lines, lines), 1)
    perm = (row // CAP % CHUNKS) * half + (row // TILE) * CAP + row % CAP == col
    perm = jnp.where(perm, 1.0, 0.0).astype(BF16)
    for part in range(2):
        pieces = []
        for c in range(CHUNKS):
            cols = pl.ds(c * width, width)
            pieces.append((keep_ref[part, :, cols] + other_ref[part, :, cols].astype(F32)).astype(BF16))
        flat = dot(perm, jnp.concatenate(pieces, axis=0)).astype(BF16)
        send_ref[:, part * TILE : (part + 1) * TILE, :] = flat.reshape(sources, TILE, width)


def weight_kernel(x_ref, c_ref, hid_ref, gg_ref, ug_ref, win_ref, wdown_ref):
    x = x_ref[...]
    win_ref[0] = dot(gg_ref[...], x).astype(BF16)
    win_ref[1] = dot(ug_ref[...], x).astype(BF16)
    wdown_ref[...] = dot(hid_ref[...], c_ref[...]).astype(BF16)


def combine_kernel(back_ref, pick_ref, weigh_ref, moe_hbm, grad_hbm, moe_ref, grad_ref, sems):
    groups, experts, _, width = back_ref.shape
    rows = moe_ref.shape[0]
    copies = []
    for part, (table, out, home) in enumerate(
        ((weigh_ref, moe_ref, moe_hbm), (pick_ref, grad_ref, grad_hbm))
    ):
        total = back_ref[0, :, part * TILE : (part + 1) * TILE, :].astype(F32)
        for g in range(1, groups):
            total = total + back_ref[g, :, part * TILE : (part + 1) * TILE, :].astype(F32)
        flat = total.astype(BF16).reshape(experts * TILE, width)
        wide = dot(table[...], flat, ((0,), (0,))).astype(BF16)
        for c in range(CHUNKS):
            out[:, c * width : (c + 1) * width] = wide[c * rows : (c + 1) * rows]
        copies.append(pltpu.make_async_copy(out, home, sems.at[part]))
        copies[-1].start()
    for copy in copies:
        copy.wait()


def body(tokens, cotangent, expert_ids, gate_weights, w_in, w_down):
    groups, experts = lax.axis_size("row"), lax.axis_size("exp")
    rows, depth = tokens.shape
    width = depth // CHUNKS
    sources = groups * experts
    hidden = w_down.shape[1]
    w_in, w_down = in_hbm(w_in[0]), in_hbm(w_down[0])
    ids, gates = expert_ids.T, gate_weights.T
    send = pl.pallas_call(
        gather_kernel,
        out_shape=pltpu.VMEM((groups, experts, 2 * TILE, width), BF16),
        in_specs=[hbm()] * 4,
        out_specs=vmem(),
        scratch_shapes=[
            pltpu.VMEM(ids.shape, ids.dtype),
            pltpu.VMEM(gates.shape, gates.dtype),
            pltpu.VMEM(tokens.shape, tokens.dtype),
            pltpu.VMEM(cotangent.shape, cotangent.dtype),
            pltpu.SemaphoreType.DMA((4,)),
        ],
        compiler_params=params(),
        name="gather_rows",
    )(in_hbm(ids), in_hbm(gates), in_hbm(tokens), in_hbm(cotangent))

    def exchange(array):
        return lax.all_to_all(array, ("row", "exp"), split_axis=0, concat_axis=0, tiled=True)

    def swap(array):
        return lax.ppermute(array, "pair", [(i, PAIR - 1 - i) for i in range(PAIR)])

    near = exchange(send.reshape(sources, 2 * TILE, width))
    far = swap(near)
    half = sources * CAP
    w_in, w_down, x_near, c_near = pl.pallas_call(
        near_kernel,
        out_shape=(pltpu.VMEM(w_in.shape, BF16), pltpu.VMEM(w_down.shape, BF16))
        + (pltpu.VMEM((half, depth), BF16),) * 2,
        in_specs=[vmem(), hbm(), hbm()],
        out_specs=[vmem()] * 4,
        scratch_shapes=[pltpu.SemaphoreType.DMA((6,))],
        compiler_params=params(),
        cost_estimate=pl.CostEstimate(flops=0, bytes_accessed=2 * (w_in.size + w_down.size), transcendentals=0),
        name="near_rows",
    )(near, w_in, w_down)
    wide, tall = (2 * half, depth), (hidden, 2 * half)
    keep, away, x, c, hid, gg, ug = pl.pallas_call(
        expert_kernel,
        out_shape=[pltpu.VMEM((2, half, depth), F32), pltpu.VMEM((2, half, depth), BF16)]
        + [jax.ShapeDtypeStruct(shape, BF16) for shape in (wide, wide, tall, tall, tall)],
        in_specs=[vmem()] * 5,
        out_specs=[vmem()] * 7,
        compiler_params=params(),
        name="expert_rows",
    )(far, x_near, c_near, w_in, w_down)
    other = swap(away)
    merged = pl.pallas_call(
        merge_kernel,
        out_shape=pltpu.VMEM((sources, 2 * TILE, width), BF16),
        in_specs=[vmem()] * 2,
        out_specs=vmem(),
        compiler_params=params(),
        name="merge_pair",
    )(keep, other)
    back = exchange(merged).reshape(groups, experts, 2 * TILE, width)
    flops = 2 * 3 * hidden * depth * 2 * half
    grad_in, grad_down = pl.pallas_call(
        weight_kernel,
        grid=(CHUNKS,),
        out_shape=(
            jax.ShapeDtypeStruct((2, hidden, depth), BF16),
            jax.ShapeDtypeStruct((hidden, depth), BF16),
        ),
        in_specs=[
            pl.BlockSpec((2 * half, width), lambda i: (0, i)),
            pl.BlockSpec((2 * half, width), lambda i: (0, i)),
        ]
        + [pl.BlockSpec((hidden, 2 * half), lambda i: (0, 0))] * 3,
        out_specs=(
            pl.BlockSpec((2, hidden, width), lambda i: (0, 0, i)),
            pl.BlockSpec((hidden, width), lambda i: (0, i)),
        ),
        compiler_params=params(),
        cost_estimate=pl.CostEstimate(
            flops=flops, bytes_accessed=3 * hidden * depth * 2 + 4 * half * depth, transcendentals=0
        ),
        name="weight_grads",
    )(x, c, hid, gg, ug)
    table = pltpu.VMEM((experts * TILE, CHUNKS * rows), BF16)
    pick, weigh = pl.pallas_call(
        table_kernel,
        out_shape=(table, table),
        in_specs=[vmem(), vmem(), pl.BlockSpec(memory_space=pl.ANY)],
        out_specs=[vmem()] * 2,
        compiler_params=params(),
        name="slot_tables",
    )(ids, gates, gg)
    moe_out, token_grad = pl.pallas_call(
        combine_kernel,
        out_shape=(pltpu.HBM((rows, depth), BF16),) * 2,
        in_specs=[vmem()] * 3,
        out_specs=[hbm()] * 2,
        scratch_shapes=[pltpu.VMEM((rows, depth), BF16)] * 2 + [pltpu.SemaphoreType.DMA((2,))],
        compiler_params=params(),
        name="combine_rows",
    )(back, pick, weigh)
    return (moe_out, token_grad, grad_in[None], grad_down[None])


def solution(mesh):
    tok, exp = mesh.shape["tok"], mesh.shape["exp"]
    fine = Mesh(mesh.devices.reshape(tok // PAIR, PAIR, exp), ("row", "pair", "exp"))
    rows = P(("row", "pair", "exp"), None)
    win, wdown = P("exp", None, ("row", "pair"), None), P("exp", ("row", "pair"), None)
    return jax.shard_map(
        body,
        mesh=fine,
        in_specs=(rows, rows, rows, rows, win, wdown),
        out_specs=(rows, rows, win, wdown),
        check_vma=False,
    )
```

time: 63.7 us -> 59.5 us (0.934)
  local copies, waits for them, and re-layouts: 3.44 us -> 0.01 us
  waiting for transfers between devices: 13.2 us -> 10.7 us
  Pallas kernels: 18.9 us -> 20.4 us
    unnamed x8 -> x4, local copies, waits for them, and re-layouts: 3.44 us -> 0.01 us
    ppermute x2, waiting for transfers between devices: 3.68 us -> 1.54 us  [swap(): return lax.ppermute(array, 'pair', [(i, PAIR - 1 - i) for i in range(PAIR)])]
    pallas_call x4 -> x6, Pallas kernels: 13 us -> 14.5 us  [the longest x1 5.91 us: body(): pl.pallas_call(expert_kernel, out_shape=[pltpu.VMEM((2, half, depth), F32...]
  transfers between devices with their start and end apart: 3 -> 3, of which waited for: 3 -> 2; matrix products, arithmetic and copies ran while one was open for 0% -> 0% of each run, Pallas kernels for 9% -> 17%
where the time goes in v2:
time: 59.5 us; the launch traced here: 59.3 us
  blocking collectives  23.3 us (39%)
  Pallas kernels  20.4 us (34%)
  waiting for transfers between devices  10.7 us (18%)
  starting transfers between devices  4.15 us (7%)
  between operations  0.71 us (1%)
    all_to_all x1, blocking collectives, exchange(): lax.all_to_all(array, ('row', 'exp'), split_axis=0, concat_axis=0, tiled=...  23.3 us
    all_to_all x1, waiting for transfers between devices, exchange(): lax.all_to_all(array, ('row', 'exp'), split_axis=0, concat_axis=0, tiled=...  9.18 us
    pallas_call x1, Pallas kernels, body(): pl.pallas_call(expert_kernel, out_shape=[pltpu.VMEM((2, half, depth), F32...  5.91 us
    pallas_call x1, Pallas kernels, body(): pl.pallas_call(weight_kernel, grid=(CHUNKS,), out_shape=(jax.ShapeDtypeSt...  5.88 us
    pallas_call x1, Pallas kernels, body(): pl.pallas_call(near_kernel, out_shape=(pltpu.VMEM(w_in.shape, BF16), pltp...  3.82 us
    all_to_all x1, starting transfers between devices, exchange(): lax.all_to_all(array, ('row', 'exp'), split_axis=0, concat_axis=0, tiled=...  3.58 us
    pallas_call x1, Pallas kernels, body(): pl.pallas_call(gather_kernel, out_shape=pltpu.VMEM((groups, experts, 2 *...  1.78 us
    ppermute x2, waiting for transfers between devices, swap(): return lax.ppermute(array, 'pair', [(i, PAIR - 1 - i) for i in range(PAIR)])  1.54 us
  transfers between devices with their start and end apart: 3, of which 2 were waited for; matrix products, arithmetic and copies ran while one was open for 0% of the time, Pallas kernels for 17%

profile of v2, /device:TPU:0, one launch (start us, length us, event | category | flops | bytes accessed | tf_op | source)
XLA Modules:
  0.0 59.3 jit_solution(3217912742903081953)
XLA Ops:
  0.6 1.8 %gather_rows.1 = bf16[2,8,32,512]{3,2,1,0:T(8,128)(2,1)S(1)} custom-call(s32[8,64]{1,0:T(8,128)} %bitcast.10, bf16[8,64]{1,0:T(8,128)(2,1)} %bitcast.12, bf16[64,4096]{1,0:T(8,128)(2,1)} %tok_hbm.1, bf16[64,4096]{1,0:T(8,128)(2,1)} %cot_hbm.1), custom_call_target="tpu_custom_call" | custom-call | tf_op jit(solution)/shard_map/gather_rows/pallas_call | solution.py:240
  2.4 23.3 %all_to_all.10.near_ref = bf16[16,32,512]{2,1,0:T(8,128)(2,1)S(1)} all-to-all(bf16[16,32,512]{2,1,0:T(8,128)(2,1)S(1)} %bitcast.9), channel_id=1, replica_groups=mesh['row'=2,'pair'=2,'exp'=8] {'row','exp'}, dimensions={0} | all-to-all | bytes 1048576 | tf_op jit(solution)/shard_map/all_to_all | solution.py:257
  25.7 0.0 collective-permute-start
  25.7 3.8 %near_rows.1 = (bf16[2,384,4096]{2,1,0:T(8,128)(2,1)S(1)}, bf16[384,4096]{1,0:T(8,128)(2,1)S(1)}, bf16[32,4096]{1,0:T(8,128)(2,1)S(1)}, bf16[32,4096]{1,0:T(8,128)(2,1)S(1)}) custom-call(bf16[16,32,512]{2,1,0:T(8,128)(2,1)S(1)} %all_to_all.10.near_ref, bf16[2,384,4096]{2,1,0:T(8,128)(2,1)} %bitcast.14, bf16[384,4096]{1,0:T(8,128)(2,1)} %bitcast.15), custom_call_target="tpu_custom_call" | custom-call | bytes 9437184 | tf_op jit(solution)/shard_map/near_rows/pallas_call | solution.py:265
  29.5 0.0 collective-permute-done.far_ref
  29.5 0.0 copy-start
  29.5 0.0 copy-start.1
  29.5 5.9 %expert_rows.1 = (f32[2,32,4096]{2,1,0:T(8,128)S(1)}, bf16[2,32,4096]{2,1,0:T(8,128)(2,1)S(1)}, bf16[64,4096]{1,0:T(8,128)(2,1)S(1)}, bf16[64,4096]{1,0:T(8,128)...) custom-call(bf16[16,32,512]{2,1,0:T(8,128)(2,1)S(1)} %collective-permute-done.far_r, ...), custom_call_target="tpu_custom_call" | custom-call | tf_op jit(solution)/shard_map/expert_rows/pallas_call | solution.py:277
  35.5 0.6 collective-permute-start.1
  36.0 1.5 %collective-permute-done.1.other_ref = bf16[2,32,4096]{2,1,0:T(8,128)(2,1)S(1)} collective-permute-done((bf16[2,32,4096]{2,1,0:T(8,128)(2,1)S(1)}, bf16[2,32,4096]{2,1,0:T(8,128)(2,1)S(1)}, u32[]{:S(2)}, u32[]{:S(2)}) %collective-permute-start.1) | collective-permute-done | bytes 524320 | tf_op jit(solution)/shard_map/ppermute | solution.py:260
  37.6 1.1 %merge_pair.1 = bf16[16,32,512]{2,1,0:T(8,128)(2,1)} custom-call(f32[2,32,4096]{2,1,0:T(8,128)S(1)} %get-tuple-element.25.keep_ref, bf16[2,32,4096]{2,1,0:T(8,128)(2,1)S(1)} %collective-permute-done.1.other_ref), custom_call_target="tpu_custom_call" | custom-call | tf_op jit(solution)/shard_map/merge_pair/pallas_call | solution.py:287
  38.7 3.6 %all-to-all-start.1 = ((bf16[16,32,512]{2,1,0:T(8,128)(2,1)}), bf16[16,32,512]{2,1,0:T(8,128)(2,1)S(1)}, u32[]{:S(2)}, u32[]{:S(2)}) async-start(bf16[16,32,512]{2,1,0:T(8,128)(2,1)} %merge_pair.1), calls=%async_computation.1 | async-start | bytes 1048576 | tf_op jit(solution)/shard_map/all_to_all | solution.py:257
  42.3 0.0 copy-done
  42.3 0.0 copy-done.1
  42.3 0.6 slot_tables.1
  42.9 5.9 %weight_grads.1 = (bf16[2,384,4096]{2,1,0:T(8,128)(2,1)}, bf16[384,4096]{1,0:T(8,128)(2,1)}) custom-call(bf16[64,4096]{1,0:T(8,128)(2,1)S(1)} %get-tuple-element.32.x_ref, bf16[64,4096]{1,0:T(8,128)(2,1)S(1)} %get-tuple-element.33.c_ref, bf16[384,64]{1,0:T(8,128)(2,1)S(1)} %get-tuple-element.34.hid_ref, ...), custom_call_target="tpu_custom_call" | custom-call | flops 603979776 | bytes 9961472 | tf_op jit(solution)/shard_map/weight_grads/pallas_call | solution.py:297
  48.8 9.2 %all-to-all-done.1 = bf16[16,32,512]{2,1,0:T(8,128)(2,1)S(1)} async-done(((bf16[16,32,512]{2,1,0:T(8,128)(2,1)}), bf16[16,32,512]{2,1,0:T(8,128)(2,1)S(1)}, u32[]{:S(2)}, u32[]{:S(2)}) %all-to-all-start.1) | async-done | bytes 524320 | tf_op jit(solution)/shard_map/all_to_all | solution.py:257
  57.9 1.3 %combine_rows.1 = (bf16[64,4096]{1,0:T(8,128)(2,1)}, bf16[64,4096]{1,0:T(8,128)(2,1)}) custom-call(bf16[2,8,32,512]{3,2,1,0:T(8,128)(2,1)S(1)} %bitcast.8, bf16[128,512]{1,0:T(8,128)(2,1)S(1)} %get-tuple-element.28.pick_ref, bf16[128,512]{1,0:T(8,128)(2,1)S(1)} %get-tuple-element.29.weigh_ref), custom_call_target="tpu_custom_call" | custom-call | tf_op jit(solution)/shard_map/combine_rows/pallas_call | solution.py:328
Async XLA Ops:
  25.7 3.8 %collective-permute-start = (bf16[16,32,512]{2,1,0:T(8,128)(2,1)S(1)}, bf16[16,32,512]{2,1,0:T(8,128)(2,1)S(1)}, u32[]{:S(2)}, u32[]{:S(2)}) collective-permute-start(bf16[16,32,512]{2,1,0:T(8,128)(2,1)S(1)} %all_to_all.10.near_ref), channel_id=1, source_target_pairs={{0,8},{8,0},{1,9},{9,1},{2,10},{10,2},{3,11},{11,3},{4,12},{12,4},... | collective-permute-start | bytes 1572872 | tf_op jit(solution)/shard_map/ppermute | solution.py:260
  29.5 12.8 %copy-start = (s32[64,8]{0,1:T(8,128)S(1)}, s32[64,8]{0,1:T(8,128)}, u32[]{:S(2)}) copy-start(s32[64,8]{0,1:T(8,128)} %param.8) | copy-start | bytes 6148
  29.5 12.8 %copy-start.1 = (bf16[64,8]{0,1:T(8,128)(2,1)S(1)}, bf16[64,8]{0,1:T(8,128)(2,1)}, u32[]{:S(2)}) copy-start(bf16[64,8]{0,1:T(8,128)(2,1)} %param.9) | copy-start | bytes 3076
  35.5 2.1 %collective-permute-start.1 = (bf16[2,32,4096]{2,1,0:T(8,128)(2,1)S(1)}, bf16[2,32,4096]{2,1,0:T(8,128)(2,1)S(1)}, u32[]{:S(2)}, u32[]{:S(2)}) collective-permute-start(bf16[2,32,4096]{2,1,0:T(8,128)(2,1)S(1)} %get-tuple-element.26), channel_id=1, source_target_pairs={{0,8},{8,0},{1,9},{9,1},{2,10},{10,2},{3,11},{11,3},{4,12},{12,4},... | collective-permute-start | bytes 1572872 | tf_op jit(solution)/shard_map/ppermute | solution.py:260
  38.7 19.2 %all-to-all-start.1 = ((bf16[16,32,512]{2,1,0:T(8,128)(2,1)}), bf16[16,32,512]{2,1,0:T(8,128)(2,1)S(1)}, u32[]{:S(2)}, u32[]{:S(2)}) async-start(bf16[16,32,512]{2,1,0:T(8,128)(2,1)} %merge_pair.1), calls=%async_computation.1 | async-start | bytes 1048576 | tf_op jit(solution)/shard_map/all_to_all | solution.py:257

commit v3 on v2

v3 whole, which is shorter than its diff:
```python
import functools

import jax
import jax.numpy as jnp
import numpy as np
from jax import lax
from jax.experimental import pallas as pl
from jax.experimental.pallas import tpu as pltpu
from jax.sharding import Mesh, PartitionSpec as P

CAP = 2
TILE = 16
CHUNKS = TILE // CAP
PAIR = 2
STEPS = 2
ORDER_SEED = 2
F32 = jnp.float32
BF16 = jnp.bfloat16
LIMIT = 24 * 1024 * 1024


def iota(shape, dim):
    return lax.broadcasted_iota(jnp.int32, shape, dim)


def dot(a, b, dims=((1,), (0,))):
    return lax.dot_general(a, b, (dims, ((), ())), preferred_element_type=F32)


def vmem():
    return pl.BlockSpec(memory_space=pltpu.VMEM)


def hbm():
    return pl.BlockSpec(memory_space=pltpu.HBM)


def in_hbm(array):
    return pltpu.with_memory_space_constraint(array, pltpu.HBM)


def params():
    return pltpu.CompilerParams(vmem_limit_bytes=LIMIT)


def cost(flops, moved):
    return pl.CostEstimate(flops=flops, bytes_accessed=moved, transcendentals=0)


def slot_tables(ids, gates, experts):
    top, rows = ids.shape
    gates = gates.astype(F32)
    owner = iota((experts, rows), 0)
    member = jnp.zeros((experts, rows), F32)
    gate = jnp.zeros((experts, rows), F32)
    for k in range(top):
        hit = ids[k : k + 1, :] == owner
        member = member + jnp.where(hit, 1.0, 0.0)
        gate = gate + jnp.where(hit, gates[k : k + 1, :], 0.0)
    earlier = jnp.where(iota((rows, rows), 0) < iota((rows, rows), 1), 1.0, 0.0)
    slot = dot(member.astype(BF16), earlier.astype(BF16))
    picks = jnp.concatenate([jnp.where(slot == c, member, 0.0) for c in range(CAP)], axis=0)
    weights = jnp.concatenate([jnp.where(slot == c, gate, 0.0) for c in range(CAP)], axis=0)
    return picks.astype(BF16), weights.astype(BF16)


def message_masks(experts, rows):
    total = experts * TILE
    line = iota((total, CAP * experts), 0)
    spread = iota((total, CAP * experts), 1) == (line % CAP) * experts + line // TILE
    repeat = iota((rows, CHUNKS * rows), 1) % rows == iota((rows, CHUNKS * rows), 0)
    shape = (total, CHUNKS * rows)
    chunk = (iota(shape, 0) // CAP) % CHUNKS == iota(shape, 1) // rows
    return jnp.where(spread, 1.0, 0.0).astype(BF16), jnp.where(repeat, 1.0, 0.0).astype(BF16), chunk


def widen(table, masks):
    spread, repeat, chunk = masks
    small = dot(spread, table).astype(BF16)
    return jnp.where(chunk, dot(small, repeat), 0.0).astype(BF16)


def gather_kernel(
    owners, ids_hbm, gates_hbm, tok_hbm, cot_hbm,
    send_ref,
    ids_ref, gates_ref, tok_ref, cot_ref, sems,
):
    rows, depth = tok_ref.shape
    width = depth // CHUNKS
    experts = max(owners) + 1
    pairs = ((ids_hbm, ids_ref), (gates_hbm, gates_ref), (tok_hbm, tok_ref), (cot_hbm, cot_ref))
    copies = [pltpu.make_async_copy(a, b, sems.at[i]) for i, (a, b) in enumerate(pairs)]
    for copy in copies:
        copy.start()
    masks = message_masks(experts, rows)
    copies[0].wait()
    copies[1].wait()
    tables = slot_tables(ids_ref[...], gates_ref[...], experts)
    wide = [widen(table, masks) for table in tables]
    for part, source in enumerate((tok_ref, cot_ref)):
        copies[2 + part].wait()
        folded = jnp.concatenate(
            [source[:, c * width : (c + 1) * width] for c in range(CHUNKS)], axis=0
        )
        moved = dot(wide[part], folded).astype(BF16).reshape(experts, TILE, width)
        for place, owner in enumerate(owners):
            send_ref[place, part * TILE : (part + 1) * TILE, :] = moved[owner]


def table_kernel(ids_ref, gates_ref, after_ref, pick_ref, weigh_ref):
    del after_ref
    rows = ids_ref.shape[1]
    experts = pick_ref.shape[1] // TILE
    masks = message_masks(experts, rows)
    picks, weights = slot_tables(ids_ref[...], gates_ref[...], experts)
    pick_ref[...] = widen(picks, masks).T
    weigh_ref[...] = widen(weights, masks).T


def unfold(ref, part, perm, out):
    sources, _, width = ref.shape
    half = sources * CAP
    flat = ref[:, part * TILE : (part + 1) * TILE, :].reshape(sources * TILE, width)
    flat = dot(perm, flat).astype(BF16)
    for c in range(CHUNKS):
        out[:, c * width : (c + 1) * width] = flat[c * half : (c + 1) * half]


def near_kernel(near_ref, w_in_hbm, w_in_ref, x_ref, c_ref, unfold_ref, fold_ref, sem):
    fetch = pltpu.make_async_copy(w_in_hbm, w_in_ref, sem)
    fetch.start()
    sources = near_ref.shape[0]
    half, lines = sources * CAP, sources * TILE
    row, col = iota((lines, lines), 0), iota((lines, lines), 1)
    perm = (row % half // CAP) * TILE + (row // half) * CAP + row % CAP == col
    perm = jnp.where(perm, 1.0, 0.0).astype(BF16)
    unfold_ref[...] = perm
    back = (row // CAP % CHUNKS) * half + (row // TILE) * CAP + row % CAP == col
    fold_ref[...] = jnp.where(back, 1.0, 0.0).astype(BF16)
    unfold(near_ref, 0, perm, x_ref)
    unfold(near_ref, 1, perm, c_ref)
    fetch.wait()


def forward_kernel(
    far_ref, x_near, unfold_ref, w_in_ref, w_down_hbm,
    x_ref, hid_ref, gate_slope_ref, up_slope_ref, w_down_ref, sem,
):
    fetch = pltpu.make_async_copy(w_down_hbm, w_down_ref, sem)
    fetch.start()
    hidden = w_down_ref.shape[0]
    half = far_ref.shape[0] * CAP
    x_ref[0:half, :] = x_near[...]
    unfold(far_ref, 0, unfold_ref[...], x_ref.at[half : 2 * half])
    both = dot(w_in_ref[...].reshape(2 * hidden, -1), x_ref[...], ((1,), (1,)))
    gate, up = both[:hidden], both[hidden:]
    sig = jax.nn.sigmoid(gate)
    silu = gate * sig
    hid_ref[...] = (silu * up).astype(BF16)
    gate_slope_ref[...] = up * sig * (1.0 + gate * (1.0 - sig))
    up_slope_ref[...] = silu
    fetch.wait()


def split_rows(value, cols, keep_ref, away_ref):
    half = keep_ref.shape[0]
    keep_ref[:, cols] = value[:half]
    away_ref[:, cols] = value[half:].astype(BF16)


def down_kernel(hid_ref, w_down_ref, keep_ref, away_ref):
    width = w_down_ref.shape[1] // CHUNKS
    rows = hid_ref[...].T
    for c in range(CHUNKS):
        cols = pl.ds(c * width, width)
        split_rows(dot(rows, w_down_ref[:, cols]), cols, keep_ref, away_ref)


def hidden_kernel(
    far_ref, c_near, unfold_ref, w_down_ref, gate_slope_ref, up_slope_ref, c_ref, gg_ref, ug_ref
):
    half = far_ref.shape[0] * CAP
    c_ref[0:half, :] = c_near[...]
    unfold(far_ref, 1, unfold_ref[...], c_ref.at[half : 2 * half])
    grad = dot(w_down_ref[...], c_ref[...], ((1,), (1,)))
    gg_ref[...] = (grad * gate_slope_ref[...]).astype(BF16)
    ug_ref[...] = (grad * up_slope_ref[...]).astype(BF16)


def back_kernel(gg_ref, ug_ref, w_in_ref, keep_ref, away_ref):
    width = w_in_ref.shape[2] // CHUNKS
    gate_rows, up_rows = gg_ref[...].T, ug_ref[...].T
    for c in range(CHUNKS):
        cols = pl.ds(c * width, width)
        value = dot(gate_rows, w_in_ref[0, :, cols]) + dot(up_rows, w_in_ref[1, :, cols])
        split_rows(value, cols, keep_ref, away_ref)


def merge_rows(part, fold_ref, keep_ref, other_ref, send_hbm, send_ref, sems):
    sources, _, width = send_ref.shape
    pieces = []
    for c in range(CHUNKS):
        cols = pl.ds(c * width, width)
        pieces.append((keep_ref[:, cols] + other_ref[:, cols].astype(F32)).astype(BF16))
    flat = jnp.concatenate(pieces, axis=0)
    each = sources // STEPS
    copies = []
    for step in range(STEPS):
        here = pl.ds(step * each, each)
        rows = dot(fold_ref[step * each * TILE : (step + 1) * each * TILE, :], flat).astype(BF16)
        send_ref[here] = rows.reshape(each, TILE, width)
        copies.append(
            pltpu.make_async_copy(
                send_ref.at[here], send_hbm.at[here, part * TILE : (part + 1) * TILE, :], sems.at[step]
            )
        )
        copies[-1].start()
    for copy in copies:
        copy.wait()


def merge_first_kernel(fold_ref, keep_ref, other_ref, send_hbm, send_ref, sems):
    merge_rows(0, fold_ref, keep_ref, other_ref, send_hbm, send_ref, sems)


def merge_second_kernel(fold_ref, keep_ref, other_ref, first_hbm, send_hbm, send_ref, sems):
    del first_hbm
    merge_rows(1, fold_ref, keep_ref, other_ref, send_hbm, send_ref, sems)


def weight_kernel(x_ref, c_ref, hid_ref, gg_ref, ug_ref, win_ref, wdown_ref):
    x = x_ref[...]
    win_ref[0] = dot(gg_ref[...], x).astype(BF16)
    win_ref[1] = dot(ug_ref[...], x).astype(BF16)
    wdown_ref[...] = dot(hid_ref[...], c_ref[...]).astype(BF16)


def combine_kernel(places, back_ref, pick_ref, weigh_ref, moe_hbm, grad_hbm, moe_ref, grad_ref, sems):
    width = back_ref.shape[2]
    rows = moe_ref.shape[0]
    reach = CHUNKS // STEPS
    copies = []
    for part, (table, out, home) in enumerate(
        ((weigh_ref, moe_ref, moe_hbm), (pick_ref, grad_ref, grad_hbm))
    ):
        lines = slice(part * TILE, (part + 1) * TILE)
        sums = []
        for spots in places:
            total = back_ref[spots[0], lines, :].astype(F32)
            for spot in spots[1:]:
                total = total + back_ref[spot, lines, :].astype(F32)
            sums.append(total.astype(BF16))
        flat = jnp.concatenate(sums, axis=0)
        for step in range(STEPS):
            low = step * reach
            wide = dot(table[low * rows : (low + reach) * rows, :], flat).astype(BF16)
            for c in range(reach):
                out[:, (low + c) * width : (low + c + 1) * width] = wide[c * rows : (c + 1) * rows]
            cols = pl.ds(low * width, reach * width)
            copies.append(pltpu.make_async_copy(out.at[:, cols], home.at[:, cols], sems.at[len(copies)]))
            copies[-1].start()
    for copy in copies:
        copy.wait()


def body(tokens, cotangent, expert_ids, gate_weights, w_in, w_down):
    groups, experts = lax.axis_size("row"), lax.axis_size("exp")
    rows, depth = tokens.shape
    width = depth // CHUNKS
    sources = groups * experts
    half = sources * CAP
    hidden = w_down.shape[1]
    w_in, w_down = in_hbm(w_in[0]), in_hbm(w_down[0])
    ids, gates = expert_ids.T, gate_weights.T
    order = [int(r) for r in np.random.RandomState(ORDER_SEED).permutation(sources)]
    owners = tuple(r % experts for r in order)
    places = tuple(
        tuple(order.index(g * experts + e) for g in range(groups)) for e in range(experts)
    )
    planes = [[(r // experts * PAIR + p) * experts + r % experts for r in order] for p in range(PAIR)]

    def exchange(array):
        return lax.all_to_all(
            array, ("row", "pair", "exp"), split_axis=0, concat_axis=0, tiled=True,
            axis_index_groups=planes,
        )

    def swap(array):
        return lax.ppermute(array, "pair", [(i, PAIR - 1 - i) for i in range(PAIR)])

    send = pl.pallas_call(
        functools.partial(gather_kernel, owners),
        out_shape=pltpu.VMEM((sources, 2 * TILE, width), BF16),
        in_specs=[hbm()] * 4,
        out_specs=vmem(),
        scratch_shapes=[
            pltpu.VMEM(ids.shape, ids.dtype),
            pltpu.VMEM(gates.shape, gates.dtype),
            pltpu.VMEM(tokens.shape, tokens.dtype),
            pltpu.VMEM(cotangent.shape, cotangent.dtype),
            pltpu.SemaphoreType.DMA((4,)),
        ],
        compiler_params=params(),
        name="gather_rows",
    )(in_hbm(ids), in_hbm(gates), in_hbm(tokens), in_hbm(cotangent))
    near = exchange(send)
    far = swap(near)
    square = pltpu.VMEM((sources * TILE, sources * TILE), BF16)
    w_in, x_near, c_near, unfolding, folding = pl.pallas_call(
        near_kernel,
        out_shape=(pltpu.VMEM(w_in.shape, BF16),)
        + (pltpu.VMEM((half, depth), BF16),) * 2
        + (square,) * 2,
        in_specs=[vmem(), hbm()],
        out_specs=[vmem()] * 5,
        scratch_shapes=[pltpu.SemaphoreType.DMA],
        compiler_params=params(),
        cost_estimate=cost(0, 4 * w_in.size),
        name="near_rows",
    )(near, w_in)
    wide = jax.ShapeDtypeStruct((2 * half, depth), BF16)
    tall = jax.ShapeDtypeStruct((hidden, 2 * half), BF16)
    slope = pltpu.VMEM(tall.shape, F32)
    x, hid, gate_slope, up_slope, w_down = pl.pallas_call(
        forward_kernel,
        out_shape=(wide, tall, slope, slope, pltpu.VMEM(w_down.shape, BF16)),
        in_specs=[vmem()] * 4 + [hbm()],
        out_specs=[vmem()] * 5,
        scratch_shapes=[pltpu.SemaphoreType.DMA],
        compiler_params=params(),
        name="gate_up",
    )(far, x_near, unfolding, w_in, w_down)
    halves = (pltpu.VMEM((half, depth), F32), pltpu.VMEM((half, depth), BF16))
    passes = 4 * hidden * depth * half
    keep_out, away_out = pl.pallas_call(
        down_kernel,
        out_shape=halves,
        in_specs=[vmem()] * 2,
        out_specs=[vmem()] * 2,
        compiler_params=params(),
        name="down",
    )(hid, w_down)
    other_out = swap(away_out)
    c, gg, ug = pl.pallas_call(
        hidden_kernel,
        out_shape=(wide, tall, tall),
        in_specs=[vmem()] * 6,
        out_specs=[vmem()] * 3,
        compiler_params=params(),
        cost_estimate=cost(passes, 2 * w_down.size),
        name="hidden_grad",
    )(far, c_near, unfolding, w_down, gate_slope, up_slope)
    keep_grad, away_grad = pl.pallas_call(
        back_kernel,
        out_shape=halves,
        in_specs=[vmem()] * 3,
        out_specs=[vmem()] * 2,
        compiler_params=params(),
        cost_estimate=cost(2 * passes, 2 * w_in.size),
        name="input_grad",
    )(gg, ug, w_in)
    other_grad = swap(away_grad)
    packet = pltpu.HBM((sources, 2 * TILE, width), BF16)
    staging = [pltpu.VMEM((sources, TILE, width), BF16), pltpu.SemaphoreType.DMA((STEPS,))]
    merged = pl.pallas_call(
        merge_first_kernel,
        out_shape=packet,
        in_specs=[vmem()] * 3,
        out_specs=hbm(),
        scratch_shapes=staging,
        compiler_params=params(),
        cost_estimate=cost(0, 8 * half * depth),
        name="merge_out",
    )(folding, keep_out, other_out)
    merged = pl.pallas_call(
        merge_second_kernel,
        out_shape=packet,
        in_specs=[vmem()] * 3 + [hbm()],
        out_specs=hbm(),
        scratch_shapes=staging,
        input_output_aliases={3: 0},
        compiler_params=params(),
        name="merge_grad",
    )(folding, keep_grad, other_grad, merged)
    back = exchange(merged)
    grad_in, grad_down = pl.pallas_call(
        weight_kernel,
        grid=(CHUNKS,),
        out_shape=(
            jax.ShapeDtypeStruct((2, hidden, depth), BF16),
            jax.ShapeDtypeStruct((hidden, depth), BF16),
        ),
        in_specs=[pl.BlockSpec((2 * half, width), lambda i: (0, i))] * 2
        + [pl.BlockSpec((hidden, 2 * half), lambda i: (0, 0))] * 3,
        out_specs=(
            pl.BlockSpec((2, hidden, width), lambda i: (0, 0, i)),
            pl.BlockSpec((hidden, width), lambda i: (0, i)),
        ),
        compiler_params=params(),
        cost_estimate=cost(3 * passes, 6 * hidden * depth + 8 * half * depth),
        name="weight_grads",
    )(x, c, hid, gg, ug)
    table = pltpu.VMEM((CHUNKS * rows, experts * TILE), BF16)
    pick, weigh = pl.pallas_call(
        table_kernel,
        out_shape=(table, table),
        in_specs=[vmem(), vmem(), pl.BlockSpec(memory_space=pl.ANY)],
        out_specs=[vmem()] * 2,
        compiler_params=params(),
        name="slot_tables",
    )(ids, gates, gg)
    moe_out, token_grad = pl.pallas_call(
        functools.partial(combine_kernel, places),
        out_shape=(pltpu.HBM((rows, depth), BF16),) * 2,
        in_specs=[vmem()] * 3,
        out_specs=[hbm()] * 2,
        scratch_shapes=[pltpu.VMEM((rows, depth), BF16)] * 2
        + [pltpu.SemaphoreType.DMA((2 * STEPS,))],
        compiler_params=params(),
        name="combine_rows",
    )(back, pick, weigh)
    return (moe_out, token_grad, grad_in[None], grad_down[None])


def solution(mesh):
    tok, exp = mesh.shape["tok"], mesh.shape["exp"]
    fine = Mesh(mesh.devices.reshape(tok // PAIR, PAIR, exp), ("row", "pair", "exp"))
    rows = P(("row", "pair", "exp"), None)
    win, wdown = P("exp", None, ("row", "pair"), None), P("exp", ("row", "pair"), None)
    return jax.shard_map(
        body,
        mesh=fine,
        in_specs=(rows, rows, rows, rows, win, wdown),
        out_specs=(rows, rows, win, wdown),
        check_vma=False,
    )
```

time: 59.5 us -> 54.7 us (0.919)
  waiting for transfers between devices: 10.7 us -> 6.73 us
  starting transfers between devices: 4.15 us -> 6.98 us
  blocking collectives: 23.3 us -> 20.7 us
  Pallas kernels: 20.4 us -> 19.2 us
    all_to_all x1, waiting for transfers between devices: 9.18 us -> 6.15 us  [exchange(): lax.all_to_all(array, ('row', 'pair', 'exp'), split_axis=0, concat_axis=0...]
    all_to_all x1, starting transfers between devices: 3.58 us -> 6.32 us  [exchange(): lax.all_to_all(array, ('row', 'pair', 'exp'), split_axis=0, concat_axis=0...]
    all_to_all x1, blocking collectives: 23.3 us -> 20.7 us  [exchange(): lax.all_to_all(array, ('row', 'pair', 'exp'), split_axis=0, concat_axis=0...]
    pallas_call x5 -> x9, Pallas kernels: 14 us -> 12.7 us  [the longest x1 2.81 us: body(): pl.pallas_call(near_kernel, out_shape=(pltpu.VMEM(w_in.shape, BF16),) + (...]
    ppermute x2 -> x3, waiting for transfers between devices: 1.54 us -> 0.58 us  [swap(): return lax.ppermute(array, 'pair', [(i, PAIR - 1 - i) for i in range(PAIR)])]
  transfers between devices with their start and end apart: 3 -> 4, of which waited for: 2 -> 2; matrix products, arithmetic and copies ran while one was open for 0% -> 0% of each run, Pallas kernels for 17% -> 23%
where the time goes in v3:
time: 54.7 us; the launch traced here: 54.4 us
  blocking collectives  20.7 us (38%)
  Pallas kernels  19.2 us (35%)
  starting transfers between devices  6.98 us (13%)
  waiting for transfers between devices  6.73 us (12%)
  between operations  0.74 us (1%)
    all_to_all x1, blocking collectives, exchange(): lax.all_to_all(array, ('row', 'pair', 'exp'), split_axis=0, concat_axis=0...  20.7 us
    all_to_all x1, starting transfers between devices, exchange(): lax.all_to_all(array, ('row', 'pair', 'exp'), split_axis=0, concat_axis=0...  6.32 us
    all_to_all x1, waiting for transfers between devices, exchange(): lax.all_to_all(array, ('row', 'pair', 'exp'), split_axis=0, concat_axis=0...  6.15 us
    pallas_call x1, Pallas kernels, body(): pl.pallas_call(weight_kernel, grid=(CHUNKS,), out_shape=(jax.ShapeDtypeSt...  5.88 us
    pallas_call x1, Pallas kernels, body(): pl.pallas_call(near_kernel, out_shape=(pltpu.VMEM(w_in.shape, BF16),) + (...  2.81 us
    pallas_call x1, Pallas kernels, body(): pl.pallas_call(forward_kernel, out_shape=(wide, tall, slope, slope, pltpu...  1.96 us
    pallas_call x1, Pallas kernels, body(): pl.pallas_call(functools.partial(gather_kernel, owners), out_shape=pltpu....  1.78 us
    pallas_call x1, Pallas kernels, body(): pl.pallas_call(back_kernel, out_shape=halves, in_specs=[vmem()] * 3, out_...  1.27 us
  transfers between devices with their start and end apart: 4, of which 2 were waited for; matrix products, arithmetic and copies ran while one was open for 0% of the time, Pallas kernels for 23%

profile of v3, /device:TPU:0, one launch (start us, length us, event | category | flops | bytes accessed | tf_op | source)
XLA Modules:
  0.0 54.4 jit_solution(5228709479594363964)
XLA Ops:
  0.6 1.8 %gather_rows.1 = bf16[16,32,512]{2,1,0:T(8,128)(2,1)S(1)} custom-call(s32[8,64]{1,0:T(8,128)} %bitcast.6, bf16[8,64]{1,0:T(8,128)(2,1)} %bitcast.8, bf16[64,4096]{1,0:T(8,128)(2,1)} %tok_hbm.1, bf16[64,4096]{1,0:T(8,128)(2,1)} %cot_hbm.1), custom_call_target="tpu_custom_call" | custom-call | tf_op jit(solution)/shard_map/gather_rows/pallas_call | solution.py:291
  2.4 20.7 %all_to_all.10.near_ref = bf16[16,32,512]{2,1,0:T(8,128)(2,1)S(1)} all-to-all(bf16[16,32,512]{2,1,0:T(8,128)(2,1)S(1)} %gather_rows.1), channel_id=1, replica_groups={{20,4,5,0,17,3,1,18,7,22,2,19,6,23,21,16},{28,12,13,8,25,11,9,26,15,30,..., dimensions={0} | all-to-all | bytes 1048576 | tf_op jit(solution)/shard_map/all_to_all | solution.py:283
  23.1 0.0 collective-permute-start
  23.1 2.8 %near_rows.1 = (bf16[2,384,4096]{2,1,0:T(8,128)(2,1)S(1)}, bf16[32,4096]{1,0:T(8,128)(2,1)S(1)}, bf16[32,4096]{1,0:T(8,128)(2,1)S(1)}, bf16[256,256]{1,0:T(8,128)(2,1)S(1)}, bf16[256,256]{1,0:T(8,128)(2,1)S(1)}) custom-call(bf16[16,32,512]{2,1,0:T(8,128)(2,1)S(1)} %all_to_all.10.near_ref, bf16[2,384,4096]{2,1,0:T(8,128)(2,1)} %bitcast.10), custom_call_target="tpu_custom_call" | custom-call | bytes 12582912 | tf_op jit(solution)/shard_map/near_rows/pallas_call | solution.py:309
  25.9 0.0 collective-permute-done.far_ref
  26.0 2.0 %gate_up.1 = (bf16[64,4096]{1,0:T(8,128)(2,1)S(1)}, bf16[384,64]{1,0:T(8,128)(2,1)S(1)}, f32[384,64]{1,0:T(8,128)S(1)}, f32[384,64]{1,0:T(8,128)S(1)}, bf16[384,4096]{1,0:T(8,128)(2,1)S(1)}) custom-call(bf16[16,32,512]{2,1,0:T(8,128)(2,1)S(1)} %collective-permute-done.far_ref, bf16[32,4096]{1,0:T(8,128)(2,1)S(1)} %get-tuple-element.30.x_near, ...), custom_call_target="tpu_custom_call" | custom-call | tf_op jit(solution)/shard_map/gate_up/pallas_call | solution.py:324
  27.9 0.7 %down.1 = (f32[32,4096]{1,0:T(8,128)S(1)}, bf16[32,4096]{1,0:T(8,128)(2,1)S(1)}) custom-call(bf16[384,64]{1,0:T(8,128)(2,1)S(1)} %get-tuple-element.39.hid_ref, bf16[384,4096]{1,0:T(8,128)(2,1)S(1)} %get-tuple-element.32.w_down_ref), custom_call_target="tpu_custom_call" | custom-call | tf_op jit(solution)/shard_map/down/pallas_call | solution.py:335
  28.6 0.6 %collective-permute-start.2 = (bf16[32,4096]{1,0:T(8,128)(2,1)S(1)}, bf16[32,4096]{1,0:T(8,128)(2,1)S(1)}, u32[]{:S(2)}, u32[]{:S(2)}) collective-permute-start(bf16[32,4096]{1,0:T(8,128)(2,1)S(1)} %get-tuple-element.41), channel_id=1, source_target_pairs={{0,8},{8,0},{1,9},{9,1},{2,10},{10,2},{3,11},{11,3},{4,12},{12,4},... | collective-permute-start | bytes 786440 | tf_op jit(solution)/shard_map/ppermute | solution.py:289
  29.2 1.1 %hidden_grad.1 = (bf16[64,4096]{1,0:T(8,128)(2,1)S(1)}, bf16[384,64]{1,0:T(8,128)(2,1)S(1)}, bf16[384,64]{1,0:T(8,128)(2,1)S(1)}) custom-call(bf16[16,32,512]{2,1,0:T(8,128)(2,1)S(1)} %collective-permute-done.far_ref, bf16[32,4096]{1,0:T(8,128)(2,1)S(1)} %get-tuple-element.28.c_near, bf16[256,256]{1,0:T(8,128)(2,1)S(1)} %get-tuple-element.29.unfold_ref, ...), custom_call_target="tpu_custom_call" | custom-call | flops 201326592 | bytes 3145728 | tf_op jit(solution)/shard_map/hidden_grad/pallas_call | solution.py:344
  30.3 0.0 copy-start
  30.3 0.0 copy-start.1
  30.4 1.3 %input_grad.1 = (f32[32,4096]{1,0:T(8,128)S(1)}, bf16[32,4096]{1,0:T(8,128)(2,1)S(1)}) custom-call(bf16[384,64]{1,0:T(8,128)(2,1)S(1)} %get-tuple-element.35.gg_ref.after_ref, bf16[384,64]{1,0:T(8,128)(2,1)S(1)} %get-tuple-element.36.ug_ref, bf16[2,384,4096]{2,1,0:T(8,128)(2,1)S(1)} %get-tuple-element.31.w_in_ref), custom_call_target="tpu_custom_call" | custom-call | flops 402653184 | bytes 6291456 | tf_op jit(solution)/shard_map/input_grad/pallas_call | solution.py:353
  31.6 0.1 collective-permute-start.1
  31.7 0.0 collective-permute-done.2.other_ref
  31.7 0.9 %merge_out.1.first_hbm = bf16[16,32,512]{2,1,0:T(8,128)(2,1)} custom-call(bf16[256,256]{1,0:T(8,128)(2,1)S(1)} %get-tuple-element.27.fold_ref, f32[32,4096]{1,0:T(8,128)S(1)} %get-tuple-element.40.keep_ref, bf16[32,4096]{1,0:T(8,128)(2,1)S(1)} %collective-permute-done.2.other_ref), custom_call_target="tpu_custom_call" | custom-call | bytes 1048576 | tf_op jit(solution)/shard_map/merge_out/pallas_call | solution.py:365
  32.7 0.6 %collective-permute-done.1.other_ref = bf16[32,4096]{1,0:T(8,128)(2,1)S(1)} collective-permute-done((bf16[32,4096]{1,0:T(8,128)(2,1)S(1)}, bf16[32,4096]{1,0:T(8,128)(2,1)S(1)}, u32[]{:S(2)}, u32[]{:S(2)}) %collective-permute-start.1) | collective-permute-done | bytes 262176 | tf_op jit(solution)/shard_map/ppermute | solution.py:289
  33.2 0.9 %merge_grad.1 = bf16[16,32,512]{2,1,0:T(8,128)(2,1)} custom-call(bf16[256,256]{1,0:T(8,128)(2,1)S(1)} %get-tuple-element.27.fold_ref, f32[32,4096]{1,0:T(8,128)S(1)} %get-tuple-element.37.keep_ref, bf16[32,4096]{1,0:T(8,128)(2,1)S(1)} %collective-permute-done.1.other_ref, bf16[16,32,512]{2,1,0:T(8,128)(2,1)} %merge_out.1.first_hbm), custom_call_target="tpu_custom_call", output_to_operand_aliasing={{}: (3, {})} | custom-call | tf_op jit(solution)/shard_map/merge_grad/pallas_call | solution.py:375
  34.2 6.3 %all-to-all-start.1 = ((bf16[16,32,512]{2,1,0:T(8,128)(2,1)}), bf16[16,32,512]{2,1,0:T(8,128)(2,1)S(1)}, u32[]{:S(2)}, u32[]{:S(2)}) async-start(bf16[16,32,512]{2,1,0:T(8,128)(2,1)} %merge_grad.1), calls=%async_computation.1 | async-start | bytes 1048576 | tf_op jit(solution)/shard_map/all_to_all | solution.py:283
  40.5 0.0 copy-done
  40.5 0.0 copy-done.1
  40.5 0.6 %slot_tables.1 = (bf16[512,128]{1,0:T(8,128)(2,1)S(1)}, bf16[512,128]{1,0:T(8,128)(2,1)S(1)}) custom-call(s32[8,64]{1,0:T(8,128)S(1)} %bitcast.7, bf16[8,64]{1,0:T(8,128)(2,1)S(1)} %bitcast.9, bf16[384,64]{1,0:T(8,128)(2,1)S(1)} %get-tuple-element.35.gg_ref.after_ref), custom_call_target="tpu_custom_call" | custom-call | tf_op jit(solution)/shard_map/slot_tables/pallas_call | solution.py:404
  41.1 5.9 %weight_grads.1 = (bf16[2,384,4096]{2,1,0:T(8,128)(2,1)}, bf16[384,4096]{1,0:T(8,128)(2,1)}) custom-call(bf16[64,4096]{1,0:T(8,128)(2,1)S(1)} %get-tuple-element.46.x_ref, bf16[64,4096]{1,0:T(8,128)(2,1)S(1)} %get-tuple-element.47.c_ref, bf16[384,64]{1,0:T(8,128)(2,1)S(1)} %get-tuple-element.39.hid_ref, ...), custom_call_target="tpu_custom_call" | custom-call | flops 603979776 | bytes 10485760 | tf_op jit(solution)/shard_map/weight_grads/pallas_call | solution.py:386
  47.0 6.2 %all-to-all-done.1.back_ref = bf16[16,32,512]{2,1,0:T(8,128)(2,1)S(1)} async-done(((bf16[16,32,512]{2,1,0:T(8,128)(2,1)}), bf16[16,32,512]{2,1,0:T(8,128)(2,1)S(1)}, u32[]{:S(2)}, u32[]{:S(2)}) %all-to-all-start.1) | async-done | bytes 524320 | tf_op jit(solution)/shard_map/all_to_all | solution.py:283
  53.2 1.2 %combine_rows.1 = (bf16[64,4096]{1,0:T(8,128)(2,1)}, bf16[64,4096]{1,0:T(8,128)(2,1)}) custom-call(bf16[16,32,512]{2,1,0:T(8,128)(2,1)S(1)} %all-to-all-done.1.back_ref, bf16[512,128]{1,0:T(8,128)(2,1)S(1)} %get-tuple-element.42.pick_ref, bf16[512,128]{1,0:T(8,128)(2,1)S(1)} %get-tuple-element.43.weigh_ref), custom_call_target="tpu_custom_call" | custom-call | tf_op jit(solution)/shard_map/combine_rows/pallas_call | solution.py:412
Async XLA Ops:
  23.1 2.8 %collective-permute-start = (bf16[16,32,512]{2,1,0:T(8,128)(2,1)S(1)}, bf16[16,32,512]{2,1,0:T(8,128)(2,1)S(1)}, u32[]{:S(2)}, u32[]{:S(2)}) collective-permute-start(bf16[16,32,512]{2,1,0:T(8,128)(2,1)S(1)} %all_to_all.10.near_ref), channel_id=1, source_target_pairs={{0,8},{8,0},{1,9},{9,1},{2,10},{10,2},{3,11},{11,3},{4,12},{12,4},... | collective-permute-start | bytes 1572872 | tf_op jit(solution)/shard_map/ppermute | solution.py:289
  28.6 3.1 %collective-permute-start.2 = (bf16[32,4096]{1,0:T(8,128)(2,1)S(1)}, bf16[32,4096]{1,0:T(8,128)(2,1)S(1)}, u32[]{:S(2)}, u32[]{:S(2)}) collective-permute-start(bf16[32,4096]{1,0:T(8,128)(2,1)S(1)} %get-tuple-element.41), channel_id=1, source_target_pairs={{0,8},{8,0},{1,9},{9,1},{2,10},{10,2},{3,11},{11,3},{4,12},{12,4},... | collective-permute-start | bytes 786440 | tf_op jit(solution)/shard_map/ppermute | solution.py:289
  30.3 10.2 %copy-start = (s32[64,8]{0,1:T(8,128)S(1)}, s32[64,8]{0,1:T(8,128)}, u32[]{:S(2)}) copy-start(s32[64,8]{0,1:T(8,128)} %param.8) | copy-start | bytes 6148
  30.3 10.1 %copy-start.1 = (bf16[64,8]{0,1:T(8,128)(2,1)S(1)}, bf16[64,8]{0,1:T(8,128)(2,1)}, u32[]{:S(2)}) copy-start(bf16[64,8]{0,1:T(8,128)(2,1)} %param.9) | copy-start | bytes 3076
  31.6 1.6 %collective-permute-start.1 = (bf16[32,4096]{1,0:T(8,128)(2,1)S(1)}, bf16[32,4096]{1,0:T(8,128)(2,1)S(1)}, u32[]{:S(2)}, u32[]{:S(2)}) collective-permute-start(bf16[32,4096]{1,0:T(8,128)(2,1)S(1)} %get-tuple-element.38), channel_id=1, source_target_pairs={{0,8},{8,0},{1,9},{9,1},{2,10},{10,2},{3,11},{11,3},{4,12},{12,4},... | collective-permute-start | bytes 786440 | tf_op jit(solution)/shard_map/ppermute | solution.py:289
  34.2 19.0 %all-to-all-start.1 = ((bf16[16,32,512]{2,1,0:T(8,128)(2,1)}), bf16[16,32,512]{2,1,0:T(8,128)(2,1)S(1)}, u32[]{:S(2)}, u32[]{:S(2)}) async-start(bf16[16,32,512]{2,1,0:T(8,128)(2,1)} %merge_grad.1), calls=%async_computation.1 | async-start | bytes 1048576 | tf_op jit(solution)/shard_map/all_to_all | solution.py:283

commit v4 on v3

--- a/solution.py
+++ b/solution.py
@@ -80,14 +80,21 @@
     return jnp.where(chunk, dot(small, repeat), 0.0).astype(BF16)
 
 
+def folded(ref, low, width):
+    return jnp.concatenate(
+        [ref[:, low + c * width : low + (c + 1) * width] for c in range(CHUNKS)], axis=0
+    )
+
+
 def gather_kernel(
-    owners, ids_hbm, gates_hbm, tok_hbm, cot_hbm,
+    order, experts, ids_hbm, gates_hbm, tok_hbm, cot_hbm,
     send_ref,
     ids_ref, gates_ref, tok_ref, cot_ref, sems,
 ):
     rows, depth = tok_ref.shape
     width = depth // CHUNKS
-    experts = max(owners) + 1
+    groups = len(order) // experts
+    narrow = width // groups
     pairs = ((ids_hbm, ids_ref), (gates_hbm, gates_ref), (tok_hbm, tok_ref), (cot_hbm, cot_ref))
     copies = [pltpu.make_async_copy(a, b, sems.at[i]) for i, (a, b) in enumerate(pairs)]
     for copy in copies:
@@ -96,15 +103,18 @@
     copies[0].wait()
     copies[1].wait()
     tables = slot_tables(ids_ref[...], gates_ref[...], experts)
-    wide = [widen(table, masks) for table in tables]
-    for part, source in enumerate((tok_ref, cot_ref)):
-        copies[2 + part].wait()
-        folded = jnp.concatenate(
-            [source[:, c * width : (c + 1) * width] for c in range(CHUNKS)], axis=0
-        )
-        moved = dot(wide[part], folded).astype(BF16).reshape(experts, TILE, width)
-        for place, owner in enumerate(owners):
-            send_ref[place, part * TILE : (part + 1) * TILE, :] = moved[owner]
+    picks, weights = [widen(table, masks) for table in tables]
+    shape = (experts, TILE, -1)
+    copies[2].wait()
+    moved = dot(picks, folded(tok_ref, 0, width)).astype(BF16).reshape(shape)
+    for place, r in enumerate(order):
+        send_ref[place, :, 0:width] = moved[r % experts]
+    copies[3].wait()
+    for g in range(groups):
+        moved = dot(weights, folded(cot_ref, g * depth // groups, narrow)).astype(BF16).reshape(shape)
+        for place, r in enumerate(order):
+            if r // experts == g:
+                send_ref[place, :, width : width + narrow] = moved[r % experts]
 
 
 def table_kernel(ids_ref, gates_ref, after_ref, pick_ref, weigh_ref):
@@ -117,11 +127,10 @@
     weigh_ref[...] = widen(weights, masks).T
 
 
-def unfold(ref, part, perm, out):
-    sources, _, width = ref.shape
+def unfold(messages, perm, out):
+    sources, _, width = messages.shape
     half = sources * CAP
-    flat = ref[:, part * TILE : (part + 1) * TILE, :].reshape(sources * TILE, width)
-    flat = dot(perm, flat).astype(BF16)
+    flat = dot(perm, messages.reshape(sources * TILE, width)).astype(BF16)
     for c in range(CHUNKS):
         out[:, c * width : (c + 1) * width] = flat[c * half : (c + 1) * half]
 
@@ -130,6 +139,7 @@
     fetch = pltpu.make_async_copy(w_in_hbm, w_in_ref, sem)
     fetch.start()
     sources = near_ref.shape[0]
+    width = x_ref.shape[1] // CHUNKS
     half, lines = sources * CAP, sources * TILE
     row, col = iota((lines, lines), 0), iota((lines, lines), 1)
     perm = (row % half // CAP) * TILE + (row // half) * CAP + row % CAP == col
@@ -137,8 +147,8 @@
     unfold_ref[...] = perm
     back = (row // CAP % CHUNKS) * half + (row // TILE) * CAP + row % CAP == col
     fold_ref[...] = jnp.where(back, 1.0, 0.0).astype(BF16)
-    unfold(near_ref, 0, perm, x_ref)
-    unfold(near_ref, 1, perm, c_ref)
+    unfold(near_ref[:, :, 0:width], perm, x_ref)
+    unfold(near_ref[:, :, width:], perm, c_ref)
     fetch.wait()
 
 
@@ -151,7 +161,8 @@
     hidden = w_down_ref.shape[0]
     half = far_ref.shape[0] * CAP
     x_ref[0:half, :] = x_near[...]
-    unfold(far_ref, 0, unfold_ref[...], x_ref.at[half : 2 * half])
+    width = x_ref.shape[1] // CHUNKS
+    unfold(far_ref[:, :, 0:width], unfold_ref[...], x_ref.at[half : 2 * half])
     both = dot(w_in_ref[...].reshape(2 * hidden, -1), x_ref[...], ((1,), (1,)))
     gate, up = both[:hidden], both[hidden:]
     sig = jax.nn.sigmoid(gate)
@@ -176,12 +187,28 @@
         split_rows(dot(rows, w_down_ref[:, cols]), cols, keep_ref, away_ref)
 
 
-def hidden_kernel(
-    far_ref, c_near, unfold_ref, w_down_ref, gate_slope_ref, up_slope_ref, c_ref, gg_ref, ug_ref
-):
-    half = far_ref.shape[0] * CAP
-    c_ref[0:half, :] = c_near[...]
-    unfold(far_ref, 1, unfold_ref[...], c_ref.at[half : 2 * half])
+def hidden_kernel(groups, *refs):
+    others, refs = refs[: 2 * (groups - 1)], refs[2 * (groups - 1) :]
+    far_ref, c_near, unfold_ref, w_down_ref, gate_slope_ref, up_slope_ref, c_ref, gg_ref, ug_ref = refs
+    half, share = c_near.shape
+    width = c_ref.shape[1] // CHUNKS
+    narrow = share // CHUNKS
+    near_rows, far_rows = c_ref.at[0:half], c_ref.at[half : 2 * half]
+    plane = lax.axis_index("row")
+    bases = [pl.multiple_of(lax.rem(plane + k, groups) * share, share) for k in range(groups)]
+    near_rows[:, pl.ds(bases[0], share)] = c_near[...]
+    homes = [(far_rows, bases[0])]
+    for base in bases[1:]:
+        homes += [(near_rows, base), (far_rows, base)]
+    lines = unfold_ref.shape[0]
+    messages = [far_ref[:, :, width:]] + [other[...] for other in others]
+    flat = jnp.concatenate([m.reshape(lines, narrow) for m in messages], axis=1)
+    flat = dot(unfold_ref[...], flat).astype(BF16)
+    for i, (rows, base) in enumerate(homes):
+        for c in range(CHUNKS):
+            rows[:, pl.ds(base + c * narrow, narrow)] = flat[
+                c * half : (c + 1) * half, i * narrow : (i + 1) * narrow
+            ]
     grad = dot(w_down_ref[...], c_ref[...], ((1,), (1,)))
     gg_ref[...] = (grad * gate_slope_ref[...]).astype(BF16)
     ug_ref[...] = (grad * up_slope_ref[...]).astype(BF16)
@@ -273,7 +300,6 @@
     w_in, w_down = in_hbm(w_in[0]), in_hbm(w_down[0])
     ids, gates = expert_ids.T, gate_weights.T
     order = [int(r) for r in np.random.RandomState(ORDER_SEED).permutation(sources)]
-    owners = tuple(r % experts for r in order)
     places = tuple(
         tuple(order.index(g * experts + e) for g in range(groups)) for e in range(experts)
     )
@@ -289,8 +315,8 @@
         return lax.ppermute(array, "pair", [(i, PAIR - 1 - i) for i in range(PAIR)])
 
     send = pl.pallas_call(
-        functools.partial(gather_kernel, owners),
-        out_shape=pltpu.VMEM((sources, 2 * TILE, width), BF16),
+        functools.partial(gather_kernel, order, experts),
+        out_shape=pltpu.VMEM((sources, TILE, width + width // groups), BF16),
         in_specs=[hbm()] * 4,
         out_specs=vmem(),
         scratch_shapes=[
@@ -305,11 +331,16 @@
     )(in_hbm(ids), in_hbm(gates), in_hbm(tokens), in_hbm(cotangent))
     near = exchange(send)
     far = swap(near)
+    share = near[:, :, width:]
+    turned = [
+        lax.ppermute(share, "row", [((i + k) % groups, i) for i in range(groups)])
+        for k in range(1, groups)
+    ]
     square = pltpu.VMEM((sources * TILE, sources * TILE), BF16)
     w_in, x_near, c_near, unfolding, folding = pl.pallas_call(
         near_kernel,
         out_shape=(pltpu.VMEM(w_in.shape, BF16),)
-        + (pltpu.VMEM((half, depth), BF16),) * 2
+        + (pltpu.VMEM((half, depth), BF16), pltpu.VMEM((half, depth // groups), BF16))
         + (square,) * 2,
         in_specs=[vmem(), hbm()],
         out_specs=[vmem()] * 5,
@@ -330,6 +361,8 @@
         compiler_params=params(),
         name="gate_up",
     )(far, x_near, unfolding, w_in, w_down)
+    hid, turned = lax.optimization_barrier((hid, turned))
+    others = [other for array in turned for other in (array, swap(array))]
     halves = (pltpu.VMEM((half, depth), F32), pltpu.VMEM((half, depth), BF16))
     passes = 4 * hidden * depth * half
     keep_out, away_out = pl.pallas_call(
@@ -342,14 +375,14 @@
     )(hid, w_down)
     other_out = swap(away_out)
     c, gg, ug = pl.pallas_call(
-        hidden_kernel,
+        functools.partial(hidden_kernel, groups),
         out_shape=(wide, tall, tall),
-        in_specs=[vmem()] * 6,
+        in_specs=[vmem()] * (6 + len(others)),
         out_specs=[vmem()] * 3,
         compiler_params=params(),
         cost_estimate=cost(passes, 2 * w_down.size),
         name="hidden_grad",
-    )(far, c_near, unfolding, w_down, gate_slope, up_slope)
+    )(*others, far, c_near, unfolding, w_down, gate_slope, up_slope)
     keep_grad, away_grad = pl.pallas_call(
         back_kernel,
         out_shape=halves,

time: 54.7 us -> 53.5 us (0.978)
  blocking collectives: 20.7 us -> 18 us
  starting transfers between devices: 6.98 us -> 8.4 us
    all_to_all x1, blocking collectives: 20.7 us -> 18 us  [exchange(): lax.all_to_all(array, ('row', 'pair', 'exp'), split_axis=0, concat_axis=0...]
    ppermute x0 -> x1, starting transfers between devices: none -> 2.05 us  [body(): lax.ppermute(share, 'row', [((i + k) % groups, i) for i in range(groups)])]
    all_to_all x1, starting transfers between devices: 6.32 us -> 5.41 us  [exchange(): lax.all_to_all(array, ('row', 'pair', 'exp'), split_axis=0, concat_axis=0...]
  transfers between devices with their start and end apart: 4 -> 6, of which waited for: 2 -> 3; matrix products, arithmetic and copies ran while one was open for 0% -> 0% of each run, Pallas kernels for 23% -> 29%
where the time goes in v4:
time: 53.5 us; the launch traced here: 53.2 us
  Pallas kernels  19.5 us (36%)
  blocking collectives  18 us (34%)
  starting transfers between devices  8.4 us (16%)
  waiting for transfers between devices  6.54 us (12%)
  between operations  0.75 us (1%)
    all_to_all x1, blocking collectives, exchange(): lax.all_to_all(array, ('row', 'pair', 'exp'), split_axis=0, concat_axis=0...  18 us
    all_to_all x1, waiting for transfers between devices, exchange(): lax.all_to_all(array, ('row', 'pair', 'exp'), split_axis=0, concat_axis=0...  6.11 us
    pallas_call x1, Pallas kernels, body(): pl.pallas_call(weight_kernel, grid=(CHUNKS,), out_shape=(jax.ShapeDtypeSt...  5.88 us
    all_to_all x1, starting transfers between devices, exchange(): lax.all_to_all(array, ('row', 'pair', 'exp'), split_axis=0, concat_axis=0...  5.41 us
    pallas_call x1, Pallas kernels, body(): pl.pallas_call(near_kernel, out_shape=(pltpu.VMEM(w_in.shape, BF16),) + (...  2.8 us
    ppermute x1, starting transfers between devices, body(): lax.ppermute(share, 'row', [((i + k) % groups, i) for i in range(groups)])  2.05 us
    pallas_call x1, Pallas kernels, body(): pl.pallas_call(forward_kernel, out_shape=(wide, tall, slope, slope, pltpu...  1.95 us
    pallas_call x1, Pallas kernels, body(): pl.pallas_call(functools.partial(gather_kernel, order, experts), out_shap...  1.78 us
  transfers between devices with their start and end apart: 6, of which 3 were waited for; matrix products, arithmetic and copies ran while one was open for 0% of the time, Pallas kernels for 29%

profile of v4, /device:TPU:0, one launch (start us, length us, event | category | flops | bytes accessed | tf_op | source)
XLA Modules:
  0.0 53.2 jit_solution(13641843477699197187)
XLA Ops:
  0.6 1.8 %gather_rows.1 = bf16[16,16,768]{2,1,0:T(8,128)(2,1)S(1)} custom-call(s32[8,64]{1,0:T(8,128)} %bitcast.6, bf16[8,64]{1,0:T(8,128)(2,1)} %bitcast.8, bf16[64,4096]{1,0:T(8,128)(2,1)} %tok_hbm.1, bf16[64,4096]{1,0:T(8,128)(2,1)} %cot_hbm.1), custom_call_target="tpu_custom_call" | custom-call | tf_op jit(solution)/shard_map/gather_rows/pallas_call | solution.py:317
  2.4 18.0 %all_to_all.10.near_ref = bf16[16,16,768]{2,1,0:T(8,128)(2,1)S(1)} all-to-all(bf16[16,16,768]{2,1,0:T(8,128)(2,1)S(1)} %gather_rows.1), channel_id=1, replica_groups={{20,4,5,0,17,3,1,18,7,22,2,19,6,23,21,16},{28,12,13,8,25,11,9,26,15,30,..., dimensions={0} | all-to-all | bytes 786432 | tf_op jit(solution)/shard_map/all_to_all | solution.py:309
  20.4 0.0 collective-permute-start
  20.4 2.0 %collective-permute-start.1 = (bf16[16,16,256]{2,1,0:T(8,128)(2,1)S(1)}, bf16[16,16,256]{2,1,0:T(8,128)(2,1)S(1)}, u32[]{:S(2)}, u32[]{:S(2)}) collective-permute-start(bf16[16,16,256]{2,1,0:T(8,128)(2,1)S(1)} %slice.4), channel_id=1, source_target_pairs={{16,0},{0,16},{17,1},{1,17},{18,2},{2,18},{19,3},{3,19},{20,4},{4,... | collective-permute-start | bytes 393224 | tf_op jit(solution)/shard_map/ppermute | solution.py:336
  22.5 2.8 %near_rows.1 = (bf16[2,384,4096]{2,1,0:T(8,128)(2,1)S(1)}, bf16[32,4096]{1,0:T(8,128)(2,1)S(1)}, bf16[32,2048]{1,0:T(8,128)(2,1)S(1)}, bf16[256,256]{1,0:T(8,128)(2,1)S(1)}, bf16[256,256]{1,0:T(8,128)(2,1)S(1)}) custom-call(bf16[16,16,768]{2,1,0:T(8,128)(2,1)S(1)} %all_to_all.10.near_ref, bf16[2,384,4096]{2,1,0:T(8,128)(2,1)} %bitcast.10), custom_call_target="tpu_custom_call" | custom-call | bytes 12582912 | tf_op jit(solution)/shard_map/near_rows/pallas_call | solution.py:340
  25.3 0.0 collective-permute-done.far_ref.refs_2_
  25.3 2.0 %gate_up.1 = (bf16[64,4096]{1,0:T(8,128)(2,1)S(1)}, bf16[384,64]{1,0:T(8,128)(2,1)S(1)}, f32[384,64]{1,0:T(8,128)S(1)}, f32[384,64]{1,0:T(8,128)S(1)}, bf16[384,4096]{1,0:T(8,128)(2,1)S(1)}) custom-call(bf16[16,16,768]{2,1,0:T(8,128)(2,1)S(1)} %collective-permute-done.far_ref.refs_2_, bf16[32,4096]{1,0:T(8,128)(2,1)S(1)} %get-tuple-element.30.x_near, ...), custom_call_target="tpu_custom_call" | custom-call | tf_op jit(solution)/shard_map/gate_up/pallas_call | solution.py:355
  27.3 0.0 collective-permute-done.1.refs_0_
  27.3 0.3 collective-permute-start.2
  27.6 0.7 %down.1 = (f32[32,4096]{1,0:T(8,128)S(1)}, bf16[32,4096]{1,0:T(8,128)(2,1)S(1)}) custom-call(bf16[384,64]{1,0:T(8,128)(2,1)S(1)} %get-tuple-element.43.hid_ref, bf16[384,4096]{1,0:T(8,128)(2,1)S(1)} %get-tuple-element.36.refs_5_.w_down_ref), custom_call_target="tpu_custom_call" | custom-call | tf_op jit(solution)/shard_map/down/pallas_call | solution.py:368
  28.3 0.3 collective-permute-start.4
  28.6 0.1 collective-permute-done.2.refs_1_
  28.7 1.4 %hidden_grad.1 = (bf16[64,4096]{1,0:T(8,128)(2,1)S(1)}, bf16[384,64]{1,0:T(8,128)(2,1)S(1)}, bf16[384,64]{1,0:T(8,128)(2,1)S(1)}) custom-call(bf16[16,16,256]{2,1,0:T(8,128)(2,1)S(1)} %collective-permute-done.1.refs_0_, bf16[16,16,256]{2,1,0:T(8,128)(2,1)S(1)} %collective-permute-done.2.refs_1_, ...), custom_call_target="tpu_custom_call" | custom-call | flops 201326592 | bytes 3145728 | tf_op jit(solution)/shard_map/hidden_grad/pallas_call | solution.py:377
  30.1 0.0 copy-start
  30.1 0.0 copy-start.1
  30.1 1.3 %input_grad.1 = (f32[32,4096]{1,0:T(8,128)S(1)}, bf16[32,4096]{1,0:T(8,128)(2,1)S(1)}) custom-call(bf16[384,64]{1,0:T(8,128)(2,1)S(1)} %get-tuple-element.39.gg_ref.after_ref, bf16[384,64]{1,0:T(8,128)(2,1)S(1)} %get-tuple-element.40.ug_ref, bf16[2,384,4096]{2,1,0:T(8,128)(2,1)S(1)} %get-tuple-element.32.w_in_ref), custom_call_target="tpu_custom_call" | custom-call | flops 402653184 | bytes 6291456 | tf_op jit(solution)/shard_map/input_grad/pallas_call | solution.py:386
  31.4 0.3 collective-permute-start.3
  31.7 0.0 collective-permute-done.4.other_ref
  31.7 0.9 %merge_out.1.first_hbm = bf16[16,32,512]{2,1,0:T(8,128)(2,1)} custom-call(bf16[256,256]{1,0:T(8,128)(2,1)S(1)} %get-tuple-element.29.fold_ref, f32[32,4096]{1,0:T(8,128)S(1)} %get-tuple-element.44.keep_ref, bf16[32,4096]{1,0:T(8,128)(2,1)S(1)} %collective-permute-done.4.other_ref), custom_call_target="tpu_custom_call" | custom-call | bytes 1048576 | tf_op jit(solution)/shard_map/merge_out/pallas_call | solution.py:398
  32.6 0.4 collective-permute-done.3.other_ref
  33.0 0.9 %merge_grad.1 = bf16[16,32,512]{2,1,0:T(8,128)(2,1)} custom-call(bf16[256,256]{1,0:T(8,128)(2,1)S(1)} %get-tuple-element.29.fold_ref, f32[32,4096]{1,0:T(8,128)S(1)} %get-tuple-element.41.keep_ref, bf16[32,4096]{1,0:T(8,128)(2,1)S(1)} %collective-permute-done.3.other_ref, bf16[16,32,512]{2,1,0:T(8,128)(2,1)} %merge_out.1.first_hbm), custom_call_target="tpu_custom_call", output_to_operand_aliasing={{}: (3, {})} | custom-call | tf_op jit(solution)/shard_map/merge_grad/pallas_call | solution.py:408
  33.9 5.4 %all-to-all-start.1 = ((bf16[16,32,512]{2,1,0:T(8,128)(2,1)}), bf16[16,32,512]{2,1,0:T(8,128)(2,1)S(1)}, u32[]{:S(2)}, u32[]{:S(2)}) async-start(bf16[16,32,512]{2,1,0:T(8,128)(2,1)} %merge_grad.1), calls=%async_computation.1 | async-start | bytes 1048576 | tf_op jit(solution)/shard_map/all_to_all | solution.py:309
  39.3 0.0 copy-done
  39.3 0.0 copy-done.1
  39.4 0.6 %slot_tables.1 = (bf16[512,128]{1,0:T(8,128)(2,1)S(1)}, bf16[512,128]{1,0:T(8,128)(2,1)S(1)}) custom-call(s32[8,64]{1,0:T(8,128)S(1)} %bitcast.7, bf16[8,64]{1,0:T(8,128)(2,1)S(1)} %bitcast.9, bf16[384,64]{1,0:T(8,128)(2,1)S(1)} %get-tuple-element.39.gg_ref.after_ref), custom_call_target="tpu_custom_call" | custom-call | tf_op jit(solution)/shard_map/slot_tables/pallas_call | solution.py:437
  40.0 5.9 %weight_grads.1 = (bf16[2,384,4096]{2,1,0:T(8,128)(2,1)}, bf16[384,4096]{1,0:T(8,128)(2,1)}) custom-call(bf16[64,4096]{1,0:T(8,128)(2,1)S(1)} %get-tuple-element.50.x_ref, bf16[64,4096]{1,0:T(8,128)(2,1)S(1)} %get-tuple-element.51.c_ref, bf16[384,64]{1,0:T(8,128)(2,1)S(1)} %get-tuple-element.43.hid_ref, ...), custom_call_target="tpu_custom_call" | custom-call | flops 603979776 | bytes 10485760 | tf_op jit(solution)/shard_map/weight_grads/pallas_call | solution.py:419
  45.9 6.1 %all-to-all-done.1.back_ref = bf16[16,32,512]{2,1,0:T(8,128)(2,1)S(1)} async-done(((bf16[16,32,512]{2,1,0:T(8,128)(2,1)}), bf16[16,32,512]{2,1,0:T(8,128)(2,1)S(1)}, u32[]{:S(2)}, u32[]{:S(2)}) %all-to-all-start.1) | async-done | bytes 524320 | tf_op jit(solution)/shard_map/all_to_all | solution.py:309
  52.0 1.2 %combine_rows.1 = (bf16[64,4096]{1,0:T(8,128)(2,1)}, bf16[64,4096]{1,0:T(8,128)(2,1)}) custom-call(bf16[16,32,512]{2,1,0:T(8,128)(2,1)S(1)} %all-to-all-done.1.back_ref, bf16[512,128]{1,0:T(8,128)(2,1)S(1)} %get-tuple-element.46.pick_ref, bf16[512,128]{1,0:T(8,128)(2,1)S(1)} %get-tuple-element.47.weigh_ref), custom_call_target="tpu_custom_call" | custom-call | tf_op jit(solution)/shard_map/combine_rows/pallas_call | solution.py:445
  (1 shorter events, 0.0 us)
Async XLA Ops:
  20.4 4.9 %collective-permute-start = (bf16[16,16,768]{2,1,0:T(8,128)(2,1)S(1)}, bf16[16,16,768]{2,1,0:T(8,128)(2,1)S(1)}, u32[]{:S(2)}, u32[]{:S(2)}) collective-permute-start(bf16[16,16,768]{2,1,0:T(8,128)(2,1)S(1)} %all_to_all.10.near_ref), channel_id=1, source_target_pairs={{0,8},{8,0},{1,9},{9,1},{2,10},{10,2},{3,11},{11,3},{4,12},{12,4},... | collective-permute-start | bytes 1179656 | tf_op jit(solution)/shard_map/ppermute | solution.py:315
  20.4 6.8 %collective-permute-start.1 = (bf16[16,16,256]{2,1,0:T(8,128)(2,1)S(1)}, bf16[16,16,256]{2,1,0:T(8,128)(2,1)S(1)}, u32[]{:S(2)}, u32[]{:S(2)}) collective-permute-start(bf16[16,16,256]{2,1,0:T(8,128)(2,1)S(1)} %slice.4), channel_id=1, source_target_pairs={{16,0},{0,16},{17,1},{1,17},{18,2},{2,18},{19,3},{3,19},{20,4},{4,... | collective-permute-start | bytes 393224 | tf_op jit(solution)/shard_map/ppermute | solution.py:336
  27.3 1.4 %collective-permute-start.2 = (bf16[16,16,256]{2,1,0:T(8,128)(2,1)S(1)}, bf16[16,16,256]{2,1,0:T(8,128)(2,1)S(1)}, u32[]{:S(2)}, u32[]{:S(2)}) collective-permute-start(bf16[16,16,256]{2,1,0:T(8,128)(2,1)S(1)} %collective-permute-done.1.refs_0_), channel_id=1, source_target_pairs={{0,8},{8,0},{1,9},{9,1},{2,10},{10,2},{3,11},{11,3},{4,12},{12,4},... | collective-permute-start | bytes 393224 | tf_op jit(solution)/shard_map/ppermute | solution.py:315
  28.3 3.4 %collective-permute-start.4 = (bf16[32,4096]{1,0:T(8,128)(2,1)S(1)}, bf16[32,4096]{1,0:T(8,128)(2,1)S(1)}, u32[]{:S(2)}, u32[]{:S(2)}) collective-permute-start(bf16[32,4096]{1,0:T(8,128)(2,1)S(1)} %get-tuple-element.45), channel_id=1, source_target_pairs={{0,8},{8,0},{1,9},{9,1},{2,10},{10,2},{3,11},{11,3},{4,12},{12,4},... | collective-permute-start | bytes 786440 | tf_op jit(solution)/shard_map/ppermute | solution.py:315
  30.1 9.2 %copy-start = (s32[64,8]{0,1:T(8,128)S(1)}, s32[64,8]{0,1:T(8,128)}, u32[]{:S(2)}) copy-start(s32[64,8]{0,1:T(8,128)} %param.8) | copy-start | bytes 6148
  30.1 9.2 %copy-start.1 = (bf16[64,8]{0,1:T(8,128)(2,1)S(1)}, bf16[64,8]{0,1:T(8,128)(2,1)}, u32[]{:S(2)}) copy-start(bf16[64,8]{0,1:T(8,128)(2,1)} %param.9) | copy-start | bytes 3076
  31.4 1.6 %collective-permute-start.3 = (bf16[32,4096]{1,0:T(8,128)(2,1)S(1)}, bf16[32,4096]{1,0:T(8,128)(2,1)S(1)}, u32[]{:S(2)}, u32[]{:S(2)}) collective-permute-start(bf16[32,4096]{1,0:T(8,128)(2,1)S(1)} %get-tuple-element.42), channel_id=1, source_target_pairs={{0,8},{8,0},{1,9},{9,1},{2,10},{10,2},{3,11},{11,3},{4,12},{12,4},... | collective-permute-start | bytes 786440 | tf_op jit(solution)/shard_map/ppermute | solution.py:315
  33.9 18.1 %all-to-all-start.1 = ((bf16[16,32,512]{2,1,0:T(8,128)(2,1)}), bf16[16,32,512]{2,1,0:T(8,128)(2,1)S(1)}, u32[]{:S(2)}, u32[]{:S(2)}) async-start(bf16[16,32,512]{2,1,0:T(8,128)(2,1)} %merge_grad.1), calls=%async_computation.1 | async-start | bytes 1048576 | tf_op jit(solution)/shard_map/all_to_all | solution.py:309

commit v5 on v4

--- a/solution.py
+++ b/solution.py
@@ -13,7 +13,7 @@
 CHUNKS = TILE // CAP
 PAIR = 2
 STEPS = 2
-ORDER_SEED = 2
+SEEDS = (40, 2)
 F32 = jnp.float32
 BF16 = jnp.bfloat16
 LIMIT = 24 * 1024 * 1024
@@ -135,7 +135,9 @@
         out[:, c * width : (c + 1) * width] = flat[c * half : (c + 1) * half]
 
 
-def near_kernel(near_ref, w_in_hbm, w_in_ref, x_ref, c_ref, unfold_ref, fold_ref, sem):
+def near_kernel(
+    origins, near_ref, far_ref, w_in_hbm, w_in_ref, x_ref, c_ref, unfold_ref, fold_ref, sem
+):
     fetch = pltpu.make_async_copy(w_in_hbm, w_in_ref, sem)
     fetch.start()
     sources = near_ref.shape[0]
@@ -145,24 +147,24 @@
     perm = (row % half // CAP) * TILE + (row // half) * CAP + row % CAP == col
     perm = jnp.where(perm, 1.0, 0.0).astype(BF16)
     unfold_ref[...] = perm
-    back = (row // CAP % CHUNKS) * half + (row // TILE) * CAP + row % CAP == col
-    fold_ref[...] = jnp.where(back, 1.0, 0.0).astype(BF16)
-    unfold(near_ref[:, :, 0:width], perm, x_ref)
-    unfold(near_ref[:, :, width:], perm, c_ref)
+    for side, ref in enumerate((near_ref, far_ref)):
+        rows = slice(side * half, (side + 1) * half)
+        unfold(ref[:, :, 0:width], perm, x_ref.at[rows])
+        unfold(ref[:, :, width:], perm, c_ref.at[rows])
+    row, col = iota((TILE, lines), 0), iota((TILE, lines), 1)
+    place = row // CAP * half + row % CAP
+    for p, s in enumerate(origins):
+        tile = jnp.where(place + s * CAP == col, 1.0, 0.0).astype(BF16)
+        fold_ref[p * TILE : (p + 1) * TILE, :] = tile
     fetch.wait()
 
 
 def forward_kernel(
-    far_ref, x_near, unfold_ref, w_in_ref, w_down_hbm,
-    x_ref, hid_ref, gate_slope_ref, up_slope_ref, w_down_ref, sem,
+    x_ref, w_in_ref, w_down_hbm, hid_ref, gate_slope_ref, up_slope_ref, w_down_ref, sem
 ):
     fetch = pltpu.make_async_copy(w_down_hbm, w_down_ref, sem)
     fetch.start()
     hidden = w_down_ref.shape[0]
-    half = far_ref.shape[0] * CAP
-    x_ref[0:half, :] = x_near[...]
-    width = x_ref.shape[1] // CHUNKS
-    unfold(far_ref[:, :, 0:width], unfold_ref[...], x_ref.at[half : 2 * half])
     both = dot(w_in_ref[...].reshape(2 * hidden, -1), x_ref[...], ((1,), (1,)))
     gate, up = both[:hidden], both[hidden:]
     sig = jax.nn.sigmoid(gate)
@@ -189,26 +191,23 @@
 
 def hidden_kernel(groups, *refs):
     others, refs = refs[: 2 * (groups - 1)], refs[2 * (groups - 1) :]
-    far_ref, c_near, unfold_ref, w_down_ref, gate_slope_ref, up_slope_ref, c_ref, gg_ref, ug_ref = refs
-    half, share = c_near.shape
-    width = c_ref.shape[1] // CHUNKS
+    c_own, unfold_ref, w_down_ref, gate_slope_ref, up_slope_ref, c_ref, gg_ref, ug_ref = refs
+    share = c_own.shape[1]
+    half = c_own.shape[0] // 2
     narrow = share // CHUNKS
-    near_rows, far_rows = c_ref.at[0:half], c_ref.at[half : 2 * half]
     plane = lax.axis_index("row")
     bases = [pl.multiple_of(lax.rem(plane + k, groups) * share, share) for k in range(groups)]
-    near_rows[:, pl.ds(bases[0], share)] = c_near[...]
-    homes = [(far_rows, bases[0])]
-    for base in bases[1:]:
-        homes += [(near_rows, base), (far_rows, base)]
-    lines = unfold_ref.shape[0]
-    messages = [far_ref[:, :, width:]] + [other[...] for other in others]
-    flat = jnp.concatenate([m.reshape(lines, narrow) for m in messages], axis=1)
-    flat = dot(unfold_ref[...], flat).astype(BF16)
-    for i, (rows, base) in enumerate(homes):
-        for c in range(CHUNKS):
-            rows[:, pl.ds(base + c * narrow, narrow)] = flat[
-                c * half : (c + 1) * half, i * narrow : (i + 1) * narrow
-            ]
+    c_ref[:, pl.ds(bases[0], share)] = c_own[...]
+    if others:
+        lines = unfold_ref.shape[0]
+        flat = jnp.concatenate([other[...].reshape(lines, narrow) for other in others], axis=1)
+        flat = dot(unfold_ref[...], flat).astype(BF16)
+        for i in range(len(others)):
+            rows = c_ref.at[i % 2 * half : (i % 2 + 1) * half]
+            for c in range(CHUNKS):
+                rows[:, pl.ds(bases[1 + i // 2] + c * narrow, narrow)] = flat[
+                    c * half : (c + 1) * half, i * narrow : (i + 1) * narrow
+                ]
     grad = dot(w_down_ref[...], c_ref[...], ((1,), (1,)))
     gg_ref[...] = (grad * gate_slope_ref[...]).astype(BF16)
     ug_ref[...] = (grad * up_slope_ref[...]).astype(BF16)
@@ -299,13 +298,15 @@
     hidden = w_down.shape[1]
     w_in, w_down = in_hbm(w_in[0]), in_hbm(w_down[0])
     ids, gates = expert_ids.T, gate_weights.T
-    order = [int(r) for r in np.random.RandomState(ORDER_SEED).permutation(sources)]
+    orders = [[int(r) for r in np.random.RandomState(seed).permutation(sources)] for seed in SEEDS]
     places = tuple(
-        tuple(order.index(g * experts + e) for g in range(groups)) for e in range(experts)
+        tuple(orders[1].index(g * experts + e) for g in range(groups)) for e in range(experts)
     )
-    planes = [[(r // experts * PAIR + p) * experts + r % experts for r in order] for p in range(PAIR)]
-
-    def exchange(array):
+
+    def exchange(array, order):
+        planes = [
+            [(r // experts * PAIR + p) * experts + r % experts for r in order] for p in range(PAIR)
+        ]
         return lax.all_to_all(
             array, ("row", "pair", "exp"), split_axis=0, concat_axis=0, tiled=True,
             axis_index_groups=planes,
@@ -315,7 +316,7 @@
         return lax.ppermute(array, "pair", [(i, PAIR - 1 - i) for i in range(PAIR)])
 
     send = pl.pallas_call(
-        functools.partial(gather_kernel, order, experts),
+        functools.partial(gather_kernel, orders[0], experts),
         out_shape=pltpu.VMEM((sources, TILE, width + width // groups), BF16),
         in_specs=[hbm()] * 4,
         out_specs=vmem(),
@@ -329,7 +330,7 @@
         compiler_params=params(),
         name="gather_rows",
     )(in_hbm(ids), in_hbm(gates), in_hbm(tokens), in_hbm(cotangent))
-    near = exchange(send)
+    near = exchange(send, orders[0])
     far = swap(near)
     share = near[:, :, width:]
     turned = [
@@ -337,30 +338,31 @@
         for k in range(1, groups)
     ]
     square = pltpu.VMEM((sources * TILE, sources * TILE), BF16)
-    w_in, x_near, c_near, unfolding, folding = pl.pallas_call(
-        near_kernel,
-        out_shape=(pltpu.VMEM(w_in.shape, BF16),)
-        + (pltpu.VMEM((half, depth), BF16), pltpu.VMEM((half, depth // groups), BF16))
-        + (square,) * 2,
-        in_specs=[vmem(), hbm()],
+    wide = jax.ShapeDtypeStruct((2 * half, depth), BF16)
+    tall = jax.ShapeDtypeStruct((hidden, 2 * half), BF16)
+    w_in, x, c_own, unfolding, folding = pl.pallas_call(
+        functools.partial(near_kernel, tuple(orders[0].index(r) for r in orders[1])),
+        out_shape=(
+            pltpu.VMEM(w_in.shape, BF16), wide, pltpu.VMEM((2 * half, depth // groups), BF16),
+            square, square,
+        ),
+        in_specs=[vmem()] * 2 + [hbm()],
         out_specs=[vmem()] * 5,
         scratch_shapes=[pltpu.SemaphoreType.DMA],
         compiler_params=params(),
         cost_estimate=cost(0, 4 * w_in.size),
         name="near_rows",
-    )(near, w_in)
-    wide = jax.ShapeDtypeStruct((2 * half, depth), BF16)
-    tall = jax.ShapeDtypeStruct((hidden, 2 * half), BF16)
+    )(near, far, w_in)
     slope = pltpu.VMEM(tall.shape, F32)
-    x, hid, gate_slope, up_slope, w_down = pl.pallas_call(
+    hid, gate_slope, up_slope, w_down = pl.pallas_call(
         forward_kernel,
-        out_shape=(wide, tall, slope, slope, pltpu.VMEM(w_down.shape, BF16)),
-        in_specs=[vmem()] * 4 + [hbm()],
-        out_specs=[vmem()] * 5,
+        out_shape=(tall, slope, slope, pltpu.VMEM(w_down.shape, BF16)),
+        in_specs=[vmem()] * 2 + [hbm()],
+        out_specs=[vmem()] * 4,
         scratch_shapes=[pltpu.SemaphoreType.DMA],
         compiler_params=params(),
         name="gate_up",
-    )(far, x_near, unfolding, w_in, w_down)
+    )(x, w_in, w_down)
     hid, turned = lax.optimization_barrier((hid, turned))
     others = [other for array in turned for other in (array, swap(array))]
     halves = (pltpu.VMEM((half, depth), F32), pltpu.VMEM((half, depth), BF16))
@@ -377,12 +379,12 @@
     c, gg, ug = pl.pallas_call(
         functools.partial(hidden_kernel, groups),
         out_shape=(wide, tall, tall),
-        in_specs=[vmem()] * (6 + len(others)),
+        in_specs=[vmem()] * (5 + len(others)),
         out_specs=[vmem()] * 3,
         compiler_params=params(),
         cost_estimate=cost(passes, 2 * w_down.size),
         name="hidden_grad",
-    )(*others, far, c_near, unfolding, w_down, gate_slope, up_slope)
+    )(*others, c_own, unfolding, w_down, gate_slope, up_slope)
     keep_grad, away_grad = pl.pallas_call(
         back_kernel,
         out_shape=halves,
@@ -415,7 +417,7 @@
         compiler_params=params(),
         name="merge_grad",
     )(folding, keep_grad, other_grad, merged)
-    back = exchange(merged)
+    back = exchange(merged, orders[1])
     grad_in, grad_down = pl.pallas_call(
         weight_kernel,
         grid=(CHUNKS,),

time: 53.5 us -> 53.3 us (level)
  starting transfers between devices: 8.4 us -> 9.67 us
  blocking collectives: 18 us -> 17 us
    all_to_all x1, blocking collectives: 18 us -> 17 us  [exchange(): lax.all_to_all(array, ('row', 'pair', 'exp'), split_axis=0, concat_axis=0...]
    all_to_all x1, starting transfers between devices: 5.41 us -> 6.4 us  [exchange(): lax.all_to_all(array, ('row', 'pair', 'exp'), split_axis=0, concat_axis=0...]
where the time goes in v5:
time: 53.3 us; the launch traced here: 53 us
  Pallas kernels  19.2 us (36%)
  blocking collectives  17 us (32%)
  starting transfers between devices  9.67 us (18%)
  waiting for transfers between devices  6.34 us (12%)
  between operations  0.74 us (1%)
    all_to_all x1, blocking collectives, exchange(): lax.all_to_all(array, ('row', 'pair', 'exp'), split_axis=0, concat_axis=0...  17 us
    all_to_all x1, starting transfers between devices, exchange(): lax.all_to_all(array, ('row', 'pair', 'exp'), split_axis=0, concat_axis=0...  6.4 us
    all_to_all x1, waiting for transfers between devices, exchange(): lax.all_to_all(array, ('row', 'pair', 'exp'), split_axis=0, concat_axis=0...  5.9 us
    pallas_call x1, Pallas kernels, body(): pl.pallas_call(weight_kernel, grid=(CHUNKS,), out_shape=(jax.ShapeDtypeSt...  5.88 us
    pallas_call x1, Pallas kernels, body(): pl.pallas_call(functools.partial(near_kernel, tuple((orders[0].index(r) f...  2.81 us
    ppermute x1, starting transfers between devices, body(): lax.ppermute(share, 'row', [((i + k) % groups, i) for i in range(groups)])  2.33 us
    pallas_call x1, Pallas kernels, body(): pl.pallas_call(forward_kernel, out_shape=(tall, slope, slope, pltpu.VMEM(...  1.9 us
    pallas_call x1, Pallas kernels, body(): pl.pallas_call(functools.partial(gather_kernel, orders[0], experts), out_...  1.78 us
  transfers between devices with their start and end apart: 6, of which 3 were waited for; matrix products, arithmetic and copies ran while one was open for 0% of the time, Pallas kernels for 29%

profile of v5, /device:TPU:0, one launch (start us, length us, event | category | flops | bytes accessed | tf_op | source)
XLA Modules:
  0.0 53.0 jit_solution(8895182290197576487)
XLA Ops:
  0.6 1.8 %gather_rows.1 = bf16[16,16,768]{2,1,0:T(8,128)(2,1)S(1)} custom-call(s32[8,64]{1,0:T(8,128)} %bitcast.6, bf16[8,64]{1,0:T(8,128)(2,1)} %bitcast.8, bf16[64,4096]{1,0:T(8,128)(2,1)} %tok_hbm.1, bf16[64,4096]{1,0:T(8,128)(2,1)} %cot_hbm.1), custom_call_target="tpu_custom_call" | custom-call | tf_op jit(solution)/shard_map/gather_rows/pallas_call | solution.py:318
  2.4 17.0 %all_to_all.10.near_ref = bf16[16,16,768]{2,1,0:T(8,128)(2,1)S(1)} all-to-all(bf16[16,16,768]{2,1,0:T(8,128)(2,1)S(1)} %gather_rows.1), channel_id=1, replica_groups={{21,0,18,20,23,3,17,4,1,2,22,16,5,7,19,6},{29,8,26,28,31,11,25,12,9,10,..., dimensions={0} | all-to-all | bytes 786432 | tf_op jit(solution)/shard_map/all_to_all | solution.py:310
  19.4 0.0 collective-permute-start
  19.4 2.3 %collective-permute-start.1 = (bf16[16,16,256]{2,1,0:T(8,128)(2,1)S(1)}, bf16[16,16,256]{2,1,0:T(8,128)(2,1)S(1)}, u32[]{:S(2)}, u32[]{:S(2)}) collective-permute-start(bf16[16,16,256]{2,1,0:T(8,128)(2,1)S(1)} %slice.4), channel_id=1, source_target_pairs={{16,0},{0,16},{17,1},{1,17},{18,2},{2,18},{19,3},{3,19},{20,4},{4,... | collective-permute-start | bytes 393224 | tf_op jit(solution)/shard_map/ppermute | solution.py:337
  21.8 0.0 collective-permute-done.far_ref
  21.8 2.8 %near_rows.1 = (bf16[2,384,4096]{2,1,0:T(8,128)(2,1)S(1)}, bf16[64,4096]{1,0:T(8,128)(2,1)S(1)}, bf16[64,2048]{1,0:T(8,128)(2,1)S(1)}, bf16[256,256]{1,0:T(8,128)(2,1)S(1)}, bf16[256,256]{1,0:T(8,128)(2,1)S(1)}) custom-call(bf16[16,16,768]{2,1,0:T(8,128)(2,1)S(1)} %all_to_all.10.near_ref, bf16[16,16,768]{2,1,0:T(8,128)(2,1)S(1)} %collective-permute-done.far_ref, ...), custom_call_target="tpu_custom_call" | custom-call | bytes 12582912 | tf_op jit(solution)/shard_map/near_rows/pallas_call | solution.py:343
  24.6 1.9 %gate_up.1 = (bf16[384,64]{1,0:T(8,128)(2,1)S(1)}, f32[384,64]{1,0:T(8,128)S(1)}, f32[384,64]{1,0:T(8,128)S(1)}, bf16[384,4096]{1,0:T(8,128)(2,1)S(1)}) custom-call(bf16[64,4096]{1,0:T(8,128)(2,1)S(1)} %get-tuple-element.29.x_ref, bf16[2,384,4096]{2,1,0:T(8,128)(2,1)S(1)} %get-tuple-element.30.w_in_ref, bf16[384,4096]{1,0:T(8,128)(2,1)} %bitcast.11), custom_call_target="tpu_custom_call" | custom-call | tf_op jit(solution)/shard_map/gate_up/pallas_call | solution.py:357
  26.5 0.0 collective-permute-done.1.refs_0_
  26.5 0.3 collective-permute-start.2
  26.8 0.7 %down.1 = (f32[32,4096]{1,0:T(8,128)S(1)}, bf16[32,4096]{1,0:T(8,128)(2,1)S(1)}) custom-call(bf16[384,64]{1,0:T(8,128)(2,1)S(1)} %get-tuple-element.42.hid_ref, bf16[384,4096]{1,0:T(8,128)(2,1)S(1)} %get-tuple-element.35.refs_4_.w_down_ref), custom_call_target="tpu_custom_call" | custom-call | tf_op jit(solution)/shard_map/down/pallas_call | solution.py:370
  27.5 0.3 collective-permute-start.4
  27.8 0.1 collective-permute-done.2.refs_1_
  27.9 1.2 %hidden_grad.1 = (bf16[64,4096]{1,0:T(8,128)(2,1)S(1)}, bf16[384,64]{1,0:T(8,128)(2,1)S(1)}, bf16[384,64]{1,0:T(8,128)(2,1)S(1)}) custom-call(bf16[16,16,256]{2,1,0:T(8,128)(2,1)S(1)} %collective-permute-done.1.refs_0_, bf16[16,16,256]{2,1,0:T(8,128)(2,1)S(1)} %collective-permute-done.2.refs_1_, bf16[64,2048]{1,0:T(8,128)(2,1)S(1)} %get-tuple-element.33.refs_2_, ...), custom_call_target="tpu_custom_call" | custom-call | flops 201326592 | bytes 3145728 | tf_op jit(solution)/shard_map/hidden_grad/pallas_call | solution.py:379
  29.1 0.0 copy-start
  29.1 0.0 copy-start.1
  29.1 1.3 %input_grad.1 = (f32[32,4096]{1,0:T(8,128)S(1)}, bf16[32,4096]{1,0:T(8,128)(2,1)S(1)}) custom-call(bf16[384,64]{1,0:T(8,128)(2,1)S(1)} %get-tuple-element.38.gg_ref.after_ref, bf16[384,64]{1,0:T(8,128)(2,1)S(1)} %get-tuple-element.39.ug_ref, bf16[2,384,4096]{2,1,0:T(8,128)(2,1)S(1)} %get-tuple-element.30.w_in_ref), custom_call_target="tpu_custom_call" | custom-call | flops 402653184 | bytes 6291456 | tf_op jit(solution)/shard_map/input_grad/pallas_call | solution.py:388
  30.4 0.3 collective-permute-start.3
  30.7 0.0 collective-permute-done.4.other_ref
  30.7 0.9 %merge_out.1.first_hbm = bf16[16,32,512]{2,1,0:T(8,128)(2,1)} custom-call(bf16[256,256]{1,0:T(8,128)(2,1)S(1)} %get-tuple-element.28.fold_ref, f32[32,4096]{1,0:T(8,128)S(1)} %get-tuple-element.43.keep_ref, bf16[32,4096]{1,0:T(8,128)(2,1)S(1)} %collective-permute-done.4.other_ref), custom_call_target="tpu_custom_call" | custom-call | bytes 1048576 | tf_op jit(solution)/shard_map/merge_out/pallas_call | solution.py:400
  31.6 0.4 collective-permute-done.3.other_ref
  32.0 0.9 %merge_grad.1 = bf16[16,32,512]{2,1,0:T(8,128)(2,1)} custom-call(bf16[256,256]{1,0:T(8,128)(2,1)S(1)} %get-tuple-element.28.fold_ref, f32[32,4096]{1,0:T(8,128)S(1)} %get-tuple-element.40.keep_ref, bf16[32,4096]{1,0:T(8,128)(2,1)S(1)} %collective-permute-done.3.other_ref, bf16[16,32,512]{2,1,0:T(8,128)(2,1)} %merge_out.1.first_hbm), custom_call_target="tpu_custom_call", output_to_operand_aliasing={{}: (3, {})} | custom-call | tf_op jit(solution)/shard_map/merge_grad/pallas_call | solution.py:410
  32.9 6.4 %all-to-all-start.1 = ((bf16[16,32,512]{2,1,0:T(8,128)(2,1)}), bf16[16,32,512]{2,1,0:T(8,128)(2,1)S(1)}, u32[]{:S(2)}, u32[]{:S(2)}) async-start(bf16[16,32,512]{2,1,0:T(8,128)(2,1)} %merge_grad.1), calls=%async_computation.1 | async-start | bytes 1048576 | tf_op jit(solution)/shard_map/all_to_all | solution.py:310
  39.3 0.0 copy-done
  39.3 0.0 copy-done.1
  39.3 0.6 %slot_tables.1 = (bf16[512,128]{1,0:T(8,128)(2,1)S(1)}, bf16[512,128]{1,0:T(8,128)(2,1)S(1)}) custom-call(s32[8,64]{1,0:T(8,128)S(1)} %bitcast.7, bf16[8,64]{1,0:T(8,128)(2,1)S(1)} %bitcast.9, bf16[384,64]{1,0:T(8,128)(2,1)S(1)} %get-tuple-element.38.gg_ref.after_ref), custom_call_target="tpu_custom_call" | custom-call | tf_op jit(solution)/shard_map/slot_tables/pallas_call | solution.py:439
  40.0 5.9 %weight_grads.1 = (bf16[2,384,4096]{2,1,0:T(8,128)(2,1)}, bf16[384,4096]{1,0:T(8,128)(2,1)}) custom-call(bf16[64,4096]{1,0:T(8,128)(2,1)S(1)} %get-tuple-element.29.x_ref, bf16[64,4096]{1,0:T(8,128)(2,1)S(1)} %get-tuple-element.49.c_ref, bf16[384,64]{1,0:T(8,128)(2,1)S(1)} %get-tuple-element.42.hid_ref, ...), custom_call_target="tpu_custom_call" | custom-call | flops 603979776 | bytes 10485760 | tf_op jit(solution)/shard_map/weight_grads/pallas_call | solution.py:421
  45.9 5.9 %all-to-all-done.1.back_ref = bf16[16,32,512]{2,1,0:T(8,128)(2,1)S(1)} async-done(((bf16[16,32,512]{2,1,0:T(8,128)(2,1)}), bf16[16,32,512]{2,1,0:T(8,128)(2,1)S(1)}, u32[]{:S(2)}, u32[]{:S(2)}) %all-to-all-start.1) | async-done | bytes 524320 | tf_op jit(solution)/shard_map/all_to_all | solution.py:310
  51.8 1.2 %combine_rows.1 = (bf16[64,4096]{1,0:T(8,128)(2,1)}, bf16[64,4096]{1,0:T(8,128)(2,1)}) custom-call(bf16[16,32,512]{2,1,0:T(8,128)(2,1)S(1)} %all-to-all-done.1.back_ref, bf16[512,128]{1,0:T(8,128)(2,1)S(1)} %get-tuple-element.45.pick_ref, bf16[512,128]{1,0:T(8,128)(2,1)S(1)} %get-tuple-element.46.weigh_ref), custom_call_target="tpu_custom_call" | custom-call | tf_op jit(solution)/shard_map/combine_rows/pallas_call | solution.py:447
  (1 shorter events, 0.0 us)
Async XLA Ops:
  19.4 2.4 %collective-permute-start = (bf16[16,16,768]{2,1,0:T(8,128)(2,1)S(1)}, bf16[16,16,768]{2,1,0:T(8,128)(2,1)S(1)}, u32[]{:S(2)}, u32[]{:S(2)}) collective-permute-start(bf16[16,16,768]{2,1,0:T(8,128)(2,1)S(1)} %all_to_all.10.near_ref), channel_id=1, source_target_pairs={{0,8},{8,0},{1,9},{9,1},{2,10},{10,2},{3,11},{11,3},{4,12},{12,4},... | collective-permute-start | bytes 1179656 | tf_op jit(solution)/shard_map/ppermute | solution.py:316
  19.4 7.1 %collective-permute-start.1 = (bf16[16,16,256]{2,1,0:T(8,128)(2,1)S(1)}, bf16[16,16,256]{2,1,0:T(8,128)(2,1)S(1)}, u32[]{:S(2)}, u32[]{:S(2)}) collective-permute-start(bf16[16,16,256]{2,1,0:T(8,128)(2,1)S(1)} %slice.4), channel_id=1, source_target_pairs={{16,0},{0,16},{17,1},{1,17},{18,2},{2,18},{19,3},{3,19},{20,4},{4,... | collective-permute-start | bytes 393224 | tf_op jit(solution)/shard_map/ppermute | solution.py:337
  26.5 1.4 %collective-permute-start.2 = (bf16[16,16,256]{2,1,0:T(8,128)(2,1)S(1)}, bf16[16,16,256]{2,1,0:T(8,128)(2,1)S(1)}, u32[]{:S(2)}, u32[]{:S(2)}) collective-permute-start(bf16[16,16,256]{2,1,0:T(8,128)(2,1)S(1)} %collective-permute-done.1.refs_0_), channel_id=1, source_target_pairs={{0,8},{8,0},{1,9},{9,1},{2,10},{10,2},{3,11},{11,3},{4,12},{12,4},... | collective-permute-start | bytes 393224 | tf_op jit(solution)/shard_map/ppermute | solution.py:316
  27.5 3.2 %collective-permute-start.4 = (bf16[32,4096]{1,0:T(8,128)(2,1)S(1)}, bf16[32,4096]{1,0:T(8,128)(2,1)S(1)}, u32[]{:S(2)}, u32[]{:S(2)}) collective-permute-start(bf16[32,4096]{1,0:T(8,128)(2,1)S(1)} %get-tuple-element.44), channel_id=1, source_target_pairs={{0,8},{8,0},{1,9},{9,1},{2,10},{10,2},{3,11},{11,3},{4,12},{12,4},... | collective-permute-start | bytes 786440 | tf_op jit(solution)/shard_map/ppermute | solution.py:316
  29.1 10.2 %copy-start = (s32[64,8]{0,1:T(8,128)S(1)}, s32[64,8]{0,1:T(8,128)}, u32[]{:S(2)}) copy-start(s32[64,8]{0,1:T(8,128)} %param.8) | copy-start | bytes 6148
  29.1 10.2 %copy-start.1 = (bf16[64,8]{0,1:T(8,128)(2,1)S(1)}, bf16[64,8]{0,1:T(8,128)(2,1)}, u32[]{:S(2)}) copy-start(bf16[64,8]{0,1:T(8,128)(2,1)} %param.9) | copy-start | bytes 3076
  30.4 1.6 %collective-permute-start.3 = (bf16[32,4096]{1,0:T(8,128)(2,1)S(1)}, bf16[32,4096]{1,0:T(8,128)(2,1)S(1)}, u32[]{:S(2)}, u32[]{:S(2)}) collective-permute-start(bf16[32,4096]{1,0:T(8,128)(2,1)S(1)} %get-tuple-element.41), channel_id=1, source_target_pairs={{0,8},{8,0},{1,9},{9,1},{2,10},{10,2},{3,11},{11,3},{4,12},{12,4},... | collective-permute-start | bytes 786440 | tf_op jit(solution)/shard_map/ppermute | solution.py:316
  32.9 18.8 %all-to-all-start.1 = ((bf16[16,32,512]{2,1,0:T(8,128)(2,1)}), bf16[16,32,512]{2,1,0:T(8,128)(2,1)S(1)}, u32[]{:S(2)}, u32[]{:S(2)}) async-start(bf16[16,32,512]{2,1,0:T(8,128)(2,1)} %merge_grad.1), calls=%async_computation.1 | async-start | bytes 1048576 | tf_op jit(solution)/shard_map/all_to_all | solution.py:310

commit v6 on v4

--- a/solution.py
+++ b/solution.py
@@ -13,7 +13,7 @@
 CHUNKS = TILE // CAP
 PAIR = 2
 STEPS = 2
-ORDER_SEED = 2
+SEEDS = (40, 2)
 F32 = jnp.float32
 BF16 = jnp.bfloat16
 LIMIT = 24 * 1024 * 1024
@@ -135,7 +135,7 @@
         out[:, c * width : (c + 1) * width] = flat[c * half : (c + 1) * half]
 
 
-def near_kernel(near_ref, w_in_hbm, w_in_ref, x_ref, c_ref, unfold_ref, fold_ref, sem):
+def near_kernel(origins, near_ref, w_in_hbm, w_in_ref, x_ref, c_ref, unfold_ref, fold_ref, sem):
     fetch = pltpu.make_async_copy(w_in_hbm, w_in_ref, sem)
     fetch.start()
     sources = near_ref.shape[0]
@@ -145,10 +145,13 @@
     perm = (row % half // CAP) * TILE + (row // half) * CAP + row % CAP == col
     perm = jnp.where(perm, 1.0, 0.0).astype(BF16)
     unfold_ref[...] = perm
-    back = (row // CAP % CHUNKS) * half + (row // TILE) * CAP + row % CAP == col
-    fold_ref[...] = jnp.where(back, 1.0, 0.0).astype(BF16)
     unfold(near_ref[:, :, 0:width], perm, x_ref)
     unfold(near_ref[:, :, width:], perm, c_ref)
+    row, col = iota((TILE, lines), 0), iota((TILE, lines), 1)
+    place = row // CAP * half + row % CAP
+    for p, s in enumerate(origins):
+        tile = jnp.where(place + s * CAP == col, 1.0, 0.0).astype(BF16)
+        fold_ref[p * TILE : (p + 1) * TILE, :] = tile
     fetch.wait()
 
 
@@ -299,13 +302,15 @@
     hidden = w_down.shape[1]
     w_in, w_down = in_hbm(w_in[0]), in_hbm(w_down[0])
     ids, gates = expert_ids.T, gate_weights.T
-    order = [int(r) for r in np.random.RandomState(ORDER_SEED).permutation(sources)]
+    orders = [[int(r) for r in np.random.RandomState(seed).permutation(sources)] for seed in SEEDS]
     places = tuple(
-        tuple(order.index(g * experts + e) for g in range(groups)) for e in range(experts)
+        tuple(orders[1].index(g * experts + e) for g in range(groups)) for e in range(experts)
     )
-    planes = [[(r // experts * PAIR + p) * experts + r % experts for r in order] for p in range(PAIR)]
-
-    def exchange(array):
+
+    def exchange(array, order):
+        planes = [
+            [(r // experts * PAIR + p) * experts + r % experts for r in order] for p in range(PAIR)
+        ]
         return lax.all_to_all(
             array, ("row", "pair", "exp"), split_axis=0, concat_axis=0, tiled=True,
             axis_index_groups=planes,
@@ -315,7 +320,7 @@
         return lax.ppermute(array, "pair", [(i, PAIR - 1 - i) for i in range(PAIR)])
 
     send = pl.pallas_call(
-        functools.partial(gather_kernel, order, experts),
+        functools.partial(gather_kernel, orders[0], experts),
         out_shape=pltpu.VMEM((sources, TILE, width + width // groups), BF16),
         in_specs=[hbm()] * 4,
         out_specs=vmem(),
@@ -329,7 +334,7 @@
         compiler_params=params(),
         name="gather_rows",
     )(in_hbm(ids), in_hbm(gates), in_hbm(tokens), in_hbm(cotangent))
-    near = exchange(send)
+    near = exchange(send, orders[0])
     far = swap(near)
     share = near[:, :, width:]
     turned = [
@@ -337,11 +342,14 @@
         for k in range(1, groups)
     ]
     square = pltpu.VMEM((sources * TILE, sources * TILE), BF16)
+    wide = jax.ShapeDtypeStruct((2 * half, depth), BF16)
+    tall = jax.ShapeDtypeStruct((hidden, 2 * half), BF16)
     w_in, x_near, c_near, unfolding, folding = pl.pallas_call(
-        near_kernel,
-        out_shape=(pltpu.VMEM(w_in.shape, BF16),)
-        + (pltpu.VMEM((half, depth), BF16), pltpu.VMEM((half, depth // groups), BF16))
-        + (square,) * 2,
+        functools.partial(near_kernel, tuple(orders[0].index(r) for r in orders[1])),
+        out_shape=(
+            pltpu.VMEM(w_in.shape, BF16), pltpu.VMEM((half, depth), BF16),
+            pltpu.VMEM((half, depth // groups), BF16), square, square,
+        ),
         in_specs=[vmem(), hbm()],
         out_specs=[vmem()] * 5,
         scratch_shapes=[pltpu.SemaphoreType.DMA],
@@ -349,8 +357,6 @@
         cost_estimate=cost(0, 4 * w_in.size),
         name="near_rows",
     )(near, w_in)
-    wide = jax.ShapeDtypeStruct((2 * half, depth), BF16)
-    tall = jax.ShapeDtypeStruct((hidden, 2 * half), BF16)
     slope = pltpu.VMEM(tall.shape, F32)
     x, hid, gate_slope, up_slope, w_down = pl.pallas_call(
         forward_kernel,
@@ -415,7 +421,7 @@
         compiler_params=params(),
         name="merge_grad",
     )(folding, keep_grad, other_grad, merged)
-    back = exchange(merged)
+    back = exchange(merged, orders[1])
     grad_in, grad_down = pl.pallas_call(
         weight_kernel,
         grid=(CHUNKS,),

time: 53.5 us -> 53.5 us (level)
  starting transfers between devices: 8.4 us -> 9.48 us
  blocking collectives: 18 us -> 17 us
    all_to_all x1, blocking collectives: 18 us -> 17 us  [exchange(): lax.all_to_all(array, ('row', 'pair', 'exp'), split_axis=0, concat_axis=0...]
    all_to_all x1, starting transfers between devices: 5.41 us -> 6.22 us  [exchange(): lax.all_to_all(array, ('row', 'pair', 'exp'), split_axis=0, concat_axis=0...]
where the time goes in v6:
time: 53.5 us; the launch traced here: 53.2 us
  Pallas kernels  19.5 us (36%)
  blocking collectives  17 us (32%)
  starting transfers between devices  9.48 us (18%)
  waiting for transfers between devices  6.43 us (12%)
  between operations  0.75 us (1%)
    all_to_all x1, blocking collectives, exchange(): lax.all_to_all(array, ('row', 'pair', 'exp'), split_axis=0, concat_axis=0...  17 us
    all_to_all x1, starting transfers between devices, exchange(): lax.all_to_all(array, ('row', 'pair', 'exp'), split_axis=0, concat_axis=0...  6.22 us
    all_to_all x1, waiting for transfers between devices, exchange(): lax.all_to_all(array, ('row', 'pair', 'exp'), split_axis=0, concat_axis=0...  5.98 us
    pallas_call x1, Pallas kernels, body(): pl.pallas_call(weight_kernel, grid=(CHUNKS,), out_shape=(jax.ShapeDtypeSt...  5.88 us
    pallas_call x1, Pallas kernels, body(): pl.pallas_call(functools.partial(near_kernel, tuple((orders[0].index(r) f...  2.8 us
    ppermute x1, starting transfers between devices, body(): lax.ppermute(share, 'row', [((i + k) % groups, i) for i in range(groups)])  2.33 us
    pallas_call x1, Pallas kernels, body(): pl.pallas_call(forward_kernel, out_shape=(wide, tall, slope, slope, pltpu...  1.97 us
    pallas_call x1, Pallas kernels, body(): pl.pallas_call(functools.partial(gather_kernel, orders[0], experts), out_...  1.78 us
  transfers between devices with their start and end apart: 6, of which 3 were waited for; matrix products, arithmetic and copies ran while one was open for 0% of the time, Pallas kernels for 29%

profile of v6, /device:TPU:0, one launch (start us, length us, event | category | flops | bytes accessed | tf_op | source)
XLA Modules:
  0.0 53.2 jit_solution(962173814105354474)
XLA Ops:
  0.6 1.8 %gather_rows.1 = bf16[16,16,768]{2,1,0:T(8,128)(2,1)S(1)} custom-call(s32[8,64]{1,0:T(8,128)} %bitcast.6, bf16[8,64]{1,0:T(8,128)(2,1)} %bitcast.8, bf16[64,4096]{1,0:T(8,128)(2,1)} %tok_hbm.1, bf16[64,4096]{1,0:T(8,128)(2,1)} %cot_hbm.1), custom_call_target="tpu_custom_call" | custom-call | tf_op jit(solution)/shard_map/gather_rows/pallas_call | solution.py:322
  2.4 17.0 %all_to_all.10.near_ref = bf16[16,16,768]{2,1,0:T(8,128)(2,1)S(1)} all-to-all(bf16[16,16,768]{2,1,0:T(8,128)(2,1)S(1)} %gather_rows.1), channel_id=1, replica_groups={{21,0,18,20,23,3,17,4,1,2,22,16,5,7,19,6},{29,8,26,28,31,11,25,12,9,10,..., dimensions={0} | all-to-all | bytes 786432 | tf_op jit(solution)/shard_map/all_to_all | solution.py:314
  19.4 0.0 collective-permute-start
  19.4 2.3 %collective-permute-start.1 = (bf16[16,16,256]{2,1,0:T(8,128)(2,1)S(1)}, bf16[16,16,256]{2,1,0:T(8,128)(2,1)S(1)}, u32[]{:S(2)}, u32[]{:S(2)}) collective-permute-start(bf16[16,16,256]{2,1,0:T(8,128)(2,1)S(1)} %slice.4), channel_id=1, source_target_pairs={{16,0},{0,16},{17,1},{1,17},{18,2},{2,18},{19,3},{3,19},{20,4},{4,... | collective-permute-start | bytes 393224 | tf_op jit(solution)/shard_map/ppermute | solution.py:341
  21.8 2.8 %near_rows.1 = (bf16[2,384,4096]{2,1,0:T(8,128)(2,1)S(1)}, bf16[32,4096]{1,0:T(8,128)(2,1)S(1)}, bf16[32,2048]{1,0:T(8,128)(2,1)S(1)}, bf16[256,256]{1,0:T(8,128)(2,1)S(1)}, bf16[256,256]{1,0:T(8,128)(2,1)S(1)}) custom-call(bf16[16,16,768]{2,1,0:T(8,128)(2,1)S(1)} %all_to_all.10.near_ref, bf16[2,384,4096]{2,1,0:T(8,128)(2,1)} %bitcast.10), custom_call_target="tpu_custom_call" | custom-call | bytes 12582912 | tf_op jit(solution)/shard_map/near_rows/pallas_call | solution.py:347
  24.6 0.0 collective-permute-done.far_ref.refs_2_
  24.6 2.0 %gate_up.1 = (bf16[64,4096]{1,0:T(8,128)(2,1)S(1)}, bf16[384,64]{1,0:T(8,128)(2,1)S(1)}, f32[384,64]{1,0:T(8,128)S(1)}, f32[384,64]{1,0:T(8,128)S(1)}, bf16[384,4096]{1,0:T(8,128)(2,1)S(1)}) custom-call(bf16[16,16,768]{2,1,0:T(8,128)(2,1)S(1)} %collective-permute-done.far_ref.refs_2_, bf16[32,4096]{1,0:T(8,128)(2,1)S(1)} %get-tuple-element.30.x_near, ...), custom_call_target="tpu_custom_call" | custom-call | tf_op jit(solution)/shard_map/gate_up/pallas_call | solution.py:361
  26.5 0.0 collective-permute-done.1.refs_0_
  26.6 0.3 collective-permute-start.2
  26.8 0.7 %down.1 = (f32[32,4096]{1,0:T(8,128)S(1)}, bf16[32,4096]{1,0:T(8,128)(2,1)S(1)}) custom-call(bf16[384,64]{1,0:T(8,128)(2,1)S(1)} %get-tuple-element.43.hid_ref, bf16[384,4096]{1,0:T(8,128)(2,1)S(1)} %get-tuple-element.36.refs_5_.w_down_ref), custom_call_target="tpu_custom_call" | custom-call | tf_op jit(solution)/shard_map/down/pallas_call | solution.py:374
  27.5 0.4 collective-permute-start.4
  27.9 0.1 collective-permute-done.2.refs_1_
  28.0 1.4 %hidden_grad.1 = (bf16[64,4096]{1,0:T(8,128)(2,1)S(1)}, bf16[384,64]{1,0:T(8,128)(2,1)S(1)}, bf16[384,64]{1,0:T(8,128)(2,1)S(1)}) custom-call(bf16[16,16,256]{2,1,0:T(8,128)(2,1)S(1)} %collective-permute-done.1.refs_0_, bf16[16,16,256]{2,1,0:T(8,128)(2,1)S(1)} %collective-permute-done.2.refs_1_, ...), custom_call_target="tpu_custom_call" | custom-call | flops 201326592 | bytes 3145728 | tf_op jit(solution)/shard_map/hidden_grad/pallas_call | solution.py:383
  29.4 0.0 copy-start
  29.4 0.0 copy-start.1
  29.4 1.3 %input_grad.1 = (f32[32,4096]{1,0:T(8,128)S(1)}, bf16[32,4096]{1,0:T(8,128)(2,1)S(1)}) custom-call(bf16[384,64]{1,0:T(8,128)(2,1)S(1)} %get-tuple-element.39.gg_ref.after_ref, bf16[384,64]{1,0:T(8,128)(2,1)S(1)} %get-tuple-element.40.ug_ref, bf16[2,384,4096]{2,1,0:T(8,128)(2,1)S(1)} %get-tuple-element.32.w_in_ref), custom_call_target="tpu_custom_call" | custom-call | flops 402653184 | bytes 6291456 | tf_op jit(solution)/shard_map/input_grad/pallas_call | solution.py:392
  30.7 0.3 collective-permute-start.3
  31.0 0.0 collective-permute-done.4.other_ref
  31.0 0.9 %merge_out.1.first_hbm = bf16[16,32,512]{2,1,0:T(8,128)(2,1)} custom-call(bf16[256,256]{1,0:T(8,128)(2,1)S(1)} %get-tuple-element.29.fold_ref, f32[32,4096]{1,0:T(8,128)S(1)} %get-tuple-element.44.keep_ref, bf16[32,4096]{1,0:T(8,128)(2,1)S(1)} %collective-permute-done.4.other_ref), custom_call_target="tpu_custom_call" | custom-call | bytes 1048576 | tf_op jit(solution)/shard_map/merge_out/pallas_call | solution.py:404
  31.9 0.4 collective-permute-done.3.other_ref
  32.3 0.9 %merge_grad.1 = bf16[16,32,512]{2,1,0:T(8,128)(2,1)} custom-call(bf16[256,256]{1,0:T(8,128)(2,1)S(1)} %get-tuple-element.29.fold_ref, f32[32,4096]{1,0:T(8,128)S(1)} %get-tuple-element.41.keep_ref, bf16[32,4096]{1,0:T(8,128)(2,1)S(1)} %collective-permute-done.3.other_ref, bf16[16,32,512]{2,1,0:T(8,128)(2,1)} %merge_out.1.first_hbm), custom_call_target="tpu_custom_call", output_to_operand_aliasing={{}: (3, {})} | custom-call | tf_op jit(solution)/shard_map/merge_grad/pallas_call | solution.py:414
  33.2 6.2 %all-to-all-start.1 = ((bf16[16,32,512]{2,1,0:T(8,128)(2,1)}), bf16[16,32,512]{2,1,0:T(8,128)(2,1)S(1)}, u32[]{:S(2)}, u32[]{:S(2)}) async-start(bf16[16,32,512]{2,1,0:T(8,128)(2,1)} %merge_grad.1), calls=%async_computation.1 | async-start | bytes 1048576 | tf_op jit(solution)/shard_map/all_to_all | solution.py:314
  39.4 0.0 copy-done
  39.4 0.0 copy-done.1
  39.4 0.6 %slot_tables.1 = (bf16[512,128]{1,0:T(8,128)(2,1)S(1)}, bf16[512,128]{1,0:T(8,128)(2,1)S(1)}) custom-call(s32[8,64]{1,0:T(8,128)S(1)} %bitcast.7, bf16[8,64]{1,0:T(8,128)(2,1)S(1)} %bitcast.9, bf16[384,64]{1,0:T(8,128)(2,1)S(1)} %get-tuple-element.39.gg_ref.after_ref), custom_call_target="tpu_custom_call" | custom-call | tf_op jit(solution)/shard_map/slot_tables/pallas_call | solution.py:443
  40.1 5.9 %weight_grads.1 = (bf16[2,384,4096]{2,1,0:T(8,128)(2,1)}, bf16[384,4096]{1,0:T(8,128)(2,1)}) custom-call(bf16[64,4096]{1,0:T(8,128)(2,1)S(1)} %get-tuple-element.50.x_ref, bf16[64,4096]{1,0:T(8,128)(2,1)S(1)} %get-tuple-element.51.c_ref, bf16[384,64]{1,0:T(8,128)(2,1)S(1)} %get-tuple-element.43.hid_ref, ...), custom_call_target="tpu_custom_call" | custom-call | flops 603979776 | bytes 10485760 | tf_op jit(solution)/shard_map/weight_grads/pallas_call | solution.py:425
  46.0 6.0 %all-to-all-done.1.back_ref = bf16[16,32,512]{2,1,0:T(8,128)(2,1)S(1)} async-done(((bf16[16,32,512]{2,1,0:T(8,128)(2,1)}), bf16[16,32,512]{2,1,0:T(8,128)(2,1)S(1)}, u32[]{:S(2)}, u32[]{:S(2)}) %all-to-all-start.1) | async-done | bytes 524320 | tf_op jit(solution)/shard_map/all_to_all | solution.py:314
  51.9 1.2 %combine_rows.1 = (bf16[64,4096]{1,0:T(8,128)(2,1)}, bf16[64,4096]{1,0:T(8,128)(2,1)}) custom-call(bf16[16,32,512]{2,1,0:T(8,128)(2,1)S(1)} %all-to-all-done.1.back_ref, bf16[512,128]{1,0:T(8,128)(2,1)S(1)} %get-tuple-element.46.pick_ref, bf16[512,128]{1,0:T(8,128)(2,1)S(1)} %get-tuple-element.47.weigh_ref), custom_call_target="tpu_custom_call" | custom-call | tf_op jit(solution)/shard_map/combine_rows/pallas_call | solution.py:451
  (1 shorter events, 0.0 us)
Async XLA Ops:
  19.4 5.2 %collective-permute-start = (bf16[16,16,768]{2,1,0:T(8,128)(2,1)S(1)}, bf16[16,16,768]{2,1,0:T(8,128)(2,1)S(1)}, u32[]{:S(2)}, u32[]{:S(2)}) collective-permute-start(bf16[16,16,768]{2,1,0:T(8,128)(2,1)S(1)} %all_to_all.10.near_ref), channel_id=1, source_target_pairs={{0,8},{8,0},{1,9},{9,1},{2,10},{10,2},{3,11},{11,3},{4,12},{12,4},... | collective-permute-start | bytes 1179656 | tf_op jit(solution)/shard_map/ppermute | solution.py:320
  19.4 7.1 %collective-permute-start.1 = (bf16[16,16,256]{2,1,0:T(8,128)(2,1)S(1)}, bf16[16,16,256]{2,1,0:T(8,128)(2,1)S(1)}, u32[]{:S(2)}, u32[]{:S(2)}) collective-permute-start(bf16[16,16,256]{2,1,0:T(8,128)(2,1)S(1)} %slice.4), channel_id=1, source_target_pairs={{16,0},{0,16},{17,1},{1,17},{18,2},{2,18},{19,3},{3,19},{20,4},{4,... | collective-permute-start | bytes 393224 | tf_op jit(solution)/shard_map/ppermute | solution.py:341
  26.6 1.4 %collective-permute-start.2 = (bf16[16,16,256]{2,1,0:T(8,128)(2,1)S(1)}, bf16[16,16,256]{2,1,0:T(8,128)(2,1)S(1)}, u32[]{:S(2)}, u32[]{:S(2)}) collective-permute-start(bf16[16,16,256]{2,1,0:T(8,128)(2,1)S(1)} %collective-permute-done.1.refs_0_), channel_id=1, source_target_pairs={{0,8},{8,0},{1,9},{9,1},{2,10},{10,2},{3,11},{11,3},{4,12},{12,4},... | collective-permute-start | bytes 393224 | tf_op jit(solution)/shard_map/ppermute | solution.py:320
  27.5 3.4 %collective-permute-start.4 = (bf16[32,4096]{1,0:T(8,128)(2,1)S(1)}, bf16[32,4096]{1,0:T(8,128)(2,1)S(1)}, u32[]{:S(2)}, u32[]{:S(2)}) collective-permute-start(bf16[32,4096]{1,0:T(8,128)(2,1)S(1)} %get-tuple-element.45), channel_id=1, source_target_pairs={{0,8},{8,0},{1,9},{9,1},{2,10},{10,2},{3,11},{11,3},{4,12},{12,4},... | collective-permute-start | bytes 786440 | tf_op jit(solution)/shard_map/ppermute | solution.py:320
  29.4 10.0 %copy-start = (s32[64,8]{0,1:T(8,128)S(1)}, s32[64,8]{0,1:T(8,128)}, u32[]{:S(2)}) copy-start(s32[64,8]{0,1:T(8,128)} %param.8) | copy-start | bytes 6148
  29.4 10.0 %copy-start.1 = (bf16[64,8]{0,1:T(8,128)(2,1)S(1)}, bf16[64,8]{0,1:T(8,128)(2,1)}, u32[]{:S(2)}) copy-start(bf16[64,8]{0,1:T(8,128)(2,1)} %param.9) | copy-start | bytes 3076
  30.7 1.6 %collective-permute-start.3 = (bf16[32,4096]{1,0:T(8,128)(2,1)S(1)}, bf16[32,4096]{1,0:T(8,128)(2,1)S(1)}, u32[]{:S(2)}, u32[]{:S(2)}) collective-permute-start(bf16[32,4096]{1,0:T(8,128)(2,1)S(1)} %get-tuple-element.42), channel_id=1, source_target_pairs={{0,8},{8,0},{1,9},{9,1},{2,10},{10,2},{3,11},{11,3},{4,12},{12,4},... | collective-permute-start | bytes 786440 | tf_op jit(solution)/shard_map/ppermute | solution.py:320
  33.2 18.7 %all-to-all-start.1 = ((bf16[16,32,512]{2,1,0:T(8,128)(2,1)}), bf16[16,32,512]{2,1,0:T(8,128)(2,1)S(1)}, u32[]{:S(2)}, u32[]{:S(2)}) async-start(bf16[16,32,512]{2,1,0:T(8,128)(2,1)} %merge_grad.1), calls=%async_computation.1 | async-start | bytes 1048576 | tf_op jit(solution)/shard_map/all_to_all | solution.py:314

commit v7 on v6

--- a/solution.py
+++ b/solution.py
@@ -13,7 +13,7 @@
 CHUNKS = TILE // CAP
 PAIR = 2
 STEPS = 2
-SEEDS = (40, 2)
+SEEDS = (40, 4)
 F32 = jnp.float32
 BF16 = jnp.bfloat16
 LIMIT = 24 * 1024 * 1024

time: 53.5 us -> 52.8 us (0.987)
  waiting for transfers between devices: 6.43 us -> 5.73 us
    all_to_all x1, waiting for transfers between devices: 5.98 us -> 5.28 us  [exchange(): lax.all_to_all(array, ('row', 'pair', 'exp'), split_axis=0, concat_axis=0...]
  transfers between devices with their start and end apart: 6 -> 6, of which waited for: 3 -> 3; matrix products, arithmetic and copies ran while one was open for 0% -> 0% of each run, Pallas kernels for 29% -> 30%
where the time goes in v7:
time: 52.8 us; the launch traced here: 52.5 us
  Pallas kernels  19.5 us (37%)
  blocking collectives  17 us (32%)
  starting transfers between devices  9.48 us (18%)
  waiting for transfers between devices  5.73 us (11%)
  between operations  0.75 us (1%)
    all_to_all x1, blocking collectives, exchange(): lax.all_to_all(array, ('row', 'pair', 'exp'), split_axis=0, concat_axis=0...  17 us
    all_to_all x1, starting transfers between devices, exchange(): lax.all_to_all(array, ('row', 'pair', 'exp'), split_axis=0, concat_axis=0...  6.22 us
    pallas_call x1, Pallas kernels, body(): pl.pallas_call(weight_kernel, grid=(CHUNKS,), out_shape=(jax.ShapeDtypeSt...  5.88 us
    all_to_all x1, waiting for transfers between devices, exchange(): lax.all_to_all(array, ('row', 'pair', 'exp'), split_axis=0, concat_axis=0...  5.28 us
    pallas_call x1, Pallas kernels, body(): pl.pallas_call(functools.partial(near_kernel, tuple((orders[0].index(r) f...  2.8 us
    ppermute x1, starting transfers between devices, body(): lax.ppermute(share, 'row', [((i + k) % groups, i) for i in range(groups)])  2.33 us
    pallas_call x1, Pallas kernels, body(): pl.pallas_call(forward_kernel, out_shape=(wide, tall, slope, slope, pltpu...  1.97 us
    pallas_call x1, Pallas kernels, body(): pl.pallas_call(functools.partial(gather_kernel, orders[0], experts), out_...  1.78 us
  transfers between devices with their start and end apart: 6, of which 3 were waited for; matrix products, arithmetic and copies ran while one was open for 0% of the time, Pallas kernels for 30%

profile of v7, /device:TPU:0, one launch (start us, length us, event | category | flops | bytes accessed | tf_op | source)
XLA Modules:
  0.0 52.5 jit_solution(4743486476092044974)
XLA Ops:
  0.6 1.8 %gather_rows.1 = bf16[16,16,768]{2,1,0:T(8,128)(2,1)S(1)} custom-call(s32[8,64]{1,0:T(8,128)} %bitcast.6, bf16[8,64]{1,0:T(8,128)(2,1)} %bitcast.8, bf16[64,4096]{1,0:T(8,128)(2,1)} %tok_hbm.1, bf16[64,4096]{1,0:T(8,128)(2,1)} %cot_hbm.1), custom_call_target="tpu_custom_call" | custom-call | tf_op jit(solution)/shard_map/gather_rows/pallas_call | solution.py:322
  2.4 17.0 %all_to_all.10.near_ref = bf16[16,16,768]{2,1,0:T(8,128)(2,1)S(1)} all-to-all(bf16[16,16,768]{2,1,0:T(8,128)(2,1)S(1)} %gather_rows.1), channel_id=1, replica_groups={{21,0,18,20,23,3,17,4,1,2,22,16,5,7,19,6},{29,8,26,28,31,11,25,12,9,10,..., dimensions={0} | all-to-all | bytes 786432 | tf_op jit(solution)/shard_map/all_to_all | solution.py:314
  19.4 0.0 collective-permute-start
  19.4 2.3 %collective-permute-start.1 = (bf16[16,16,256]{2,1,0:T(8,128)(2,1)S(1)}, bf16[16,16,256]{2,1,0:T(8,128)(2,1)S(1)}, u32[]{:S(2)}, u32[]{:S(2)}) collective-permute-start(bf16[16,16,256]{2,1,0:T(8,128)(2,1)S(1)} %slice.4), channel_id=1, source_target_pairs={{16,0},{0,16},{17,1},{1,17},{18,2},{2,18},{19,3},{3,19},{20,4},{4,... | collective-permute-start | bytes 393224 | tf_op jit(solution)/shard_map/ppermute | solution.py:341
  21.8 2.8 %near_rows.1 = (bf16[2,384,4096]{2,1,0:T(8,128)(2,1)S(1)}, bf16[32,4096]{1,0:T(8,128)(2,1)S(1)}, bf16[32,2048]{1,0:T(8,128)(2,1)S(1)}, bf16[256,256]{1,0:T(8,128)(2,1)S(1)}, bf16[256,256]{1,0:T(8,128)(2,1)S(1)}) custom-call(bf16[16,16,768]{2,1,0:T(8,128)(2,1)S(1)} %all_to_all.10.near_ref, bf16[2,384,4096]{2,1,0:T(8,128)(2,1)} %bitcast.10), custom_call_target="tpu_custom_call" | custom-call | bytes 12582912 | tf_op jit(solution)/shard_map/near_rows/pallas_call | solution.py:347
  24.6 0.0 collective-permute-done.far_ref.refs_2_
  24.6 2.0 %gate_up.1 = (bf16[64,4096]{1,0:T(8,128)(2,1)S(1)}, bf16[384,64]{1,0:T(8,128)(2,1)S(1)}, f32[384,64]{1,0:T(8,128)S(1)}, f32[384,64]{1,0:T(8,128)S(1)}, bf16[384,4096]{1,0:T(8,128)(2,1)S(1)}) custom-call(bf16[16,16,768]{2,1,0:T(8,128)(2,1)S(1)} %collective-permute-done.far_ref.refs_2_, bf16[32,4096]{1,0:T(8,128)(2,1)S(1)} %get-tuple-element.30.x_near, ...), custom_call_target="tpu_custom_call" | custom-call | tf_op jit(solution)/shard_map/gate_up/pallas_call | solution.py:361
  26.5 0.0 collective-permute-done.1.refs_0_
  26.6 0.3 collective-permute-start.2
  26.8 0.7 %down.1 = (f32[32,4096]{1,0:T(8,128)S(1)}, bf16[32,4096]{1,0:T(8,128)(2,1)S(1)}) custom-call(bf16[384,64]{1,0:T(8,128)(2,1)S(1)} %get-tuple-element.43.hid_ref, bf16[384,4096]{1,0:T(8,128)(2,1)S(1)} %get-tuple-element.36.refs_5_.w_down_ref), custom_call_target="tpu_custom_call" | custom-call | tf_op jit(solution)/shard_map/down/pallas_call | solution.py:374
  27.5 0.4 collective-permute-start.4
  27.9 0.1 collective-permute-done.2.refs_1_
  28.0 1.4 %hidden_grad.1 = (bf16[64,4096]{1,0:T(8,128)(2,1)S(1)}, bf16[384,64]{1,0:T(8,128)(2,1)S(1)}, bf16[384,64]{1,0:T(8,128)(2,1)S(1)}) custom-call(bf16[16,16,256]{2,1,0:T(8,128)(2,1)S(1)} %collective-permute-done.1.refs_0_, bf16[16,16,256]{2,1,0:T(8,128)(2,1)S(1)} %collective-permute-done.2.refs_1_, ...), custom_call_target="tpu_custom_call" | custom-call | flops 201326592 | bytes 3145728 | tf_op jit(solution)/shard_map/hidden_grad/pallas_call | solution.py:383
  29.4 0.0 copy-start
  29.4 0.0 copy-start.1
  29.4 1.3 %input_grad.1 = (f32[32,4096]{1,0:T(8,128)S(1)}, bf16[32,4096]{1,0:T(8,128)(2,1)S(1)}) custom-call(bf16[384,64]{1,0:T(8,128)(2,1)S(1)} %get-tuple-element.39.gg_ref.after_ref, bf16[384,64]{1,0:T(8,128)(2,1)S(1)} %get-tuple-element.40.ug_ref, bf16[2,384,4096]{2,1,0:T(8,128)(2,1)S(1)} %get-tuple-element.32.w_in_ref), custom_call_target="tpu_custom_call" | custom-call | flops 402653184 | bytes 6291456 | tf_op jit(solution)/shard_map/input_grad/pallas_call | solution.py:392
  30.7 0.3 collective-permute-start.3
  31.0 0.0 collective-permute-done.4.other_ref
  31.0 0.9 %merge_out.1.first_hbm = bf16[16,32,512]{2,1,0:T(8,128)(2,1)} custom-call(bf16[256,256]{1,0:T(8,128)(2,1)S(1)} %get-tuple-element.29.fold_ref, f32[32,4096]{1,0:T(8,128)S(1)} %get-tuple-element.44.keep_ref, bf16[32,4096]{1,0:T(8,128)(2,1)S(1)} %collective-permute-done.4.other_ref), custom_call_target="tpu_custom_call" | custom-call | bytes 1048576 | tf_op jit(solution)/shard_map/merge_out/pallas_call | solution.py:404
  31.9 0.4 collective-permute-done.3.other_ref
  32.3 0.9 %merge_grad.1 = bf16[16,32,512]{2,1,0:T(8,128)(2,1)} custom-call(bf16[256,256]{1,0:T(8,128)(2,1)S(1)} %get-tuple-element.29.fold_ref, f32[32,4096]{1,0:T(8,128)S(1)} %get-tuple-element.41.keep_ref, bf16[32,4096]{1,0:T(8,128)(2,1)S(1)} %collective-permute-done.3.other_ref, bf16[16,32,512]{2,1,0:T(8,128)(2,1)} %merge_out.1.first_hbm), custom_call_target="tpu_custom_call", output_to_operand_aliasing={{}: (3, {})} | custom-call | tf_op jit(solution)/shard_map/merge_grad/pallas_call | solution.py:414
  33.2 6.2 %all-to-all-start.1 = ((bf16[16,32,512]{2,1,0:T(8,128)(2,1)}), bf16[16,32,512]{2,1,0:T(8,128)(2,1)S(1)}, u32[]{:S(2)}, u32[]{:S(2)}) async-start(bf16[16,32,512]{2,1,0:T(8,128)(2,1)} %merge_grad.1), calls=%async_computation.1 | async-start | bytes 1048576 | tf_op jit(solution)/shard_map/all_to_all | solution.py:314
  39.4 0.0 copy-done
  39.4 0.0 copy-done.1
  39.4 0.6 %slot_tables.1 = (bf16[512,128]{1,0:T(8,128)(2,1)S(1)}, bf16[512,128]{1,0:T(8,128)(2,1)S(1)}) custom-call(s32[8,64]{1,0:T(8,128)S(1)} %bitcast.7, bf16[8,64]{1,0:T(8,128)(2,1)S(1)} %bitcast.9, bf16[384,64]{1,0:T(8,128)(2,1)S(1)} %get-tuple-element.39.gg_ref.after_ref), custom_call_target="tpu_custom_call" | custom-call | tf_op jit(solution)/shard_map/slot_tables/pallas_call | solution.py:443
  40.1 5.9 %weight_grads.1 = (bf16[2,384,4096]{2,1,0:T(8,128)(2,1)}, bf16[384,4096]{1,0:T(8,128)(2,1)}) custom-call(bf16[64,4096]{1,0:T(8,128)(2,1)S(1)} %get-tuple-element.50.x_ref, bf16[64,4096]{1,0:T(8,128)(2,1)S(1)} %get-tuple-element.51.c_ref, bf16[384,64]{1,0:T(8,128)(2,1)S(1)} %get-tuple-element.43.hid_ref, ...), custom_call_target="tpu_custom_call" | custom-call | flops 603979776 | bytes 10485760 | tf_op jit(solution)/shard_map/weight_grads/pallas_call | solution.py:425
  46.0 5.3 %all-to-all-done.1.back_ref = bf16[16,32,512]{2,1,0:T(8,128)(2,1)S(1)} async-done(((bf16[16,32,512]{2,1,0:T(8,128)(2,1)}), bf16[16,32,512]{2,1,0:T(8,128)(2,1)S(1)}, u32[]{:S(2)}, u32[]{:S(2)}) %all-to-all-start.1) | async-done | bytes 524320 | tf_op jit(solution)/shard_map/all_to_all | solution.py:314
  51.2 1.2 %combine_rows.1 = (bf16[64,4096]{1,0:T(8,128)(2,1)}, bf16[64,4096]{1,0:T(8,128)(2,1)}) custom-call(bf16[16,32,512]{2,1,0:T(8,128)(2,1)S(1)} %all-to-all-done.1.back_ref, bf16[512,128]{1,0:T(8,128)(2,1)S(1)} %get-tuple-element.46.pick_ref, bf16[512,128]{1,0:T(8,128)(2,1)S(1)} %get-tuple-element.47.weigh_ref), custom_call_target="tpu_custom_call" | custom-call | tf_op jit(solution)/shard_map/combine_rows/pallas_call | solution.py:451
  (1 shorter events, 0.0 us)
Async XLA Ops:
  19.4 5.2 %collective-permute-start = (bf16[16,16,768]{2,1,0:T(8,128)(2,1)S(1)}, bf16[16,16,768]{2,1,0:T(8,128)(2,1)S(1)}, u32[]{:S(2)}, u32[]{:S(2)}) collective-permute-start(bf16[16,16,768]{2,1,0:T(8,128)(2,1)S(1)} %all_to_all.10.near_ref), channel_id=1, source_target_pairs={{0,8},{8,0},{1,9},{9,1},{2,10},{10,2},{3,11},{11,3},{4,12},{12,4},... | collective-permute-start | bytes 1179656 | tf_op jit(solution)/shard_map/ppermute | solution.py:320
  19.4 7.1 %collective-permute-start.1 = (bf16[16,16,256]{2,1,0:T(8,128)(2,1)S(1)}, bf16[16,16,256]{2,1,0:T(8,128)(2,1)S(1)}, u32[]{:S(2)}, u32[]{:S(2)}) collective-permute-start(bf16[16,16,256]{2,1,0:T(8,128)(2,1)S(1)} %slice.4), channel_id=1, source_target_pairs={{16,0},{0,16},{17,1},{1,17},{18,2},{2,18},{19,3},{3,19},{20,4},{4,... | collective-permute-start | bytes 393224 | tf_op jit(solution)/shard_map/ppermute | solution.py:341
  26.6 1.4 %collective-permute-start.2 = (bf16[16,16,256]{2,1,0:T(8,128)(2,1)S(1)}, bf16[16,16,256]{2,1,0:T(8,128)(2,1)S(1)}, u32[]{:S(2)}, u32[]{:S(2)}) collective-permute-start(bf16[16,16,256]{2,1,0:T(8,128)(2,1)S(1)} %collective-permute-done.1.refs_0_), channel_id=1, source_target_pairs={{0,8},{8,0},{1,9},{9,1},{2,10},{10,2},{3,11},{11,3},{4,12},{12,4},... | collective-permute-start | bytes 393224 | tf_op jit(solution)/shard_map/ppermute | solution.py:320
  27.5 3.4 %collective-permute-start.4 = (bf16[32,4096]{1,0:T(8,128)(2,1)S(1)}, bf16[32,4096]{1,0:T(8,128)(2,1)S(1)}, u32[]{:S(2)}, u32[]{:S(2)}) collective-permute-start(bf16[32,4096]{1,0:T(8,128)(2,1)S(1)} %get-tuple-element.45), channel_id=1, source_target_pairs={{0,8},{8,0},{1,9},{9,1},{2,10},{10,2},{3,11},{11,3},{4,12},{12,4},... | collective-permute-start | bytes 786440 | tf_op jit(solution)/shard_map/ppermute | solution.py:320
  29.4 10.0 %copy-start = (s32[64,8]{0,1:T(8,128)S(1)}, s32[64,8]{0,1:T(8,128)}, u32[]{:S(2)}) copy-start(s32[64,8]{0,1:T(8,128)} %param.8) | copy-start | bytes 6148
  29.4 10.0 %copy-start.1 = (bf16[64,8]{0,1:T(8,128)(2,1)S(1)}, bf16[64,8]{0,1:T(8,128)(2,1)}, u32[]{:S(2)}) copy-start(bf16[64,8]{0,1:T(8,128)(2,1)} %param.9) | copy-start | bytes 3076
  30.7 1.6 %collective-permute-start.3 = (bf16[32,4096]{1,0:T(8,128)(2,1)S(1)}, bf16[32,4096]{1,0:T(8,128)(2,1)S(1)}, u32[]{:S(2)}, u32[]{:S(2)}) collective-permute-start(bf16[32,4096]{1,0:T(8,128)(2,1)S(1)} %get-tuple-element.42), channel_id=1, source_target_pairs={{0,8},{8,0},{1,9},{9,1},{2,10},{10,2},{3,11},{11,3},{4,12},{12,4},... | collective-permute-start | bytes 786440 | tf_op jit(solution)/shard_map/ppermute | solution.py:320
  33.2 18.0 %all-to-all-start.1 = ((bf16[16,32,512]{2,1,0:T(8,128)(2,1)}), bf16[16,32,512]{2,1,0:T(8,128)(2,1)S(1)}, u32[]{:S(2)}, u32[]{:S(2)}) async-start(bf16[16,32,512]{2,1,0:T(8,128)(2,1)} %merge_grad.1), calls=%async_computation.1 | async-start | bytes 1048576 | tf_op jit(solution)/shard_map/all_to_all | solution.py:314

commit v8 on v7

--- a/solution.py
+++ b/solution.py
@@ -13,7 +13,7 @@
 CHUNKS = TILE // CAP
 PAIR = 2
 STEPS = 2
-SEEDS = (40, 4)
+SEEDS = (40, 38)
 F32 = jnp.float32
 BF16 = jnp.bfloat16
 LIMIT = 24 * 1024 * 1024

time: 52.8 us -> 52.5 us (level)
  no operation moved by 1% of the time
where the time goes in v8:
time: 52.5 us; the launch traced here: 52.2 us
  Pallas kernels  19.5 us (37%)
  blocking collectives  17 us (32%)
  starting transfers between devices  9.47 us (18%)
  waiting for transfers between devices  5.46 us (10%)
  between operations  0.75 us (1%)
    all_to_all x1, blocking collectives, exchange(): lax.all_to_all(array, ('row', 'pair', 'exp'), split_axis=0, concat_axis=0...  17 us
    all_to_all x1, starting transfers between devices, exchange(): lax.all_to_all(array, ('row', 'pair', 'exp'), split_axis=0, concat_axis=0...  6.22 us
    pallas_call x1, Pallas kernels, body(): pl.pallas_call(weight_kernel, grid=(CHUNKS,), out_shape=(jax.ShapeDtypeSt...  5.88 us
    all_to_all x1, waiting for transfers between devices, exchange(): lax.all_to_all(array, ('row', 'pair', 'exp'), split_axis=0, concat_axis=0...  4.99 us
    pallas_call x1, Pallas kernels, body(): pl.pallas_call(functools.partial(near_kernel, tuple((orders[0].index(r) f...  2.8 us
    ppermute x1, starting transfers between devices, body(): lax.ppermute(share, 'row', [((i + k) % groups, i) for i in range(groups)])  2.33 us
    pallas_call x1, Pallas kernels, body(): pl.pallas_call(forward_kernel, out_shape=(wide, tall, slope, slope, pltpu...  1.98 us
    pallas_call x1, Pallas kernels, body(): pl.pallas_call(functools.partial(gather_kernel, orders[0], experts), out_...  1.78 us
  transfers between devices with their start and end apart: 6, of which 3 were waited for; matrix products, arithmetic and copies ran while one was open for 0% of the time, Pallas kernels for 30%

profile of v8, /device:TPU:0, one launch (start us, length us, event | category | flops | bytes accessed | tf_op | source)
XLA Modules:
  0.0 52.2 jit_solution(13225083329745492224)
XLA Ops:
  0.6 1.8 %gather_rows.1 = bf16[16,16,768]{2,1,0:T(8,128)(2,1)S(1)} custom-call(s32[8,64]{1,0:T(8,128)} %bitcast.6, bf16[8,64]{1,0:T(8,128)(2,1)} %bitcast.8, bf16[64,4096]{1,0:T(8,128)(2,1)} %tok_hbm.1, bf16[64,4096]{1,0:T(8,128)(2,1)} %cot_hbm.1), custom_call_target="tpu_custom_call" | custom-call | tf_op jit(solution)/shard_map/gather_rows/pallas_call | solution.py:322
  2.4 17.0 %all_to_all.10.near_ref = bf16[16,16,768]{2,1,0:T(8,128)(2,1)S(1)} all-to-all(bf16[16,16,768]{2,1,0:T(8,128)(2,1)S(1)} %gather_rows.1), channel_id=1, replica_groups={{21,0,18,20,23,3,17,4,1,2,22,16,5,7,19,6},{29,8,26,28,31,11,25,12,9,10,..., dimensions={0} | all-to-all | bytes 786432 | tf_op jit(solution)/shard_map/all_to_all | solution.py:314
  19.4 0.0 collective-permute-start
  19.4 2.3 %collective-permute-start.1 = (bf16[16,16,256]{2,1,0:T(8,128)(2,1)S(1)}, bf16[16,16,256]{2,1,0:T(8,128)(2,1)S(1)}, u32[]{:S(2)}, u32[]{:S(2)}) collective-permute-start(bf16[16,16,256]{2,1,0:T(8,128)(2,1)S(1)} %slice.4), channel_id=1, source_target_pairs={{16,0},{0,16},{17,1},{1,17},{18,2},{2,18},{19,3},{3,19},{20,4},{4,... | collective-permute-start | bytes 393224 | tf_op jit(solution)/shard_map/ppermute | solution.py:341
  21.8 2.8 %near_rows.1 = (bf16[2,384,4096]{2,1,0:T(8,128)(2,1)S(1)}, bf16[32,4096]{1,0:T(8,128)(2,1)S(1)}, bf16[32,2048]{1,0:T(8,128)(2,1)S(1)}, bf16[256,256]{1,0:T(8,128)(2,1)S(1)}, bf16[256,256]{1,0:T(8,128)(2,1)S(1)}) custom-call(bf16[16,16,768]{2,1,0:T(8,128)(2,1)S(1)} %all_to_all.10.near_ref, bf16[2,384,4096]{2,1,0:T(8,128)(2,1)} %bitcast.10), custom_call_target="tpu_custom_call" | custom-call | bytes 12582912 | tf_op jit(solution)/shard_map/near_rows/pallas_call | solution.py:347
  24.6 0.0 collective-permute-done.far_ref.refs_2_
  24.6 2.0 %gate_up.1 = (bf16[64,4096]{1,0:T(8,128)(2,1)S(1)}, bf16[384,64]{1,0:T(8,128)(2,1)S(1)}, f32[384,64]{1,0:T(8,128)S(1)}, f32[384,64]{1,0:T(8,128)S(1)}, bf16[384,4096]{1,0:T(8,128)(2,1)S(1)}) custom-call(bf16[16,16,768]{2,1,0:T(8,128)(2,1)S(1)} %collective-permute-done.far_ref.refs_2_, bf16[32,4096]{1,0:T(8,128)(2,1)S(1)} %get-tuple-element.30.x_near, ...), custom_call_target="tpu_custom_call" | custom-call | tf_op jit(solution)/shard_map/gate_up/pallas_call | solution.py:361
  26.6 0.0 collective-permute-done.1.refs_0_
  26.6 0.3 collective-permute-start.2
  26.8 0.7 %down.1 = (f32[32,4096]{1,0:T(8,128)S(1)}, bf16[32,4096]{1,0:T(8,128)(2,1)S(1)}) custom-call(bf16[384,64]{1,0:T(8,128)(2,1)S(1)} %get-tuple-element.43.hid_ref, bf16[384,4096]{1,0:T(8,128)(2,1)S(1)} %get-tuple-element.36.refs_5_.w_down_ref), custom_call_target="tpu_custom_call" | custom-call | tf_op jit(solution)/shard_map/down/pallas_call | solution.py:374
  27.5 0.4 collective-permute-start.4
  27.9 0.1 collective-permute-done.2.refs_1_
  28.0 1.4 %hidden_grad.1 = (bf16[64,4096]{1,0:T(8,128)(2,1)S(1)}, bf16[384,64]{1,0:T(8,128)(2,1)S(1)}, bf16[384,64]{1,0:T(8,128)(2,1)S(1)}) custom-call(bf16[16,16,256]{2,1,0:T(8,128)(2,1)S(1)} %collective-permute-done.1.refs_0_, bf16[16,16,256]{2,1,0:T(8,128)(2,1)S(1)} %collective-permute-done.2.refs_1_, ...), custom_call_target="tpu_custom_call" | custom-call | flops 201326592 | bytes 3145728 | tf_op jit(solution)/shard_map/hidden_grad/pallas_call | solution.py:383
  29.4 0.0 copy-start
  29.4 0.0 copy-start.1
  29.4 1.3 %input_grad.1 = (f32[32,4096]{1,0:T(8,128)S(1)}, bf16[32,4096]{1,0:T(8,128)(2,1)S(1)}) custom-call(bf16[384,64]{1,0:T(8,128)(2,1)S(1)} %get-tuple-element.39.gg_ref.after_ref, bf16[384,64]{1,0:T(8,128)(2,1)S(1)} %get-tuple-element.40.ug_ref, bf16[2,384,4096]{2,1,0:T(8,128)(2,1)S(1)} %get-tuple-element.32.w_in_ref), custom_call_target="tpu_custom_call" | custom-call | flops 402653184 | bytes 6291456 | tf_op jit(solution)/shard_map/input_grad/pallas_call | solution.py:392
  30.7 0.3 collective-permute-start.3
  30.9 0.0 collective-permute-done.4.other_ref
  30.9 0.9 %merge_out.1.first_hbm = bf16[16,32,512]{2,1,0:T(8,128)(2,1)} custom-call(bf16[256,256]{1,0:T(8,128)(2,1)S(1)} %get-tuple-element.29.fold_ref, f32[32,4096]{1,0:T(8,128)S(1)} %get-tuple-element.44.keep_ref, bf16[32,4096]{1,0:T(8,128)(2,1)S(1)} %collective-permute-done.4.other_ref), custom_call_target="tpu_custom_call" | custom-call | bytes 1048576 | tf_op jit(solution)/shard_map/merge_out/pallas_call | solution.py:404
  31.9 0.4 collective-permute-done.3.other_ref
  32.3 0.9 %merge_grad.1 = bf16[16,32,512]{2,1,0:T(8,128)(2,1)} custom-call(bf16[256,256]{1,0:T(8,128)(2,1)S(1)} %get-tuple-element.29.fold_ref, f32[32,4096]{1,0:T(8,128)S(1)} %get-tuple-element.41.keep_ref, bf16[32,4096]{1,0:T(8,128)(2,1)S(1)} %collective-permute-done.3.other_ref, bf16[16,32,512]{2,1,0:T(8,128)(2,1)} %merge_out.1.first_hbm), custom_call_target="tpu_custom_call", output_to_operand_aliasing={{}: (3, {})} | custom-call | tf_op jit(solution)/shard_map/merge_grad/pallas_call | solution.py:414
  33.2 6.2 %all-to-all-start.1 = ((bf16[16,32,512]{2,1,0:T(8,128)(2,1)}), bf16[16,32,512]{2,1,0:T(8,128)(2,1)S(1)}, u32[]{:S(2)}, u32[]{:S(2)}) async-start(bf16[16,32,512]{2,1,0:T(8,128)(2,1)} %merge_grad.1), calls=%async_computation.1 | async-start | bytes 1048576 | tf_op jit(solution)/shard_map/all_to_all | solution.py:314
  39.4 0.0 copy-done
  39.4 0.0 copy-done.1
  39.4 0.6 %slot_tables.1 = (bf16[512,128]{1,0:T(8,128)(2,1)S(1)}, bf16[512,128]{1,0:T(8,128)(2,1)S(1)}) custom-call(s32[8,64]{1,0:T(8,128)S(1)} %bitcast.7, bf16[8,64]{1,0:T(8,128)(2,1)S(1)} %bitcast.9, bf16[384,64]{1,0:T(8,128)(2,1)S(1)} %get-tuple-element.39.gg_ref.after_ref), custom_call_target="tpu_custom_call" | custom-call | tf_op jit(solution)/shard_map/slot_tables/pallas_call | solution.py:443
  40.1 5.9 %weight_grads.1 = (bf16[2,384,4096]{2,1,0:T(8,128)(2,1)}, bf16[384,4096]{1,0:T(8,128)(2,1)}) custom-call(bf16[64,4096]{1,0:T(8,128)(2,1)S(1)} %get-tuple-element.50.x_ref, bf16[64,4096]{1,0:T(8,128)(2,1)S(1)} %get-tuple-element.51.c_ref, bf16[384,64]{1,0:T(8,128)(2,1)S(1)} %get-tuple-element.43.hid_ref, ...), custom_call_target="tpu_custom_call" | custom-call | flops 603979776 | bytes 10485760 | tf_op jit(solution)/shard_map/weight_grads/pallas_call | solution.py:425
  46.0 5.0 %all-to-all-done.1.back_ref = bf16[16,32,512]{2,1,0:T(8,128)(2,1)S(1)} async-done(((bf16[16,32,512]{2,1,0:T(8,128)(2,1)}), bf16[16,32,512]{2,1,0:T(8,128)(2,1)S(1)}, u32[]{:S(2)}, u32[]{:S(2)}) %all-to-all-start.1) | async-done | bytes 524320 | tf_op jit(solution)/shard_map/all_to_all | solution.py:314
  51.0 1.2 %combine_rows.1 = (bf16[64,4096]{1,0:T(8,128)(2,1)}, bf16[64,4096]{1,0:T(8,128)(2,1)}) custom-call(bf16[16,32,512]{2,1,0:T(8,128)(2,1)S(1)} %all-to-all-done.1.back_ref, bf16[512,128]{1,0:T(8,128)(2,1)S(1)} %get-tuple-element.46.pick_ref, bf16[512,128]{1,0:T(8,128)(2,1)S(1)} %get-tuple-element.47.weigh_ref), custom_call_target="tpu_custom_call" | custom-call | tf_op jit(solution)/shard_map/combine_rows/pallas_call | solution.py:451
  (1 shorter events, 0.0 us)
Async XLA Ops:
  19.4 5.2 %collective-permute-start = (bf16[16,16,768]{2,1,0:T(8,128)(2,1)S(1)}, bf16[16,16,768]{2,1,0:T(8,128)(2,1)S(1)}, u32[]{:S(2)}, u32[]{:S(2)}) collective-permute-start(bf16[16,16,768]{2,1,0:T(8,128)(2,1)S(1)} %all_to_all.10.near_ref), channel_id=1, source_target_pairs={{0,8},{8,0},{1,9},{9,1},{2,10},{10,2},{3,11},{11,3},{4,12},{12,4},... | collective-permute-start | bytes 1179656 | tf_op jit(solution)/shard_map/ppermute | solution.py:320
  19.4 7.1 %collective-permute-start.1 = (bf16[16,16,256]{2,1,0:T(8,128)(2,1)S(1)}, bf16[16,16,256]{2,1,0:T(8,128)(2,1)S(1)}, u32[]{:S(2)}, u32[]{:S(2)}) collective-permute-start(bf16[16,16,256]{2,1,0:T(8,128)(2,1)S(1)} %slice.4), channel_id=1, source_target_pairs={{16,0},{0,16},{17,1},{1,17},{18,2},{2,18},{19,3},{3,19},{20,4},{4,... | collective-permute-start | bytes 393224 | tf_op jit(solution)/shard_map/ppermute | solution.py:341
  26.6 1.4 %collective-permute-start.2 = (bf16[16,16,256]{2,1,0:T(8,128)(2,1)S(1)}, bf16[16,16,256]{2,1,0:T(8,128)(2,1)S(1)}, u32[]{:S(2)}, u32[]{:S(2)}) collective-permute-start(bf16[16,16,256]{2,1,0:T(8,128)(2,1)S(1)} %collective-permute-done.1.refs_0_), channel_id=1, source_target_pairs={{0,8},{8,0},{1,9},{9,1},{2,10},{10,2},{3,11},{11,3},{4,12},{12,4},... | collective-permute-start | bytes 393224 | tf_op jit(solution)/shard_map/ppermute | solution.py:320
  27.5 3.4 %collective-permute-start.4 = (bf16[32,4096]{1,0:T(8,128)(2,1)S(1)}, bf16[32,4096]{1,0:T(8,128)(2,1)S(1)}, u32[]{:S(2)}, u32[]{:S(2)}) collective-permute-start(bf16[32,4096]{1,0:T(8,128)(2,1)S(1)} %get-tuple-element.45), channel_id=1, source_target_pairs={{0,8},{8,0},{1,9},{9,1},{2,10},{10,2},{3,11},{11,3},{4,12},{12,4},... | collective-permute-start | bytes 786440 | tf_op jit(solution)/shard_map/ppermute | solution.py:320
  29.4 10.0 %copy-start = (s32[64,8]{0,1:T(8,128)S(1)}, s32[64,8]{0,1:T(8,128)}, u32[]{:S(2)}) copy-start(s32[64,8]{0,1:T(8,128)} %param.8) | copy-start | bytes 6148
  29.4 10.0 %copy-start.1 = (bf16[64,8]{0,1:T(8,128)(2,1)S(1)}, bf16[64,8]{0,1:T(8,128)(2,1)}, u32[]{:S(2)}) copy-start(bf16[64,8]{0,1:T(8,128)(2,1)} %param.9) | copy-start | bytes 3076
  30.7 1.6 %collective-permute-start.3 = (bf16[32,4096]{1,0:T(8,128)(2,1)S(1)}, bf16[32,4096]{1,0:T(8,128)(2,1)S(1)}, u32[]{:S(2)}, u32[]{:S(2)}) collective-permute-start(bf16[32,4096]{1,0:T(8,128)(2,1)S(1)} %get-tuple-element.42), channel_id=1, source_target_pairs={{0,8},{8,0},{1,9},{9,1},{2,10},{10,2},{3,11},{11,3},{4,12},{12,4},... | collective-permute-start | bytes 786440 | tf_op jit(solution)/shard_map/ppermute | solution.py:320
  33.2 17.8 %all-to-all-start.1 = ((bf16[16,32,512]{2,1,0:T(8,128)(2,1)}), bf16[16,32,512]{2,1,0:T(8,128)(2,1)S(1)}, u32[]{:S(2)}, u32[]{:S(2)}) async-start(bf16[16,32,512]{2,1,0:T(8,128)(2,1)} %merge_grad.1), calls=%async_computation.1 | async-start | bytes 1048576 | tf_op jit(solution)/shard_map/all_to_all | solution.py:314
